TPU v7x, 128 devices: a whole 4x4x4 slice. The times are simulated.
128 devices in a mesh: section: 4 (over x), seq: 8 (over y_lo, z), mp: 4 (over y_hi, core).
Axes of the slice: x: 4, y: 4 (y_hi: 2, y_lo: 2; y = y_hi * 2 + y_lo), z: 4, core: 2. Of those that a mesh axis runs over, the one named last changes fastest.
Arguments:
- decoder_rows: bfloat16 [4, 4096, 4096], P('section', ('seq', 'mp'))
- encoder_panel: bfloat16 [4, 4096, 4096], P(None, 'seq', ('section', 'mp'))
- norm_gain: bfloat16 [4, 4096], P('section'), may hold values from 0.099609375 to 1.8984375
- w_query: bfloat16 [4, 4096, 2048], P('section', None, 'mp'), may hold values from -0.09375 to 0.09375
- w_key: bfloat16 [4, 4096, 2048], P('section', None, 'mp'), may hold values from -0.09375 to 0.09375
- w_value: bfloat16 [4, 4096, 2048], P('section', None, 'mp'), may hold values from -0.09375 to 0.09375
- w_output: bfloat16 [4, 2048, 4096], P('section', 'mp'), may hold values from -0.125 to 0.125
- decoder_segments: int32 [4, 4096], P('section', 'seq'), may hold values from 0 to 7, never falling along the last dimension, each value on 1 to 2048 neighbouring positions
- encoder_segments: int32 [4, 4096], P('section'), may hold values from 0 to 7, never falling along the last dimension, each value on 1 to 2048 neighbouring positions
Outputs:
- combined: bfloat16 [4, 4096, 4096], P('section', ('seq', 'mp'))
Inputs may be any that keep to these rules, and one draw needn't show every extreme that they name: `decoder_segments`: ids never fall along a sequence; every one of the 8 documents has one or more decoder tokens in each micro-batch, and the longest one holds half of the decoder tokens. `encoder_segments`: ids never fall along a sequence; every one of the 8 documents has one or more encoder tokens in each micro-batch, and the longest one holds half of them.
All inputs are finite; a program needn't handle non-finite values.
Results may differ from a plain program's by a relative error of at most 0.017.
The roundings to bfloat16 on the way count: a program that leaves them out, or rounds other values in their place, can miss the bound.
Values may be sent and summed in bfloat16 or wider, within the bound.
No kernel may reach another device: no remote copies, remote signals or barrier semaphores. Data moves between devices by JAX's collectives and lax.ppermute only.
A program may use at most 128 MiB of HBM per device.

v0:
```python
import jax
import jax.numpy as jnp
from jax import lax
from jax.sharding import PartitionSpec as P

HD = 256


def normed_rows(layer_rows, gain):
    widened = layer_rows.astype(jnp.float32)
    mean_square = jnp.mean(widened * widened, axis=-1, keepdims=True)
    return (widened * lax.rsqrt(mean_square + 1e-06) * gain.astype(jnp.float32)).astype(
        jnp.bfloat16
    )


def attend_block(running, query_heads, query_ids, key_block, value_block, key_ids):
    row_peak, row_total, context = running
    head_count = query_heads.shape[1]
    key_count = key_block.shape[0]
    key_heads = key_block.reshape(key_count, head_count, HD)
    value_heads = value_block.reshape(key_count, head_count, HD)
    scores = jnp.einsum(
        "qhd,khd->hqk", query_heads, key_heads, preferred_element_type=jnp.float32
    ) * HD ** (-0.5)
    matching = (query_ids[:, None] == key_ids[None, :])[None]
    new_peak = jnp.maximum(row_peak, jnp.max(jnp.where(matching, scores, -1e30), axis=-1))
    weights = jnp.where(matching, jnp.exp(scores - new_peak[:, :, None]), 0.0)
    new_total = jnp.sum(weights, axis=-1)
    update = jnp.einsum(
        "hqk,khd->qhd",
        weights.astype(jnp.bfloat16),
        value_heads,
        preferred_element_type=jnp.float32,
    )
    return (new_peak, new_total, update)


def per_device(
    decoder_rows,
    encoder_panel,
    norm_gain,
    w_query,
    w_key,
    w_value,
    w_output,
    decoder_segments,
    encoder_segments,
):
    local_rows = decoder_rows[0]
    hidden = normed_rows(local_rows, norm_gain[0])
    query_weight = w_query[0]
    queries = jnp.dot(
        lax.all_gather(hidden, "mp", axis=0, tiled=True),
        query_weight,
        preferred_element_type=jnp.float32,
    ).astype(jnp.bfloat16)
    whole_panel = lax.all_gather(encoder_panel, ("section", "mp"), axis=2, tiled=True)
    own_panel = lax.dynamic_index_in_dim(whole_panel, lax.axis_index("section"), 0, keepdims=False)
    key_rows = jnp.dot(own_panel, w_key[0], preferred_element_type=jnp.float32).astype(jnp.bfloat16)
    value_rows = jnp.dot(own_panel, w_value[0], preferred_element_type=jnp.float32).astype(
        jnp.bfloat16
    )
    query_count = queries.shape[0]
    head_count = queries.shape[1] // HD
    query_heads = queries.reshape(query_count, head_count, HD)
    query_ids = decoder_segments[0]
    encoder_ids = encoder_segments[0]
    initial = (
        jnp.full((head_count, query_count), -1e30, jnp.float32),
        jnp.zeros((head_count, query_count), jnp.float32),
        jnp.zeros((query_count, head_count, HD), jnp.float32),
    )
    key_block = lax.all_gather(key_rows, "seq", axis=0, tiled=True)
    value_block = lax.all_gather(value_rows, "seq", axis=0, tiled=True)
    row_peak, row_total, context = attend_block(
        initial, query_heads, query_ids, key_block, value_block, encoder_ids
    )
    context = (
        (context / jnp.transpose(row_total)[:, :, None])
        .astype(jnp.bfloat16)
        .reshape(query_count, -1)
    )
    output_weight = w_output[0]
    summed = lax.psum_scatter(
        jnp.dot(context, output_weight, preferred_element_type=jnp.float32).astype(jnp.bfloat16),
        "mp",
        scatter_dimension=0,
        tiled=True,
    ).astype(jnp.float32)
    return (summed + local_rows.astype(jnp.float32)).astype(jnp.bfloat16)[None]


def solution(mesh):
    in_specs = (
        P("section", ("seq", "mp"), None),
        P(None, "seq", ("section", "mp")),
        P("section", None),
        P("section", None, "mp"),
        P("section", None, "mp"),
        P("section", None, "mp"),
        P("section", "mp", None),
        P("section", "seq"),
        P("section", None),
    )
    out_specs = P("section", ("seq", "mp"), None)
    return jax.shard_map(
        per_device, mesh=mesh, in_specs=in_specs, out_specs=out_specs, check_vma=False
    )
```

profile of v0, /device:TPU:1, one launch (start us, length us, event | category | flops | bytes accessed | tf_op | source)
XLA Modules:
  0.0 360.3 jit_solution(7788391347884872066)
XLA Ops:
  6.5 0.0 all-gather.5.cloned.1.call-start
  6.5 0.7 all-gather.5.cloned.1.call-update
  7.3 0.0 all-gather.9.cloned.1.call-start
  7.3 0.7 mul.39
  8.0 1.5 fusion.19
  9.6 2.5 fusion.21
  12.1 0.0 all-gather.9.cloned.1.call-update
  12.1 0.0 all-gather.11.cloned.1.call-start
  12.2 124.3 %all-gather.5.cloned.1.call-done = bf16[4,512,4096]{2,1,0:T(8,128)(2,1)} async-done(((bf16[4,512,256]{2,1,0:T(8,128)(2,1)}), bf16[4,512,4096]{2,1,0:T(8,128)(2,1)}) %all-gather.5.cloned.1.call-update) | async-done | bytes 16777232 | tf_op jit(solution)/shard_map/all_gather | solution.py:58
  136.5 6.6 %fusion.34 = bf16[512,512]{1,0:T(8,128)(2,1)} fusion(bf16[1,4096,512]{2,1,0:T(8,128)(2,1)} %param.13, bf16[4,512,4096]{2,1,0:T(8,128)(2,1)} %all-gather.5.cloned.1.call-done, s32[]{:T(128)S(6)} %select_n.11), kind=kOutput, calls=%fused_computation.32 | convolution fusion | flops 2147745792 | bytes 8912900 | tf_op jit(solution)/shard_map/dot_general | solution.py:60
  143.1 0.0 all-gather.11.cloned.1.call-update
  143.1 0.0 copy-start.3
  143.1 0.0 copy-start.4
  143.2 0.0 all-gather.7.cloned.1.call-start
  143.2 7.3 %fusion.26 = bf16[512,512]{1,0:T(8,128)(2,1)} fusion(bf16[1,4096,512]{2,1,0:T(8,128)(2,1)} %param.14, bf16[4,512,4096]{2,1,0:T(8,128)(2,1)} %all-gather.5.cloned.1.call-done, s32[]{:T(128)S(6)} %select_n.11), kind=kOutput, calls=%fused_computation.30 | convolution fusion | flops 2147745792 | bytes 8912900 | tf_op jit(solution)/shard_map/dot_general | solution.py:61
  150.5 0.0 all-gather.7.cloned.1.call-update
  150.5 0.0 reduce-scatter.2.cloned.1.call-start
  150.6 0.0 copy-done.3
  150.6 0.0 copy-done.4
  150.6 1.3 broadcast_compare_fusion
  151.9 23.0 %all-gather.9.cloned.1.call-done = bf16[512,4096]{1,0:T(8,128)(2,1)} async-done(((bf16[128,4096]{1,0:T(8,128)(2,1)}), bf16[512,4096]{1,0:T(8,128)(2,1)}) %all-gather.9.cloned.1.call-update) | async-done | bytes 4194320 | tf_op jit(solution)/shard_map/all_gather | solution.py:54
  174.9 5.8 %fusion.31 = bf16[512,512]{0,1:T(8,128)(2,1)S(1)} fusion(bf16[512,4096]{1,0:T(8,128)(2,1)} %all-gather.9.cloned.1.call-done, bf16[1,4096,512]{2,1,0:T(8,128)(2,1)} %param.12), kind=kOutput, calls=%fused_computation.31 | convolution fusion | flops 2147745792 | bytes 8912896 | tf_op jit(solution)/shard_map/dot_general | solution.py:53
  180.7 47.6 %all-gather.11.cloned.1.call-done = bf16[4096,512]{1,0:T(8,128)(2,1)} async-done(((bf16[512,512]{1,0:T(8,128)(2,1)}), bf16[4096,512]{1,0:T(8,128)(2,1)}) %all-gather.11.cloned.1.call-update) | async-done | bytes 4194320 | tf_op jit(solution)/shard_map/all_gather | solution.py:74
  228.3 7.0 %select_reduce_fusion = (f32[2,512]{1,0:T(2,128)S(1)}, f32[2,512,4096]{2,1,0:T(8,128)S(1)}) fusion(pred[512,4096]{1,0:T(8,128)(4,1)S(1)} %broadcast_compare_fusion, bf16[512,2,256]{0,2,1:T(8,128)(2,1)S(1)} %bitcast.62, bf16[512,2,8,256]{3,2,1,0:T(8,128)(2,1)} %bitcast.61), kind=kOutput, calls=%fused_computation.1 | convolution fusion | flops 2160065536 | bytes 23597056 | tf_op jit(solution)/shard_map/qhd,khd->hqk/dot_general | solution.py:23
  235.4 0.0 copy-start
  235.4 5.7 %copy-done = f32[2,512,4096]{2,1,0:T(8,128)} copy-done((f32[2,512,4096]{2,1,0:T(8,128)}, f32[2,512,4096]{2,1,0:T(8,128)S(1)}, u32[]{:S(2)}) %copy-start) | copy-done | bytes 16777240
  241.1 4.8 %fusion = f32[2,512]{1,0:T(2,128)S(1)} fusion(f32[2,512,4096]{2,1,0:T(8,128)S(1)} %get-tuple-element.6, f32[2,512]{1,0:T(2,128)S(1)} %broadcast_maximum_fusion, pred[512,4096]{1,0:T(8,128)(4,1)S(1)} %broadcast_compare_fusion), kind=kLoop, calls=%fused_computation.2 | loop fusion | flops 16776192 | bytes 18882560 | tf_op jit(solution)/shard_map/reduce_sum | solution.py:29
  245.9 35.4 %all-gather.7.cloned.1.call-done = bf16[4096,512]{1,0:T(8,128)(2,1)} async-done(((bf16[512,512]{1,0:T(8,128)(2,1)}), bf16[4096,512]{1,0:T(8,128)(2,1)}) %all-gather.7.cloned.1.call-update) | async-done | bytes 4194320 | tf_op jit(solution)/shard_map/all_gather | solution.py:75
  281.3 6.4 %copy.14 = bf16[4096,512]{0,1:T(8,128)(2,1)} copy(bf16[4096,512]{1,0:T(8,128)(2,1)} %all-gather.7.cloned.1.call-done) | data formatting | bytes 8388608 | tf_op jit(solution)/shard_map/reshape | solution.py:22
  287.7 0.0 copy-start.2
  287.7 9.1 %divide_convert_fusion = bf16[512,2,256]{0,2,1:T(8,128)(2,1)S(1)} fusion(bf16[4096,2,256]{0,2,1:T(8,128)(2,1)} %bitcast.55, f32[2,512,4096]{2,1,0:T(8,128)} %copy-done, f32[2,512]{1,0:T(2,128)S(1)} %broadcast_maximum_fusion, pred[512,4096]{1,0:T(8,128)(4,1)S(1)} %broadcast_compare_fusion, f32[512,2]{0,1:T(2,128)S(1)} %bitcast.59), kind=kOutput, calls=%fused_computation.34 | convolution fusion | flops 2164785152 | bytes 23601152 | tf_op jit(solution)/shard_map/hqk,khd->qhd/dot_general | solution.py:30
  296.8 0.0 copy-done.2
  296.8 4.3 %convolution_convert_fusion = bf16[512,4096]{1,0:T(8,128)(2,1)} fusion(bf16[512,512]{0,1:T(8,128)(2,1)S(1)} %bitcast.56, bf16[1,512,4096]{2,1,0:T(8,128)(2,1)S(1)} %copy-done.2), kind=kOutput, calls=%fused_computation.6 | convolution fusion | flops 2149580800 | bytes 8912896 | tf_op jit(solution)/shard_map/dot_general | solution.py:86
  301.1 0.0 copy-start.1
  301.1 0.0 reduce-scatter.2.cloned.1.call-update
  301.2 50.2 %reduce-scatter.2.cloned.1.call-done = bf16[128,4096]{1,0:T(8,128)(2,1)} async-done(((bf16[512,4096]{1,0:T(8,128)(2,1)}), bf16[128,4096]{1,0:T(8,128)(2,1)}) %reduce-scatter.2.cloned.1.call-update) | async-done | bytes 1048592 | tf_op jit(solution)/shard_map/reduce_scatter | solution.py:85
  351.4 0.0 copy-done.1
  351.4 2.4 fusion.39
  (2 shorter events, 0.0 us)
Async XLA Ops:
  6.5 130.0 %all-gather.5.cloned.1.call-start = ((), (), s32[]{:S(2)}) async-start(), calls=%async_computation.1 | async-start | bytes 17825792 | tf_op jit(solution)/shard_map/all_gather | solution.py:58
  7.3 167.6 %all-gather.9.cloned.1.call-start = ((), (), s32[]{:S(2)}) async-start(), calls=%async_computation.3 | async-start | bytes 5242880 | tf_op jit(solution)/shard_map/all_gather | solution.py:54
  12.1 216.2 %all-gather.11.cloned.1.call-start = ((), (), s32[]{:S(2)}) async-start(), calls=%async_computation.4 | async-start | bytes 4718592 | tf_op jit(solution)/shard_map/all_gather | solution.py:74
  143.1 7.4 %copy-start.3 = (s32[1,4096]{1,0:T(1,128)S(1)}, s32[1,4096]{1,0:T(1,128)}, u32[]{:S(2)}) copy-start(s32[1,4096]{1,0:T(1,128)} %param.17) | copy-start | bytes 49156
  143.1 7.4 %copy-start.4 = (s32[1,512]{1,0:T(1,128)S(1)}, s32[1,512]{1,0:T(1,128)}, u32[]{:S(2)}) copy-start(s32[1,512]{1,0:T(1,128)} %param.16) | copy-start | bytes 6148
  143.2 138.1 %all-gather.7.cloned.1.call-start = ((), (), s32[]{:S(2)}) async-start(), calls=%async_computation.2 | async-start | bytes 4718592 | tf_op jit(solution)/shard_map/all_gather | solution.py:75
  150.5 200.9 %reduce-scatter.2.cloned.1.call-start = ((), (), s32[]{:S(2)}) async-start(), calls=%async_computation.5 | async-start | bytes 5242880 | tf_op jit(solution)/shard_map/reduce_scatter | solution.py:85
  235.4 5.7 %copy-start = (f32[2,512,4096]{2,1,0:T(8,128)}, f32[2,512,4096]{2,1,0:T(8,128)S(1)}, u32[]{:S(2)}) copy-start(f32[2,512,4096]{2,1,0:T(8,128)S(1)} %get-tuple-element.6) | copy-start | bytes 50331652
  287.7 9.1 %copy-start.2 = (bf16[1,512,4096]{2,1,0:T(8,128)(2,1)S(1)}, bf16[1,512,4096]{2,1,0:T(8,128)(2,1)}, u32[]{:S(2)}) copy-start(bf16[1,512,4096]{2,1,0:T(8,128)(2,1)} %param.15) | copy-start | bytes 12582916
  301.1 50.2 %copy-start.1 = (bf16[1,128,4096]{2,1,0:T(8,128)(2,1)S(1)}, bf16[1,128,4096]{2,1,0:T(8,128)(2,1)}, u32[]{:S(2)}) copy-start(bf16[1,128,4096]{2,1,0:T(8,128)(2,1)} %param.9) | copy-start | bytes 3145732
Sparse Core Ops, SparseCore 0:
  9.6 126.8 all-gather.4
  138.2 36.6 all-gather.8
  176.5 51.7 all-gather.10
  229.8 51.4 all-gather.6
  301.3 50.0 reduce-scatter.1
where the time goes:
time: 361 us; the launch traced here: 360 us
  waiting for transfers between devices  281 us (78%)
  matrix products  40.2 us (11%)
  other arithmetic  13.3 us (4%)
  between operations  13.2 us (4%)
  local copies, waits for them, and re-layouts  12.1 us (3%)
    all_gather x1, waiting for transfers between devices, per_device(): lax.all_gather(encoder_panel, ('section', 'mp'), axis=2, tiled=True)  124 us
    reduce_scatter x1, waiting for transfers between devices, per_device(): lax.psum_scatter(jnp.dot(context, output_weight, preferred_element_type=j...  50.2 us
    all_gather x1, waiting for transfers between devices, per_device(): key_block = lax.all_gather(key_rows, 'seq', axis=0, tiled=True)  47.6 us
    all_gather x1, waiting for transfers between devices, per_device(): value_block = lax.all_gather(value_rows, 'seq', axis=0, tiled=True)  35.4 us
    all_gather x1, waiting for transfers between devices, per_device(): lax.all_gather(hidden, 'mp', axis=0, tiled=True)  23 us
    dot_general x1, matrix products, attend_block(): jnp.einsum('hqk,khd->qhd', weights.astype(jnp.bfloat16), value_heads, pre...  9.12 us
    dot_general x1, matrix products, per_device(): jnp.dot(own_panel, w_value[0], preferred_element_type=jnp.float32)  7.27 us
  transfers between devices with their start and end apart: 5, of which 5 were waited for; matrix products, arithmetic and copies ran while one was open for 10% of the time, Pallas kernels for 0%

commit v1 on v0

v1 whole, which is shorter than its diff:
```python
import functools
import math

import jax
import jax.numpy as jnp
from jax import lax
from jax.experimental import pallas as pl
from jax.experimental.pallas import tpu as pltpu
from jax.sharding import PartitionSpec as P

HD = 256
AXES = ("section", "seq", "mp")
SHAPE = (4, 2, 4, 2, 2)
CHUNKS = 2
MIB = 1 << 20
F32 = jnp.float32
BF16 = jnp.bfloat16


def route(target):
    pairs = []
    for source in range(math.prod(SHAPE)):
        at, rest = [], source
        for size in reversed(SHAPE):
            at.append(rest % size)
            rest //= size
        there = 0
        for place, size in zip(target(*reversed(at)), SHAPE):
            there = there * size + place % size
        pairs.append((source, there))
    return pairs


CORE = route(lambda x, l, z, h, c: (x, l, z, h, c + 1))
Y_FAR = route(lambda x, l, z, h, c: (x, l, z, h + 1, c))
Y_CUT = route(lambda x, l, z, h, c: (x, l + 1, z, h + 1, c))
Y_LOW = route(lambda x, l, z, h, c: (x, l + 1, z, h, c))
Z_UP = route(lambda x, l, z, h, c: (x, l, z + 1, h, c))
Z_DOWN = route(lambda x, l, z, h, c: (x, l, z - 1, h, c))
X_UP = route(lambda x, l, z, h, c: (x + 1, l, z, h, c))
X_DOWN = route(lambda x, l, z, h, c: (x - 1, l, z, h, c))
X_TWO = route(lambda x, l, z, h, c: (x + 2, l, z, h, c))
X_ORDER = (0, -1, 1, 2)


def send(array, pairs):
    return lax.ppermute(array, AXES, pairs)


def vmem(count):
    return [pl.BlockSpec(memory_space=pltpu.VMEM)] * count


def smem(count):
    return [pl.BlockSpec(memory_space=pltpu.SMEM)] * count


def params(mib):
    return pltpu.CompilerParams(vmem_limit_bytes=mib * MIB)


def normed_rows(layer_rows, gain):
    widened = layer_rows.astype(F32)
    mean_square = jnp.mean(widened * widened, axis=-1, keepdims=True)
    return (widened * lax.rsqrt(mean_square + 1e-06) * gain.astype(F32)).astype(BF16)


def dot(a, b):
    return jnp.dot(a, b, preferred_element_type=F32)


def key_value_kernel(place, b0, b1, b2, b3, w_key, w_value, mine, other, panel):
    section, low, mp = place[0], place[1], place[2]
    for flip, block in enumerate((b0, b1, b2, b3)):
        for step, offset in enumerate(X_ORDER):
            column = ((section + offset + 4) % 4 * 4 + jnp.bitwise_xor(mp, flip)) * 256
            panel[:, pl.ds(pl.multiple_of(column, 256), 256)] = block[step]
    for out, side in ((mine, low), (other, 1 - low)):
        columns = pl.ds(pl.multiple_of(side * HD, HD), HD)
        for at, weight in ((0, w_key), (1, w_value)):
            out[at] = dot(panel[...], weight[:, columns]).astype(BF16)


def key_values(place, blocks, w_key, w_value):
    rows = blocks[0].shape[1]
    out = jax.ShapeDtypeStruct((2, rows, HD), BF16)
    return pl.pallas_call(
        key_value_kernel,
        out_shape=(out, out),
        in_specs=smem(1) + vmem(6),
        out_specs=tuple(vmem(2)),
        scratch_shapes=[pltpu.VMEM((rows, 4096), BF16)],
        compiler_params=params(24),
        cost_estimate=pl.CostEstimate(
            flops=2 * rows * 4096 * 1024, bytes_accessed=8 * MIB + rows * 8192, transcendentals=0
        ),
        name="key_values",
    )(place, *blocks, w_key, w_value)


def query_kernel(place, h0, h1, w_query, mine, other):
    low = place[1]
    rows = h0.shape[0]
    for out, side in ((mine, low), (other, 1 - low)):
        columns = pl.ds(pl.multiple_of(side * HD, HD), HD)
        for at, block in enumerate((h0, h1)):
            out[at * rows : (at + 1) * rows] = dot(block[...], w_query[:, columns]).astype(BF16)


def queries(place, blocks, w_query):
    rows = blocks[0].shape[0] * 2
    out = jax.ShapeDtypeStruct((rows, HD), BF16)
    return pl.pallas_call(
        query_kernel,
        out_shape=(out, out),
        in_specs=smem(1) + vmem(3),
        out_specs=tuple(vmem(2)),
        compiler_params=params(16),
        cost_estimate=pl.CostEstimate(
            flops=2 * rows * 4096 * 512, bytes_accessed=4 * MIB + rows * 8192, transcendentals=0
        ),
        name="queries",
    )(place, *blocks, w_query)


def attend_kernel(pieces, spans, query_span, key_span, query, query_ids, key_ids, *refs):
    parts, (out, peak, total, context) = refs[:pieces], refs[pieces:]
    block = 256

    def one_block(at, _):
        rows = pl.ds(pl.multiple_of(at * block, block), block)
        peak[...] = jnp.full_like(peak, -1e30)
        total[...] = jnp.zeros_like(total)
        context[...] = jnp.zeros_like(context)
        for part, keys_values in enumerate(parts):
            span = spans[part]
            meets = (key_span[0, span] <= query_span[1, at]) & (key_span[1, span] >= query_span[0, at])

            @pl.when(meets)
            def _():
                scores = lax.dot_general(
                    query[rows], keys_values[0], (((1,), (1,)), ((), ())), preferred_element_type=F32
                ) * HD ** (-0.5)
                matching = query_ids[rows] == key_ids[pl.ds(span, 1)]
                scores = jnp.where(matching, scores, -1e30)
                old = peak[...]
                new = jnp.maximum(old, jnp.max(scores, axis=-1, keepdims=True))
                weights = jnp.where(matching, jnp.exp(scores - new), 0.0)
                shrink = jnp.exp(old - new)
                peak[...] = new
                total[...] = total[...] * shrink + jnp.sum(weights, axis=-1, keepdims=True)
                context[...] = context[...] * shrink + dot(weights.astype(BF16), keys_values[1])

        out[rows] = (context[...] / total[...]).astype(BF16)
        return 0

    lax.fori_loop(0, query.shape[0] // block, one_block, 0)


def attend(spans, query_span, key_span, query, query_ids, key_ids, parts):
    rows = query.shape[0]
    return pl.pallas_call(
        functools.partial(attend_kernel, len(parts)),
        out_shape=jax.ShapeDtypeStruct((rows, HD), BF16),
        in_specs=smem(3) + vmem(3 + len(parts)),
        out_specs=vmem(1)[0],
        scratch_shapes=[
            pltpu.VMEM((256, 1), F32),
            pltpu.VMEM((256, 1), F32),
            pltpu.VMEM((256, HD), F32),
        ],
        compiler_params=params(24),
        cost_estimate=pl.CostEstimate(
            flops=2 * rows * 4096 * 256, bytes_accessed=6 * MIB, transcendentals=rows * 1024
        ),
        name="attend",
    )(spans, query_span, key_span, query, query_ids, key_ids, *parts)


def output_kernel(place, mine, other, w_output, out):
    low = place[1]
    first = w_output[pl.ds(pl.multiple_of(low * HD, HD), HD)]
    second = w_output[pl.ds(pl.multiple_of((1 - low) * HD, HD), HD)]
    out[...] = (dot(mine[...], first) + dot(other[...], second)).astype(BF16)


def outputs(place, mine, other, w_output):
    rows = mine.shape[0]
    return pl.pallas_call(
        output_kernel,
        grid=(4,),
        out_shape=jax.ShapeDtypeStruct((rows, 4096), BF16),
        in_specs=smem(1) + vmem(2) + [pl.BlockSpec((512, 1024), lambda i: (0, i))],
        out_specs=pl.BlockSpec((rows, 1024), lambda i: (0, i)),
        compiler_params=params(16),
        cost_estimate=pl.CostEstimate(
            flops=2 * rows * 4096 * 512, bytes_accessed=4 * MIB + rows * 8192, transcendentals=0
        ),
        name="outputs",
    )(place, mine, other, w_output)


def per_device(
    decoder_rows,
    encoder_panel,
    norm_gain,
    w_query,
    w_key,
    w_value,
    w_output,
    decoder_segments,
    encoder_segments,
):
    section = lax.axis_index("section")
    seq = lax.axis_index("seq")
    mp = lax.axis_index("mp")
    low, z = seq // 4, seq % 4
    place = jnp.stack([section, low, mp]).astype(jnp.int32)

    rows = 512 // CHUNKS
    crossed = []
    for chunk in range(CHUNKS):

        def panel_of(offset):
            return lax.dynamic_slice(
                encoder_panel, ((section + offset) % 4, chunk * rows, 0), (1, rows, 256)
            )

        crossed.append(
            jnp.concatenate(
                [
                    panel_of(0),
                    send(panel_of(1), X_UP),
                    send(panel_of(3), X_DOWN),
                    send(panel_of(2), X_TWO),
                ]
            )
        )
    panels = []
    for own in crossed:
        far = send(own, Y_FAR)
        panels.append((own, send(own, CORE), far, send(far, CORE)))

    local_rows = decoder_rows[0]
    hidden = normed_rows(local_rows, norm_gain[0])
    hidden_cut = send(hidden, Y_CUT)
    query_near = queries(place, (hidden, send(hidden, CORE)), w_query[0])
    query_far = queries(place, (hidden_cut, send(hidden_cut, CORE)), w_query[0])
    query_mine = jnp.concatenate([query_near[0], query_far[0]])
    query_other = send(jnp.concatenate([query_near[1], query_far[1]]), Y_LOW)
    query = jnp.concatenate([query_mine, query_other])

    ids_own = decoder_segments[0].reshape(4, 128)
    ids_low = send(ids_own, Y_LOW)
    query_ids = jnp.stack(
        [
            (ids_own if flip_low == 0 else ids_low)[jnp.bitwise_xor(mp, flip)]
            for flip_low, flip in ((0, 0), (0, 1), (1, 2), (1, 3), (1, 0), (1, 1), (0, 2), (0, 3))
        ]
    ).reshape(1024)
    query_blocks = query_ids.reshape(4, 256)
    query_span = jnp.stack([query_blocks.min(axis=1), query_blocks.max(axis=1)])
    key_ids = encoder_segments[0].reshape(8 * CHUNKS, rows)
    key_span = jnp.stack([key_ids[:, 0], key_ids[:, -1]])

    parts, spans = [], []

    def note(part, flip_low, step, chunk):
        parts.append(part)
        spans.append((jnp.bitwise_xor(low, flip_low) * 4 + (z + step) % 4) * CHUNKS + chunk)

    for chunk in range(CHUNKS):
        mine, other = key_values(place, panels[chunk], w_key[0], w_value[0])
        for flip_low, held in ((0, mine), (1, send(other, Y_LOW))):
            below, above = send(held, Z_UP), send(held, Z_DOWN)
            across = jnp.stack([send(below[0], Z_UP), send(above[1], Z_DOWN)])
            note(held, flip_low, 0, chunk)
            note(below, flip_low, 3, chunk)
            note(above, flip_low, 1, chunk)
            note(across, flip_low, 2, chunk)

    context = attend(
        jnp.stack(spans).astype(jnp.int32),
        query_span,
        key_span,
        query,
        query_ids[:, None],
        key_ids,
        parts,
    )

    context_other = send(context[512:], Y_LOW)
    across = outputs(place, context[256:512], context_other[256:], w_output[0])
    near = outputs(place, context[:256], context_other[:256], w_output[0])
    across_sum = (across[:128].astype(F32) + send(across[128:], CORE).astype(F32)).astype(BF16)
    arrived = send(across_sum, Y_CUT)
    near_sum = near[:128].astype(F32) + send(near[128:], CORE).astype(F32)
    summed = near_sum + arrived.astype(F32)
    return (summed + local_rows.astype(F32)).astype(BF16)[None]


def solution(mesh):
    in_specs = (
        P("section", ("seq", "mp"), None),
        P(None, "seq", ("section", "mp")),
        P("section", None),
        P("section", None, "mp"),
        P("section", None, "mp"),
        P("section", None, "mp"),
        P("section", "mp", None),
        P("section", "seq"),
        P("section", None),
    )
    out_specs = P("section", ("seq", "mp"), None)
    return jax.shard_map(
        per_device, mesh=mesh, in_specs=in_specs, out_specs=out_specs, check_vma=False
    )
```

time: 361 us -> 186 us (0.52)
  the two profiles are of different devices: /device:TPU:1 before, /device:TPU:66 now
where the time goes in v1:
time: 186 us; the launch traced here: 182 us
  waiting for transfers between devices  86.9 us (47%)
  starting transfers between devices  47.5 us (26%)
  Pallas kernels  33.5 us (18%)
  local copies, waits for them, and re-layouts  8.91 us (5%)
  other arithmetic  4.99 us (3%)
    ppermute x39, waiting for transfers between devices, send(): return lax.ppermute(array, AXES, pairs)  86.9 us
    ppermute x39, starting transfers between devices, send(): return lax.ppermute(array, AXES, pairs)  47.5 us
    pallas_call x1, Pallas kernels, attend(): pl.pallas_call(functools.partial(attend_kernel, len(parts)), out_shape=ja...  15.4 us
    pallas_call x2, Pallas kernels, key_values(): pl.pallas_call(key_value_kernel, out_shape=(out, out), in_specs=smem(1) +...  8.17 us
    pallas_call x2, Pallas kernels, outputs(): pl.pallas_call(output_kernel, grid=(4,), out_shape=jax.ShapeDtypeStruct((...  5.41 us
    unnamed x27, local copies, waits for them, and re-layouts  4.95 us
    pallas_call x2, Pallas kernels, queries(): pl.pallas_call(query_kernel, out_shape=(out, out), in_specs=smem(1) + vme...  4.57 us
  transfers between devices with their start and end apart: 39, of which 18 were waited for; matrix products, arithmetic and copies ran while one was open for 3% of the time, Pallas kernels for 8%

profile of v1, /device:TPU:66, one launch (start us, length us, event | category | flops | bytes accessed | tf_op | source)
XLA Modules:
  0.0 182.2 jit_solution(1856721141723667906)
XLA Ops:
  0.0 2.1 %constant_dynamic-slice_fusion.3 = (bf16[1,256,256]{2,1,0:T(8,128)(2,1)S(1)}, bf16[1,256,256]{2,1,0:T(8,128)(2,1)S(1)}, bf16[1,256,256]{2,1,0:T(8,128)(2,1)S(1)}...) fusion(bf16[4,512,256]{2,1,0:T(8,128)(2,1)} %param.10, ...), kind=kLoop, calls=%fused_computation.30 | loop fusion | bytes 2097168 | tf_op jit(solution)/shard_map/dynamic_slice | solution.py:225
  2.1 2.1 %collective-permute-start.7 = (bf16[1,256,256]{2,1,0:T(8,128)(2,1)S(1)}, bf16[1,256,256]{2,1,0:T(8,128)(2,1)S(1)}, u32[]{:S(2)}, u32[]{:S(2)}) collective-permute-start(bf16[1,256,256]{2,1,0:T(8,128)(2,1)S(1)} %get-tuple-element.27), channel_id=1, source_target_pairs={{0,64},{1,65},{2,66},{3,67},{4,68},{5,69},{6,70},{7,71},{8,72},{9,... | collective-permute-start | bytes 393224 | tf_op jit(solution)/shard_map/ppermute | solution.py:47
  4.3 1.4 collective-permute-start.6
  6.6 3.4 %collective-permute-done.7 = bf16[1,256,256]{2,1,0:T(8,128)(2,1)S(1)} collective-permute-done((bf16[1,256,256]{2,1,0:T(8,128)(2,1)S(1)}, bf16[1,256,256]{2,1,0:T(8,128)(2,1)S(1)}, u32[]{:S(2)}, u32[]{:S(2)}) %collective-permute-start.7) | collective-permute-done | bytes 131104 | tf_op jit(solution)/shard_map/ppermute | solution.py:47
  10.0 1.7 collective-permute-done.6
  11.8 3.3 %collective-permute-start.9 = (bf16[4,256,256]{2,1,0:T(8,128)(2,1)S(1)}, bf16[4,256,256]{2,1,0:T(8,128)(2,1)}, u32[]{:S(2)}, u32[]{:S(2)}) collective-permute-start(bf16[4,256,256]{2,1,0:T(8,128)(2,1)S(1)} %pad_maximum_fusion.1.b0), channel_id=1, source_target_pairs={{0,2},{1,3},{2,0},{3,1},{4,6},{5,7},{6,4},{7,5},{8,10},{9,11},{10,... | collective-permute-start | bytes 1572872 | tf_op jit(solution)/shard_map/ppermute | solution.py:47
  15.4 1.1 collective-permute-start.2
  16.5 2.1 %collective-permute-start.22 = (bf16[1,256,256]{2,1,0:T(8,128)(2,1)}, bf16[1,256,256]{2,1,0:T(8,128)(2,1)S(1)}, u32[]{:S(2)}, u32[]{:S(2)}) collective-permute-start(bf16[1,256,256]{2,1,0:T(8,128)(2,1)} %get-tuple-element.31), channel_id=1, source_target_pairs={{0,64},{1,65},{2,66},{3,67},{4,68},{5,69},{6,70},{7,71},{8,72},{9,... | collective-permute-start | bytes 393224 | tf_op jit(solution)/shard_map/ppermute | solution.py:47
  18.6 1.4 collective-permute-start.21
  22.0 2.5 %collective-permute-done.22 = bf16[1,256,256]{2,1,0:T(8,128)(2,1)S(1)} collective-permute-done((bf16[1,256,256]{2,1,0:T(8,128)(2,1)}, bf16[1,256,256]{2,1,0:T(8,128)(2,1)S(1)}, u32[]{:S(2)}, u32[]{:S(2)}) %collective-permute-start.22) | collective-permute-done | bytes 131104 | tf_op jit(solution)/shard_map/ppermute | solution.py:47
  24.5 1.5 collective-permute-done.21
  26.1 1.1 pad_maximum_fusion.2.b0
  27.2 2.4 %collective-permute-done = s32[4,128]{1,0:T(4,128)S(1)} collective-permute-done((s32[4,128]{1,0:T(4,128)S(1)}, s32[4,128]{1,0:T(4,128)S(1)}, u32[]{:S(2)}, u32[]{:S(2)}) %collective-permute-start) | collective-permute-done | bytes 2080 | tf_op jit(solution)/shard_map/ppermute | solution.py:47
  29.6 1.7 collective-permute-start.24
  32.3 11.6 %collective-permute-done.24.b2 = bf16[4,256,256]{2,1,0:T(8,128)(2,1)} collective-permute-done((bf16[4,256,256]{2,1,0:T(8,128)(2,1)S(1)}, bf16[4,256,256]{2,1,0:T(8,128)(2,1)}, u32[]{:S(2)}, u32[]{:S(2)}) %collective-permute-start.24) | collective-permute-done | bytes 524320 | tf_op jit(solution)/shard_map/ppermute | solution.py:47
  44.2 1.0 copy.10.query_ids
  45.4 15.4 %collective-permute-done.2.h0 = bf16[128,4096]{1,0:T(8,128)(2,1)S(1)} collective-permute-done((bf16[128,4096]{1,0:T(8,128)(2,1)S(1)}, bf16[128,4096]{1,0:T(8,128)(2,1)S(1)}, u32[]{:S(2)}, u32[]{:S(2)}) %collective-permute-start.2) | collective-permute-done | bytes 1048608 | tf_op jit(solution)/shard_map/ppermute | solution.py:47
  60.9 2.2 %copy-done.1 = bf16[1,4096,512]{2,1,0:T(8,128)(2,1)S(1)} copy-done((bf16[1,4096,512]{2,1,0:T(8,128)(2,1)S(1)}, bf16[1,4096,512]{2,1,0:T(8,128)(2,1)}, u32[]{:S(2)}) %copy-start.1) | copy-done | bytes 4194328
  63.1 2.2 %copy-done.3 = bf16[1,4096,512]{2,1,0:T(8,128)(2,1)S(1)} copy-done((bf16[1,4096,512]{2,1,0:T(8,128)(2,1)S(1)}, bf16[1,4096,512]{2,1,0:T(8,128)(2,1)}, u32[]{:S(2)}) %copy-start.3) | copy-done | bytes 4194328
  65.3 4.2 %key_values.2 = (bf16[2,256,256]{2,1,0:T(8,128)(2,1)S(1)}, bf16[2,256,256]{2,1,0:T(8,128)(2,1)S(1)}) custom-call(s32[3]{0:T(128)S(1)} %pad_add_fusion.2.place, bf16[4,256,256]{2,1,0:T(8,128)(2,1)S(1)} %pad_maximum_fusion.1.b0, bf16[4,256,256]{2,1,0:T(8,128)(2,1)} %collective-permute-done.8.b1, bf16[4,256,256]{2,1,0:T(8,128)(2,1)} %collective-permute-done.9.b2, ...), custom_call_target="tpu_custom_call" | custom-call | flops 2147483648 | bytes 10485760 | tf_op jit(solution)/shard_map/key_values/pallas_call | solution.py:87
  69.7 2.7 %queries.2 = (bf16[256,256]{1,0:T(8,128)(2,1)S(1)}, bf16[256,256]{1,0:T(8,128)(2,1)S(1)}) custom-call(s32[3]{0:T(128)S(1)} %pad_add_fusion.2.place, bf16[128,4096]{1,0:T(8,128)(2,1)S(1)} %fusion.2.h0, bf16[128,4096]{1,0:T(8,128)(2,1)} %collective-permute-done.1.h1, bf16[4096,512]{1,0:T(8,128)(2,1)S(1)} %bitcast.61), custom_call_target="tpu_custom_call" | custom-call | flops 1073741824 | bytes 6291456 | tf_op jit(solution)/shard_map/queries/pallas_call | solution.py:113
  72.4 2.0 %collective-permute-start.11 = (bf16[2,256,256]{2,1,0:T(8,128)(2,1)S(1)}, bf16[2,256,256]{2,1,0:T(8,128)(2,1)S(1)}, u32[]{:S(2)}, u32[]{:S(2)}) collective-permute-start(bf16[2,256,256]{2,1,0:T(8,128)(2,1)S(1)} %get-tuple-element.17.refs_0_), channel_id=1, source_target_pairs={{0,4},{1,5},{2,6},{3,7},{4,8},{5,9},{6,10},{7,11},{8,12},{9,13},{1... | collective-permute-start | bytes 786440 | tf_op jit(solution)/shard_map/ppermute | solution.py:47
  74.4 4.0 %key_values.3 = (bf16[2,256,256]{2,1,0:T(8,128)(2,1)S(1)}, bf16[2,256,256]{2,1,0:T(8,128)(2,1)S(1)}) custom-call(s32[3]{0:T(128)S(1)} %pad_add_fusion.2.place, bf16[4,256,256]{2,1,0:T(8,128)(2,1)S(1)} %pad_maximum_fusion.2.b0, bf16[4,256,256]{2,1,0:T(8,128)(2,1)} %collective-permute-done.23.b1, bf16[4,256,256]{2,1,0:T(8,128)(2,1)} %collective-permute-done.24.b2, ...), custom_call_target="tpu_custom_call" | custom-call | flops 2147483648 | bytes 10485760 | tf_op jit(solution)/shard_map/key_values/pallas_call | solution.py:87
  78.4 3.1 %collective-permute-start.26 = (bf16[2,256,256]{2,1,0:T(8,128)(2,1)S(1)}, bf16[2,256,256]{2,1,0:T(8,128)(2,1)S(1)}, u32[]{:S(2)}, u32[]{:S(2)}) collective-permute-start(bf16[2,256,256]{2,1,0:T(8,128)(2,1)S(1)} %get-tuple-element.19.refs_8_), channel_id=1, source_target_pairs={{0,4},{1,5},{2,6},{3,7},{4,8},{5,9},{6,10},{7,11},{8,12},{9,13},{1... | collective-permute-start | bytes 786440 | tf_op jit(solution)/shard_map/ppermute | solution.py:47
  81.5 1.5 collective-permute-start.15
  83.6 5.7 %collective-permute-done.27.refs_10_ = bf16[2,256,256]{2,1,0:T(8,128)(2,1)S(1)} collective-permute-done((bf16[2,256,256]{2,1,0:T(8,128)(2,1)S(1)}, bf16[2,256,256]{2,1,0:T(8,128)(2,1)S(1)}, u32[]{:S(2)}, u32[]{:S(2)}) %collective-permute-start.27) | collective-permute-done | bytes 262176 | tf_op jit(solution)/shard_map/ppermute | solution.py:47
  89.6 1.1 collective-permute-done.15.refs_4_
  90.7 2.0 %collective-permute-start.13 = (bf16[256,256]{1,0:T(8,128)(2,1)S(1)}, bf16[256,256]{1,0:T(8,128)(2,1)S(1)}, u32[]{:S(2)}, u32[]{:S(2)}) collective-permute-start(bf16[256,256]{1,0:T(8,128)(2,1)S(1)} %slice_bitcast_fusion.7), channel_id=1, source_target_pairs={{0,4},{1,5},{2,6},{3,7},{4,8},{5,9},{6,10},{7,11},{8,12},{9,13},{1... | collective-permute-start | bytes 393224 | tf_op jit(solution)/shard_map/ppermute | solution.py:47
  92.8 2.3 %collective-permute-done.14 = bf16[256,256]{1,0:T(8,128)(2,1)S(1)} collective-permute-done((bf16[256,256]{1,0:T(8,128)(2,1)S(1)}, bf16[256,256]{1,0:T(8,128)(2,1)S(1)}, u32[]{:S(2)}, u32[]{:S(2)}) %collective-permute-start.14) | collective-permute-done | bytes 131104 | tf_op jit(solution)/shard_map/ppermute | solution.py:47
  95.9 1.9 %collective-permute-start.16 = (bf16[2,256,256]{2,1,0:T(8,128)(2,1)S(1)}, bf16[2,256,256]{2,1,0:T(8,128)(2,1)S(1)}, u32[]{:S(2)}, u32[]{:S(2)}) collective-permute-start(bf16[2,256,256]{2,1,0:T(8,128)(2,1)S(1)} %collective-permute-done.15.refs_4_), channel_id=1, source_target_pairs={{0,4},{1,5},{2,6},{3,7},{4,8},{5,9},{6,10},{7,11},{8,12},{9,13},{1... | collective-permute-start | bytes 786440 | tf_op jit(solution)/shard_map/ppermute | solution.py:47
  97.8 3.1 %collective-permute-start.28 = (bf16[256,256]{1,0:T(8,128)(2,1)S(1)}, bf16[256,256]{1,0:T(8,128)(2,1)S(1)}, u32[]{:S(2)}, u32[]{:S(2)}) collective-permute-start(bf16[256,256]{1,0:T(8,128)(2,1)S(1)} %slice_bitcast_fusion.3), channel_id=1, source_target_pairs={{0,4},{1,5},{2,6},{3,7},{4,8},{5,9},{6,10},{7,11},{8,12},{9,13},{1... | collective-permute-start | bytes 393224 | tf_op jit(solution)/shard_map/ppermute | solution.py:47
  101.6 1.8 collective-permute-done.16.refs_5_
  103.4 2.3 %collective-permute-start.31 = (bf16[2,256,256]{2,1,0:T(8,128)(2,1)S(1)}, bf16[2,256,256]{2,1,0:T(8,128)(2,1)S(1)}, u32[]{:S(2)}, u32[]{:S(2)}) collective-permute-start(bf16[2,256,256]{2,1,0:T(8,128)(2,1)S(1)} %collective-permute-done.30.refs_12_), channel_id=1, source_target_pairs={{0,4},{1,5},{2,6},{3,7},{4,8},{5,9},{6,10},{7,11},{8,12},{9,13},{1... | collective-permute-start | bytes 786440 | tf_op jit(solution)/shard_map/ppermute | solution.py:47
  105.8 2.7 %collective-permute-done.32.refs_14_ = bf16[2,256,256]{2,1,0:T(8,128)(2,1)S(1)} collective-permute-done((bf16[2,256,256]{2,1,0:T(8,128)(2,1)S(1)}, bf16[2,256,256]{2,1,0:T(8,128)(2,1)S(1)}, u32[]{:S(2)}, u32[]{:S(2)}) %collective-permute-start.32) | collective-permute-done | bytes 262176 | tf_op jit(solution)/shard_map/ppermute | solution.py:47
  108.5 1.7 collective-permute-done.31.refs_13_
  110.2 3.3 %collective-permute-start.18 = (bf16[256,256]{1,0:T(8,128)(2,1)S(1)}, bf16[256,256]{1,0:T(8,128)(2,1)S(1)}, u32[]{:S(2)}, u32[]{:S(2)}) collective-permute-start(bf16[256,256]{1,0:T(8,128)(2,1)S(1)} %slice_bitcast_fusion.5), channel_id=1, source_target_pairs={{0,4},{1,5},{2,6},{3,7},{4,8},{5,9},{6,10},{7,11},{8,12},{9,13},{1... | collective-permute-start | bytes 393224 | tf_op jit(solution)/shard_map/ppermute | solution.py:47
  113.6 1.9 %queries.3 = (bf16[256,256]{1,0:T(8,128)(2,1)S(1)}, bf16[256,256]{1,0:T(8,128)(2,1)S(1)}) custom-call(s32[3]{0:T(128)S(1)} %pad_add_fusion.2.place, bf16[128,4096]{1,0:T(8,128)(2,1)S(1)} %collective-permute-done.2.h0, bf16[128,4096]{1,0:T(8,128)(2,1)S(1)} %collective-permute-done.3.h1, bf16[4096,512]{1,0:T(8,128)(2,1)S(1)} %bitcast.62), custom_call_target="tpu_custom_call" | custom-call | flops 1073741824 | bytes 6291456 | tf_op jit(solution)/shard_map/queries/pallas_call | solution.py:113
  115.5 3.8 %collective-permute-start.33 = (bf16[256,256]{1,0:T(8,128)(2,1)S(1)}, bf16[256,256]{1,0:T(8,128)(2,1)S(1)}, u32[]{:S(2)}, u32[]{:S(2)}) collective-permute-start(bf16[256,256]{1,0:T(8,128)(2,1)S(1)} %slice_bitcast_fusion.1), channel_id=1, source_target_pairs={{0,4},{1,5},{2,6},{3,7},{4,8},{5,9},{6,10},{7,11},{8,12},{9,13},{1... | collective-permute-start | bytes 393224 | tf_op jit(solution)/shard_map/ppermute | solution.py:47
  119.3 1.6 collective-permute-start.4
  121.8 3.8 %collective-permute-done.4 = bf16[512,256]{1,0:T(8,128)(2,1)S(1)} collective-permute-done((bf16[512,256]{1,0:T(8,128)(2,1)S(1)}, bf16[512,256]{1,0:T(8,128)(2,1)S(1)}, u32[]{:S(2)}, u32[]{:S(2)}) %collective-permute-start.4) | collective-permute-done | bytes 262176 | tf_op jit(solution)/shard_map/ppermute | solution.py:47
  125.7 15.4 %attend.1 = bf16[1024,256]{1,0:T(8,128)(2,1)S(1)} custom-call(s32[16]{0:T(128)S(1)} %stack.134.spans, s32[2,4]{1,0:T(2,128)S(1)} %pad_add_fusion.query_span, s32[2,16]{1,0:T(2,128)S(1)} %pad_add_fusion.1.key_span, bf16[1024,256]{1,0:T(8,128)(2,1)S(1)} %pad_maximum_fusion.query, s32[1024,1]{1,0:T(8,128)S(1)} %copy-done.6, ...), custom_call_target="tpu_custom_call" | custom-call | flops 2147483648 | bytes 6291456 | tf_op jit(solution)/shard_map/attend/pallas_call | solution.py:162
  141.1 1.7 collective-permute-start.35
  142.8 4.8 %collective-permute-done.35 = bf16[512,256]{1,0:T(8,128)(2,1)S(1)} collective-permute-done((bf16[512,256]{1,0:T(8,128)(2,1)S(1)}, bf16[512,256]{1,0:T(8,128)(2,1)S(1)}, u32[]{:S(2)}, u32[]{:S(2)}) %collective-permute-start.35) | collective-permute-done | bytes 262176 | tf_op jit(solution)/shard_map/ppermute | solution.py:47
  147.6 2.7 %outputs.3 = bf16[256,4096]{1,0:T(8,128)(2,1)S(1)} custom-call(s32[3]{0:T(128)S(1)} %pad_add_fusion.2.place, bf16[256,256]{1,0:T(8,128)(2,1)S(1)} %get-tuple-element.34.mine, bf16[256,256]{1,0:T(8,128)(2,1)S(1)} %get-tuple-element.36.other, bf16[512,4096]{1,0:T(8,128)(2,1)S(1)} %bitcast.67), custom_call_target="tpu_custom_call" | custom-call | flops 1073741824 | bytes 6291456 | tf_op jit(solution)/shard_map/outputs/pallas_call | solution.py:189
  150.5 2.7 %outputs.2 = bf16[256,4096]{1,0:T(8,128)(2,1)S(1)} custom-call(s32[3]{0:T(128)S(1)} %pad_add_fusion.2.place, bf16[256,256]{1,0:T(8,128)(2,1)S(1)} %get-tuple-element.33.mine, bf16[256,256]{1,0:T(8,128)(2,1)S(1)} %get-tuple-element.35.other, bf16[512,4096]{1,0:T(8,128)(2,1)S(1)} %bitcast.68), custom_call_target="tpu_custom_call" | custom-call | flops 1073741824 | bytes 6291456 | tf_op jit(solution)/shard_map/outputs/pallas_call | solution.py:189
  154.1 3.1 %collective-permute-start.38 = (bf16[128,4096]{1,0:T(8,128)(2,1)S(1)}, bf16[128,4096]{1,0:T(8,128)(2,1)S(1)}, u32[]{:S(2)}, u32[]{:S(2)}) collective-permute-start(bf16[128,4096]{1,0:T(8,128)(2,1)S(1)} %add_convert_fusion), channel_id=1, source_target_pairs={{0,18},{1,19},{2,16},{3,17},{4,22},{5,23},{6,20},{7,21},{8,26},{9,... | collective-permute-start | bytes 3145736 | tf_op jit(solution)/shard_map/ppermute | solution.py:47
  157.2 23.4 %collective-permute-done.38 = bf16[128,4096]{1,0:T(8,128)(2,1)S(1)} collective-permute-done((bf16[128,4096]{1,0:T(8,128)(2,1)S(1)}, bf16[128,4096]{1,0:T(8,128)(2,1)S(1)}, u32[]{:S(2)}, u32[]{:S(2)}) %collective-permute-start.38) | collective-permute-done | bytes 1048608 | tf_op jit(solution)/shard_map/ppermute | solution.py:47
  180.6 1.6 fusion.4
  (108 shorter events, 9.7 us)
Async XLA Ops:
  0.0 6.3 %copy-start.10 = (bf16[1,4096]{1,0:T(2,128)(2,1)S(1)}, bf16[1,4096]{1,0:T(2,128)(2,1)}, u32[]{:S(2)}) copy-start(bf16[1,4096]{1,0:T(2,128)(2,1)} %param.11) | copy-start | bytes 24580
  0.0 6.3 %copy-start.7 = (bf16[1,128,4096]{2,1,0:T(8,128)(2,1)S(1)}, bf16[1,128,4096]{2,1,0:T(8,128)(2,1)}, u32[]{:S(2)}) copy-start(bf16[1,128,4096]{2,1,0:T(8,128)(2,1)} %param.9) | copy-start | bytes 3145732
  2.1 7.9 %collective-permute-start.7 = (bf16[1,256,256]{2,1,0:T(8,128)(2,1)S(1)}, bf16[1,256,256]{2,1,0:T(8,128)(2,1)S(1)}, u32[]{:S(2)}, u32[]{:S(2)}) collective-permute-start(bf16[1,256,256]{2,1,0:T(8,128)(2,1)S(1)} %get-tuple-element.27), channel_id=1, source_target_pairs={{0,64},{1,65},{2,66},{3,67},{4,68},{5,69},{6,70},{7,71},{8,72},{9,... | collective-permute-start | bytes 393224 | tf_op jit(solution)/shard_map/ppermute | solution.py:47
  4.3 7.4 %collective-permute-start.6 = (bf16[1,256,256]{2,1,0:T(8,128)(2,1)S(1)}, bf16[1,256,256]{2,1,0:T(8,128)(2,1)S(1)}, u32[]{:S(2)}, u32[]{:S(2)}) collective-permute-start(bf16[1,256,256]{2,1,0:T(8,128)(2,1)S(1)} %get-tuple-element.28), channel_id=1, source_target_pairs={{0,96},{1,97},{2,98},{3,99},{4,100},{5,101},{6,102},{7,103},{8,104... | collective-permute-start | bytes 393224 | tf_op jit(solution)/shard_map/ppermute | solution.py:47
  5.7 6.0 %collective-permute-start.5 = (bf16[1,256,256]{2,1,0:T(8,128)(2,1)S(1)}, bf16[1,256,256]{2,1,0:T(8,128)(2,1)S(1)}, u32[]{:S(2)}, u32[]{:S(2)}) collective-permute-start(bf16[1,256,256]{2,1,0:T(8,128)(2,1)S(1)} %get-tuple-element.29), channel_id=1, source_target_pairs={{0,32},{1,33},{2,34},{3,35},{4,36},{5,37},{6,38},{7,39},{8,40},{9,... | collective-permute-start | bytes 393224 | tf_op jit(solution)/shard_map/ppermute | solution.py:47
  6.3 14.9 %copy-start.11 = (s32[1,4096]{1,0:T(1,128)S(1)}, s32[1,4096]{1,0:T(1,128)}, u32[]{:S(2)}) copy-start(s32[1,4096]{1,0:T(1,128)} %param.17) | copy-start | bytes 49156
  6.3 19.7 %copy-start.12 = (s32[1,512]{1,0:T(1,128)S(1)}, s32[1,512]{1,0:T(1,128)}, u32[]{:S(2)}) copy-start(s32[1,512]{1,0:T(1,128)} %param.16) | copy-start | bytes 6148
  11.8 19.7 %collective-permute-start.9 = (bf16[4,256,256]{2,1,0:T(8,128)(2,1)S(1)}, bf16[4,256,256]{2,1,0:T(8,128)(2,1)}, u32[]{:S(2)}, u32[]{:S(2)}) collective-permute-start(bf16[4,256,256]{2,1,0:T(8,128)(2,1)S(1)} %pad_maximum_fusion.1.b0), channel_id=1, source_target_pairs={{0,2},{1,3},{2,0},{3,1},{4,6},{5,7},{6,4},{7,5},{8,10},{9,11},{10,... | collective-permute-start | bytes 1572872 | tf_op jit(solution)/shard_map/ppermute | solution.py:47
  15.4 45.5 %collective-permute-start.2 = (bf16[128,4096]{1,0:T(8,128)(2,1)S(1)}, bf16[128,4096]{1,0:T(8,128)(2,1)S(1)}, u32[]{:S(2)}, u32[]{:S(2)}) collective-permute-start(bf16[128,4096]{1,0:T(8,128)(2,1)S(1)} %fusion.2.h0), channel_id=1, source_target_pairs={{0,18},{1,19},{2,16},{3,17},{4,22},{5,23},{6,20},{7,21},{8,26},{9,... | collective-permute-start | bytes 3145736 | tf_op jit(solution)/shard_map/ppermute | solution.py:47
  16.5 8.0 %collective-permute-start.22 = (bf16[1,256,256]{2,1,0:T(8,128)(2,1)}, bf16[1,256,256]{2,1,0:T(8,128)(2,1)S(1)}, u32[]{:S(2)}, u32[]{:S(2)}) collective-permute-start(bf16[1,256,256]{2,1,0:T(8,128)(2,1)} %get-tuple-element.31), channel_id=1, source_target_pairs={{0,64},{1,65},{2,66},{3,67},{4,68},{5,69},{6,70},{7,71},{8,72},{9,... | collective-permute-start | bytes 393224 | tf_op jit(solution)/shard_map/ppermute | solution.py:47
  18.6 7.4 %collective-permute-start.21 = (bf16[1,256,256]{2,1,0:T(8,128)(2,1)}, bf16[1,256,256]{2,1,0:T(8,128)(2,1)}, u32[]{:S(2)}, u32[]{:S(2)}) collective-permute-start(bf16[1,256,256]{2,1,0:T(8,128)(2,1)} %get-tuple-element.32), channel_id=1, source_target_pairs={{0,96},{1,97},{2,98},{3,99},{4,100},{5,101},{6,102},{7,103},{8,104... | collective-permute-start | bytes 393224 | tf_op jit(solution)/shard_map/ppermute | solution.py:47
  20.0 5.9 %collective-permute-start.20 = (bf16[1,256,256]{2,1,0:T(8,128)(2,1)S(1)}, bf16[1,256,256]{2,1,0:T(8,128)(2,1)}, u32[]{:S(2)}, u32[]{:S(2)}) collective-permute-start(bf16[1,256,256]{2,1,0:T(8,128)(2,1)S(1)} %get-tuple-element.26), channel_id=1, source_target_pairs={{0,32},{1,33},{2,34},{3,35},{4,36},{5,37},{6,38},{7,39},{8,40},{9,... | collective-permute-start | bytes 393224 | tf_op jit(solution)/shard_map/ppermute | solution.py:47
  24.5 45.2 %collective-permute-start.1 = (bf16[128,4096]{1,0:T(8,128)(2,1)S(1)}, bf16[128,4096]{1,0:T(8,128)(2,1)}, u32[]{:S(2)}, u32[]{:S(2)}) collective-permute-start(bf16[128,4096]{1,0:T(8,128)(2,1)S(1)} %fusion.2.h0), channel_id=1, source_target_pairs={{0,1},{1,0},{2,3},{3,2},{4,5},{5,4},{6,7},{7,6},{8,9},{9,8},{10,11... | collective-permute-start | bytes 3145736 | tf_op jit(solution)/shard_map/ppermute | solution.py:47
  26.0 3.6 %collective-permute-start = (s32[4,128]{1,0:T(4,128)S(1)}, s32[4,128]{1,0:T(4,128)S(1)}, u32[]{:S(2)}, u32[]{:S(2)}) collective-permute-start(s32[4,128]{1,0:T(4,128)S(1)} %bitcast.79), channel_id=1, source_target_pairs={{0,16},{1,17},{2,18},{3,19},{4,20},{5,21},{6,22},{7,23},{8,24},{9,... | collective-permute-start | bytes 6152 | tf_op jit(solution)/shard_map/ppermute | solution.py:47
  26.0 5.7 %collective-permute-start.8 = (bf16[4,256,256]{2,1,0:T(8,128)(2,1)S(1)}, bf16[4,256,256]{2,1,0:T(8,128)(2,1)}, u32[]{:S(2)}, u32[]{:S(2)}) collective-permute-start(bf16[4,256,256]{2,1,0:T(8,128)(2,1)S(1)} %pad_maximum_fusion.1.b0), channel_id=1, source_target_pairs={{0,1},{1,0},{2,3},{3,2},{4,5},{5,4},{6,7},{7,6},{8,9},{9,8},{10,11... | collective-permute-start | bytes 1572872 | tf_op jit(solution)/shard_map/ppermute | solution.py:47
  29.6 14.3 %collective-permute-start.24 = (bf16[4,256,256]{2,1,0:T(8,128)(2,1)S(1)}, bf16[4,256,256]{2,1,0:T(8,128)(2,1)}, u32[]{:S(2)}, u32[]{:S(2)}) collective-permute-start(bf16[4,256,256]{2,1,0:T(8,128)(2,1)S(1)} %pad_maximum_fusion.2.b0), channel_id=1, source_target_pairs={{0,2},{1,3},{2,0},{3,1},{4,6},{5,7},{6,4},{7,5},{8,10},{9,11},{10,... | collective-permute-start | bytes 1572872 | tf_op jit(solution)/shard_map/ppermute | solution.py:47
  31.5 29.4 %collective-permute-start.10 = (bf16[4,256,256]{2,1,0:T(8,128)(2,1)}, bf16[4,256,256]{2,1,0:T(8,128)(2,1)}, u32[]{:S(2)}, u32[]{:S(2)}) collective-permute-start(bf16[4,256,256]{2,1,0:T(8,128)(2,1)} %collective-permute-done.9.b2), channel_id=1, source_target_pairs={{0,1},{1,0},{2,3},{3,2},{4,5},{5,4},{6,7},{7,6},{8,9},{9,8},{10,11... | collective-permute-start | bytes 1572872 | tf_op jit(solution)/shard_map/ppermute | solution.py:47
  31.7 42.6 %collective-permute-start.23 = (bf16[4,256,256]{2,1,0:T(8,128)(2,1)S(1)}, bf16[4,256,256]{2,1,0:T(8,128)(2,1)}, u32[]{:S(2)}, u32[]{:S(2)}) collective-permute-start(bf16[4,256,256]{2,1,0:T(8,128)(2,1)S(1)} %pad_maximum_fusion.2.b0), channel_id=1, source_target_pairs={{0,1},{1,0},{2,3},{3,2},{4,5},{5,4},{6,7},{7,6},{8,9},{9,8},{10,11... | collective-permute-start | bytes 1572872 | tf_op jit(solution)/shard_map/ppermute | solution.py:47
  43.8 30.5 %collective-permute-start.25 = (bf16[4,256,256]{2,1,0:T(8,128)(2,1)}, bf16[4,256,256]{2,1,0:T(8,128)(2,1)}, u32[]{:S(2)}, u32[]{:S(2)}) collective-permute-start(bf16[4,256,256]{2,1,0:T(8,128)(2,1)} %collective-permute-done.24.b2), channel_id=1, source_target_pairs={{0,1},{1,0},{2,3},{3,2},{4,5},{5,4},{6,7},{7,6},{8,9},{9,8},{10,11... | collective-permute-start | bytes 1572872 | tf_op jit(solution)/shard_map/ppermute | solution.py:47
  60.9 52.6 %collective-permute-start.3 = (bf16[128,4096]{1,0:T(8,128)(2,1)S(1)}, bf16[128,4096]{1,0:T(8,128)(2,1)S(1)}, u32[]{:S(2)}, u32[]{:S(2)}) collective-permute-start(bf16[128,4096]{1,0:T(8,128)(2,1)S(1)} %collective-permute-done.2.h0), channel_id=1, source_target_pairs={{0,1},{1,0},{2,3},{3,2},{4,5},{5,4},{6,7},{7,6},{8,9},{9,8},{10,11... | collective-permute-start | bytes 3145736 | tf_op jit(solution)/shard_map/ppermute | solution.py:47
  65.3 9.1 %copy-start.4 = (bf16[1,4096,512]{2,1,0:T(8,128)(2,1)S(1)}, bf16[1,4096,512]{2,1,0:T(8,128)(2,1)}, u32[]{:S(2)}) copy-start(bf16[1,4096,512]{2,1,0:T(8,128)(2,1)} %param.14) | copy-start | bytes 12582916
  69.5 12.0 %collective-permute-start.12 = (bf16[2,256,256]{2,1,0:T(8,128)(2,1)S(1)}, bf16[2,256,256]{2,1,0:T(8,128)(2,1)S(1)}, u32[]{:S(2)}, u32[]{:S(2)}) collective-permute-start(bf16[2,256,256]{2,1,0:T(8,128)(2,1)S(1)} %get-tuple-element.17.refs_0_), channel_id=1, source_target_pairs={{0,12},{1,13},{2,14},{3,15},{4,0},{5,1},{6,2},{7,3},{8,4},{9,5},{1... | collective-permute-start | bytes 786440 | tf_op jit(solution)/shard_map/ppermute | solution.py:47
  69.6 4.7 %copy-start.2 = (bf16[1,4096,512]{2,1,0:T(8,128)(2,1)S(1)}, bf16[1,4096,512]{2,1,0:T(8,128)(2,1)}, u32[]{:S(2)}) copy-start(bf16[1,4096,512]{2,1,0:T(8,128)(2,1)} %param.13) | copy-start | bytes 12582916
  72.4 10.7 %collective-permute-start.11 = (bf16[2,256,256]{2,1,0:T(8,128)(2,1)S(1)}, bf16[2,256,256]{2,1,0:T(8,128)(2,1)S(1)}, u32[]{:S(2)}, u32[]{:S(2)}) collective-permute-start(bf16[2,256,256]{2,1,0:T(8,128)(2,1)S(1)} %get-tuple-element.17.refs_0_), channel_id=1, source_target_pairs={{0,4},{1,5},{2,6},{3,7},{4,8},{5,9},{6,10},{7,11},{8,12},{9,13},{1... | collective-permute-start | bytes 786440 | tf_op jit(solution)/shard_map/ppermute | solution.py:47
  78.4 14.4 %collective-permute-start.26 = (bf16[2,256,256]{2,1,0:T(8,128)(2,1)S(1)}, bf16[2,256,256]{2,1,0:T(8,128)(2,1)S(1)}, u32[]{:S(2)}, u32[]{:S(2)}) collective-permute-start(bf16[2,256,256]{2,1,0:T(8,128)(2,1)S(1)} %get-tuple-element.19.refs_8_), channel_id=1, source_target_pairs={{0,4},{1,5},{2,6},{3,7},{4,8},{5,9},{6,10},{7,11},{8,12},{9,13},{1... | collective-permute-start | bytes 786440 | tf_op jit(solution)/shard_map/ppermute | solution.py:47
  81.5 7.9 %collective-permute-start.27 = (bf16[2,256,256]{2,1,0:T(8,128)(2,1)S(1)}, bf16[2,256,256]{2,1,0:T(8,128)(2,1)S(1)}, u32[]{:S(2)}, u32[]{:S(2)}) collective-permute-start(bf16[2,256,256]{2,1,0:T(8,128)(2,1)S(1)} %get-tuple-element.19.refs_8_), channel_id=1, source_target_pairs={{0,12},{1,13},{2,14},{3,15},{4,0},{5,1},{6,2},{7,3},{8,4},{9,5},{1... | collective-permute-start | bytes 786440 | tf_op jit(solution)/shard_map/ppermute | solution.py:47
  81.5 9.2 %collective-permute-start.15 = (bf16[2,256,256]{2,1,0:T(8,128)(2,1)S(1)}, bf16[2,256,256]{2,1,0:T(8,128)(2,1)S(1)}, u32[]{:S(2)}, u32[]{:S(2)}) collective-permute-start(bf16[2,256,256]{2,1,0:T(8,128)(2,1)S(1)} %get-tuple-element.18), channel_id=1, source_target_pairs={{0,16},{1,17},{2,18},{3,19},{4,20},{5,21},{6,22},{7,23},{8,24},{9,... | collective-permute-start | bytes 786440 | tf_op jit(solution)/shard_map/ppermute | solution.py:47
  83.0 14.8 %collective-permute-start.30 = (bf16[2,256,256]{2,1,0:T(8,128)(2,1)S(1)}, bf16[2,256,256]{2,1,0:T(8,128)(2,1)S(1)}, u32[]{:S(2)}, u32[]{:S(2)}) collective-permute-start(bf16[2,256,256]{2,1,0:T(8,128)(2,1)S(1)} %get-tuple-element.20), channel_id=1, source_target_pairs={{0,16},{1,17},{2,18},{3,19},{4,20},{5,21},{6,22},{7,23},{8,24},{9,... | collective-permute-start | bytes 786440 | tf_op jit(solution)/shard_map/ppermute | solution.py:47
  89.3 5.7 %collective-permute-start.14 = (bf16[256,256]{1,0:T(8,128)(2,1)S(1)}, bf16[256,256]{1,0:T(8,128)(2,1)S(1)}, u32[]{:S(2)}, u32[]{:S(2)}) collective-permute-start(bf16[256,256]{1,0:T(8,128)(2,1)S(1)} %slice_bitcast_fusion.6), channel_id=1, source_target_pairs={{0,12},{1,13},{2,14},{3,15},{4,0},{5,1},{6,2},{7,3},{8,4},{9,5},{1... | collective-permute-start | bytes 393224 | tf_op jit(solution)/shard_map/ppermute | solution.py:47
  90.7 5.2 %collective-permute-start.13 = (bf16[256,256]{1,0:T(8,128)(2,1)S(1)}, bf16[256,256]{1,0:T(8,128)(2,1)S(1)}, u32[]{:S(2)}, u32[]{:S(2)}) collective-permute-start(bf16[256,256]{1,0:T(8,128)(2,1)S(1)} %slice_bitcast_fusion.7), channel_id=1, source_target_pairs={{0,4},{1,5},{2,6},{3,7},{4,8},{5,9},{6,10},{7,11},{8,12},{9,13},{1... | collective-permute-start | bytes 393224 | tf_op jit(solution)/shard_map/ppermute | solution.py:47
  92.8 8.6 %collective-permute-start.17 = (bf16[2,256,256]{2,1,0:T(8,128)(2,1)S(1)}, bf16[2,256,256]{2,1,0:T(8,128)(2,1)S(1)}, u32[]{:S(2)}, u32[]{:S(2)}) collective-permute-start(bf16[2,256,256]{2,1,0:T(8,128)(2,1)S(1)} %collective-permute-done.15.refs_4_), channel_id=1, source_target_pairs={{0,12},{1,13},{2,14},{3,15},{4,0},{5,1},{6,2},{7,3},{8,4},{9,5},{1... | collective-permute-start | bytes 786440 | tf_op jit(solution)/shard_map/ppermute | solution.py:47
  95.0 20.4 %collective-permute-start.29 = (bf16[256,256]{1,0:T(8,128)(2,1)S(1)}, bf16[256,256]{1,0:T(8,128)(2,1)S(1)}, u32[]{:S(2)}, u32[]{:S(2)}) collective-permute-start(bf16[256,256]{1,0:T(8,128)(2,1)S(1)} %slice_bitcast_fusion.2), channel_id=1, source_target_pairs={{0,12},{1,13},{2,14},{3,15},{4,0},{5,1},{6,2},{7,3},{8,4},{9,5},{1... | collective-permute-start | bytes 393224 | tf_op jit(solution)/shard_map/ppermute | solution.py:47
  95.9 7.5 %collective-permute-start.16 = (bf16[2,256,256]{2,1,0:T(8,128)(2,1)S(1)}, bf16[2,256,256]{2,1,0:T(8,128)(2,1)S(1)}, u32[]{:S(2)}, u32[]{:S(2)}) collective-permute-start(bf16[2,256,256]{2,1,0:T(8,128)(2,1)S(1)} %collective-permute-done.15.refs_4_), channel_id=1, source_target_pairs={{0,4},{1,5},{2,6},{3,7},{4,8},{5,9},{6,10},{7,11},{8,12},{9,13},{1... | collective-permute-start | bytes 786440 | tf_op jit(solution)/shard_map/ppermute | solution.py:47
  97.8 21.4 %collective-permute-start.28 = (bf16[256,256]{1,0:T(8,128)(2,1)S(1)}, bf16[256,256]{1,0:T(8,128)(2,1)S(1)}, u32[]{:S(2)}, u32[]{:S(2)}) collective-permute-start(bf16[256,256]{1,0:T(8,128)(2,1)S(1)} %slice_bitcast_fusion.3), channel_id=1, source_target_pairs={{0,4},{1,5},{2,6},{3,7},{4,8},{5,9},{6,10},{7,11},{8,12},{9,13},{1... | collective-permute-start | bytes 393224 | tf_op jit(solution)/shard_map/ppermute | solution.py:47
  101.3 7.1 %collective-permute-start.32 = (bf16[2,256,256]{2,1,0:T(8,128)(2,1)S(1)}, bf16[2,256,256]{2,1,0:T(8,128)(2,1)S(1)}, u32[]{:S(2)}, u32[]{:S(2)}) collective-permute-start(bf16[2,256,256]{2,1,0:T(8,128)(2,1)S(1)} %collective-permute-done.30.refs_12_), channel_id=1, source_target_pairs={{0,12},{1,13},{2,14},{3,15},{4,0},{5,1},{6,2},{7,3},{8,4},{9,5},{1... | collective-permute-start | bytes 786440 | tf_op jit(solution)/shard_map/ppermute | solution.py:47
  103.4 6.8 %collective-permute-start.31 = (bf16[2,256,256]{2,1,0:T(8,128)(2,1)S(1)}, bf16[2,256,256]{2,1,0:T(8,128)(2,1)S(1)}, u32[]{:S(2)}, u32[]{:S(2)}) collective-permute-start(bf16[2,256,256]{2,1,0:T(8,128)(2,1)S(1)} %collective-permute-done.30.refs_12_), channel_id=1, source_target_pairs={{0,4},{1,5},{2,6},{3,7},{4,8},{5,9},{6,10},{7,11},{8,12},{9,13},{1... | collective-permute-start | bytes 786440 | tf_op jit(solution)/shard_map/ppermute | solution.py:47
  108.4 12.4 %collective-permute-start.19 = (bf16[256,256]{1,0:T(8,128)(2,1)S(1)}, bf16[256,256]{1,0:T(8,128)(2,1)S(1)}, u32[]{:S(2)}, u32[]{:S(2)}) collective-permute-start(bf16[256,256]{1,0:T(8,128)(2,1)S(1)} %slice_bitcast_fusion.4), channel_id=1, source_target_pairs={{0,12},{1,13},{2,14},{3,15},{4,0},{5,1},{6,2},{7,3},{8,4},{9,5},{1... | collective-permute-start | bytes 393224 | tf_op jit(solution)/shard_map/ppermute | solution.py:47
  110.2 10.7 %collective-permute-start.18 = (bf16[256,256]{1,0:T(8,128)(2,1)S(1)}, bf16[256,256]{1,0:T(8,128)(2,1)S(1)}, u32[]{:S(2)}, u32[]{:S(2)}) collective-permute-start(bf16[256,256]{1,0:T(8,128)(2,1)S(1)} %slice_bitcast_fusion.5), channel_id=1, source_target_pairs={{0,4},{1,5},{2,6},{3,7},{4,8},{5,9},{6,10},{7,11},{8,12},{9,13},{1... | collective-permute-start | bytes 393224 | tf_op jit(solution)/shard_map/ppermute | solution.py:47
  113.5 7.4 %collective-permute-start.34 = (bf16[256,256]{1,0:T(8,128)(2,1)S(1)}, bf16[256,256]{1,0:T(8,128)(2,1)S(1)}, u32[]{:S(2)}, u32[]{:S(2)}) collective-permute-start(bf16[256,256]{1,0:T(8,128)(2,1)S(1)} %slice_bitcast_fusion), channel_id=1, source_target_pairs={{0,12},{1,13},{2,14},{3,15},{4,0},{5,1},{6,2},{7,3},{8,4},{9,5},{1... | collective-permute-start | bytes 393224 | tf_op jit(solution)/shard_map/ppermute | solution.py:47
  115.4 10.2 %copy-start.6 = (s32[1024,1]{1,0:T(8,128)S(1)}, s32[1024,1]{1,0:T(8,128)}, u32[]{:S(2)}) copy-start(s32[1024,1]{1,0:T(8,128)} %copy.10.query_ids) | copy-start | bytes 12292
  115.5 6.3 %collective-permute-start.33 = (bf16[256,256]{1,0:T(8,128)(2,1)S(1)}, bf16[256,256]{1,0:T(8,128)(2,1)S(1)}, u32[]{:S(2)}, u32[]{:S(2)}) collective-permute-start(bf16[256,256]{1,0:T(8,128)(2,1)S(1)} %slice_bitcast_fusion.1), channel_id=1, source_target_pairs={{0,4},{1,5},{2,6},{3,7},{4,8},{5,9},{6,10},{7,11},{8,12},{9,13},{1... | collective-permute-start | bytes 393224 | tf_op jit(solution)/shard_map/ppermute | solution.py:47
  119.3 6.4 %collective-permute-start.4 = (bf16[512,256]{1,0:T(8,128)(2,1)S(1)}, bf16[512,256]{1,0:T(8,128)(2,1)S(1)}, u32[]{:S(2)}, u32[]{:S(2)}) collective-permute-start(bf16[512,256]{1,0:T(8,128)(2,1)S(1)} %pad_maximum_fusion.3), channel_id=1, source_target_pairs={{0,16},{1,17},{2,18},{3,19},{4,20},{5,21},{6,22},{7,23},{8,24},{9,... | collective-permute-start | bytes 786440 | tf_op jit(solution)/shard_map/ppermute | solution.py:47
  125.7 21.9 %copy-start.5 = (bf16[1,512,4096]{2,1,0:T(8,128)(2,1)S(1)}, bf16[1,512,4096]{2,1,0:T(8,128)(2,1)}, u32[]{:S(2)}) copy-start(bf16[1,512,4096]{2,1,0:T(8,128)(2,1)} %param.15) | copy-start | bytes 12582916
  141.1 6.5 %collective-permute-start.35 = (bf16[512,256]{1,0:T(8,128)(2,1)S(1)}, bf16[512,256]{1,0:T(8,128)(2,1)S(1)}, u32[]{:S(2)}, u32[]{:S(2)}) collective-permute-start(bf16[512,256]{1,0:T(8,128)(2,1)S(1)} %slice.87), channel_id=1, source_target_pairs={{0,16},{1,17},{2,18},{3,19},{4,20},{5,21},{6,22},{7,23},{8,24},{9,... | collective-permute-start | bytes 786440 | tf_op jit(solution)/shard_map/ppermute | solution.py:47
  150.4 3.5 %collective-permute-start.37 = (bf16[128,4096]{1,0:T(8,128)(2,1)S(1)}, bf16[128,4096]{1,0:T(8,128)(2,1)S(1)}, u32[]{:S(2)}, u32[]{:S(2)}) collective-permute-start(bf16[128,4096]{1,0:T(8,128)(2,1)S(1)} %slice.94), channel_id=1, source_target_pairs={{0,1},{1,0},{2,3},{3,2},{4,5},{5,4},{6,7},{7,6},{8,9},{9,8},{10,11... | collective-permute-start | bytes 3145736 | tf_op jit(solution)/shard_map/ppermute | solution.py:47
  153.3 27.3 %copy-start.8 = (bf16[1,128,4096]{2,1,0:T(8,128)(2,1)S(1)}, bf16[1,128,4096]{2,1,0:T(8,128)(2,1)}, u32[]{:S(2)}) copy-start(bf16[1,128,4096]{2,1,0:T(8,128)(2,1)} %param.9) | copy-start | bytes 3145732
  153.3 3.9 %collective-permute-start.36 = (bf16[128,4096]{1,0:T(8,128)(2,1)S(1)}, bf16[128,4096]{1,0:T(8,128)(2,1)S(1)}, u32[]{:S(2)}, u32[]{:S(2)}) collective-permute-start(bf16[128,4096]{1,0:T(8,128)(2,1)S(1)} %slice.90), channel_id=1, source_target_pairs={{0,1},{1,0},{2,3},{3,2},{4,5},{5,4},{6,7},{7,6},{8,9},{9,8},{10,11... | collective-permute-start | bytes 3145736 | tf_op jit(solution)/shard_map/ppermute | solution.py:47
  154.1 26.5 %collective-permute-start.38 = (bf16[128,4096]{1,0:T(8,128)(2,1)S(1)}, bf16[128,4096]{1,0:T(8,128)(2,1)S(1)}, u32[]{:S(2)}, u32[]{:S(2)}) collective-permute-start(bf16[128,4096]{1,0:T(8,128)(2,1)S(1)} %add_convert_fusion), channel_id=1, source_target_pairs={{0,18},{1,19},{2,16},{3,17},{4,22},{5,23},{6,20},{7,21},{8,26},{9,... | collective-permute-start | bytes 3145736 | tf_op jit(solution)/shard_map/ppermute | solution.py:47
  (4 other events, 10.3 us)

commit v2 on v0

v2 whole, which is shorter than its diff:
```python
import functools
import math

import jax
import jax.numpy as jnp
from jax import lax
from jax.experimental import pallas as pl
from jax.experimental.pallas import tpu as pltpu
from jax.sharding import PartitionSpec as P

HD = 256
AXES = ("section", "seq", "mp")
SHAPE = (4, 2, 4, 2, 2)
KEYS = 256
ATTEND_ROWS = 512
MIB = 1 << 20
F32 = jnp.float32
BF16 = jnp.bfloat16


def route(target):
    pairs = []
    for source in range(math.prod(SHAPE)):
        at, rest = [], source
        for size in reversed(SHAPE):
            at.append(rest % size)
            rest //= size
        there = 0
        for place, size in zip(target(*reversed(at)), SHAPE):
            there = there * size + place % size
        pairs.append((source, there))
    return pairs


CORE = route(lambda x, l, z, h, c: (x, l, z, h, c + 1))
Y_FAR = route(lambda x, l, z, h, c: (x, l, z, h + 1, c))
Y_CUT = route(lambda x, l, z, h, c: (x, l + 1, z, h + 1, c))
Y_LOW_CORE = route(lambda x, l, z, h, c: (x, l + 1, z, h, c + 1))
Y_LOW = route(lambda x, l, z, h, c: (x, l + 1, z, h, c))
Z_UP = route(lambda x, l, z, h, c: (x, l, z + 1, h, c))
Z_DOWN = route(lambda x, l, z, h, c: (x, l, z - 1, h, c))
X_UP = route(lambda x, l, z, h, c: (x + 1, l, z, h, c))
X_DOWN = route(lambda x, l, z, h, c: (x - 1, l, z, h, c))
X_TWO = route(lambda x, l, z, h, c: (x + 2, l, z, h, c))
X_ORDER = (0, -1, 1, 2)


def send(array, pairs):
    return lax.ppermute(array, AXES, pairs)


def vmem(count):
    return [pl.BlockSpec(memory_space=pltpu.VMEM)] * count


def smem(count):
    return [pl.BlockSpec(memory_space=pltpu.SMEM)] * count


def params(mib):
    return pltpu.CompilerParams(vmem_limit_bytes=mib * MIB)


def normed_rows(layer_rows, gain):
    widened = layer_rows.astype(F32)
    mean_square = jnp.mean(widened * widened, axis=-1, keepdims=True)
    return (widened * lax.rsqrt(mean_square + 1e-06) * gain.astype(F32)).astype(BF16)


def dot(a, b):
    return jnp.dot(a, b, preferred_element_type=F32)


def fetch(source, held, arrived, pieces, piece):
    copies = [
        pltpu.make_async_copy(source.at[piece(at)], held.at[piece(at)], arrived.at[at])
        for at in range(pieces)
    ]
    for copy in copies:
        copy.start()
    return lambda at: copies[at].wait()


def row_piece(at):
    return (pl.ds(at * 1024, 1024),)


def key_value_kernel(place, *refs):
    blocks, (w_key, w_value, mine, other, panel, keys, values, sums, arrived) = refs[:16], refs[16:]
    wait_key = fetch(w_key, keys, arrived.at[0], 4, row_piece)
    wait_value = fetch(w_value, values, arrived.at[1], 4, row_piece)
    for at, block in enumerate(blocks):
        step, flip = divmod(at, 4)
        column = place[3 + step] * 1024 + jnp.bitwise_xor(place[2], flip) * 256
        panel[:, pl.ds(pl.multiple_of(column, 256), 256)] = block[0]
    for step in range(4):
        block = panel[:, step * 1024 : (step + 1) * 1024]
        for at, (wait, held) in enumerate(((wait_key, keys), (wait_value, values))):
            wait(step)
            product = dot(block, held[step * 1024 : (step + 1) * 1024])
            if step == 0:
                sums[at] = product
            else:
                sums[at] += product
    for out, side in ((mine, place[1]), (other, 1 - place[1])):
        for at in range(2):
            out[at] = sums[at, :, pl.ds(pl.multiple_of(side * HD, HD), HD)].astype(BF16)


def hbm(count):
    return [pl.BlockSpec(memory_space=pltpu.HBM)] * count


def key_values(place, blocks, w_key, w_value):
    rows = blocks[0].shape[1]
    out = jax.ShapeDtypeStruct((2, rows, HD), BF16)
    return pl.pallas_call(
        key_value_kernel,
        out_shape=(out, out),
        in_specs=smem(1) + vmem(16) + hbm(2),
        out_specs=tuple(vmem(2)),
        scratch_shapes=[
            pltpu.VMEM((rows, 4096), BF16),
            pltpu.VMEM((4096, 512), BF16),
            pltpu.VMEM((4096, 512), BF16),
            pltpu.VMEM((2, rows, 512), F32),
            pltpu.SemaphoreType.DMA((2, 4)),
        ],
        compiler_params=params(48),
        cost_estimate=pl.CostEstimate(
            flops=2 * rows * 4096 * 1024, bytes_accessed=8 * MIB + rows * 8192, transcendentals=0
        ),
        name="key_values",
    )(place, *blocks, w_key, w_value)


def query_kernel(place, h0, h1, w_query, mine, other, weight, sums, arrived):
    wait = fetch(w_query, weight, arrived, 4, row_piece)
    rows = h0.shape[0]
    for step in range(4):
        span = slice(step * 1024, (step + 1) * 1024)
        wait(step)
        product = dot(jnp.concatenate([h0[:, span], h1[:, span]]), weight[span])
        if step == 0:
            sums[...] = product
        else:
            sums[...] += product
    for out, side in ((mine, place[1]), (other, 1 - place[1])):
        out[...] = sums[:, pl.ds(pl.multiple_of(side * HD, HD), HD)].astype(BF16)


def queries(place, blocks, w_query):
    rows = blocks[0].shape[0]
    out = jax.ShapeDtypeStruct((2 * rows, HD), BF16)
    return pl.pallas_call(
        query_kernel,
        out_shape=(out, out),
        in_specs=smem(1) + vmem(2) + hbm(1),
        out_specs=tuple(vmem(2)),
        scratch_shapes=[
            pltpu.VMEM((4096, 512), BF16),
            pltpu.VMEM((2 * rows, 512), F32),
            pltpu.SemaphoreType.DMA((4,)),
        ],
        compiler_params=params(48),
        cost_estimate=pl.CostEstimate(
            flops=4 * rows * 4096 * 512, bytes_accessed=4 * MIB + rows * 16384, transcendentals=0
        ),
        name="queries",
    )(place, *blocks, w_query)


def attend_kernel(pieces, keys, place, span_ids, *refs):
    ids_own, ids_low, key_ids, near, far_low, near_low, far = refs[:7]
    arrays, outs, (query, ids, scores, peak, total, context) = refs[7:-10], refs[-10:-6], refs[-6:]
    block = ATTEND_ROWS
    scale = HD ** (-0.5) * math.log2(math.e)
    low, mp, z = place[1], place[2], place[7]

    for at, rows in enumerate((near, far_low, near_low, far)):
        query[at * 256 : (at + 1) * 256] = rows[...]
    for at, held in enumerate((ids_own, ids_low)):
        for flip in range(4):
            first = at * block + flip * 128
            row = held[pl.ds(jnp.bitwise_xor(mp, flip), 1)]
            ids[first : first + 128] = jnp.transpose(jnp.broadcast_to(row, (128, 128)))

    def one_block(at, _):
        rows = pl.ds(pl.multiple_of(at * block, block), block)
        lowest, highest_id = span_ids[at, 0], span_ids[at, 1]
        peak[...] = jnp.full_like(peak, -1e30)
        total[...] = jnp.zeros_like(total)
        context[...] = jnp.zeros_like(context)

        def rows_of(held, row):
            array, lead = held
            return arrays[array].at[lead + (pl.ds(row, keys),)]

        def for_each_part(step):
            for part, (flip_low, turn, piece_keys, piece_values, row) in enumerate(pieces):
                first = (jnp.bitwise_xor(low, flip_low) * 4 + (z + turn) % 4) * 512 + row
                meets = (span_ids[2, first] <= highest_id) & (span_ids[2, first + keys - 1] >= lowest)
                pl.when(meets)(
                    functools.partial(
                        step, part, rows_of(piece_keys, row), rows_of(piece_values, row), first
                    )
                )

        def score(part, part_keys, part_values, first):
            product = lax.dot_general(
                query[rows], part_keys[...], (((1,), (1,)), ((), ())), preferred_element_type=F32
            )
            own_ids = ids[rows]
            highest = peak[...]
            for lane in range(0, keys, 128):
                lane_ids = key_ids[:, pl.ds(pl.multiple_of(first + lane, 128), 128)]
                kept = jnp.where(own_ids == lane_ids, product[:, lane : lane + 128] * scale, -1e30)
                scores[part, :, lane : lane + 128] = kept
                highest = jnp.maximum(highest, kept)
            peak[...] = highest

        for_each_part(score)
        highest = jnp.max(peak[...], axis=-1, keepdims=True)

        def weigh(part, part_keys, part_values, first):
            weights = jnp.exp2(scores[part] - highest)
            sums = total[...]
            for lane in range(0, keys, 128):
                sums = sums + weights[:, lane : lane + 128]
            total[...] = sums
            context[...] += dot(weights.astype(BF16), part_values[...])

        for_each_part(weigh)
        whole = jnp.sum(total[...], axis=-1, keepdims=True)
        context[...] = context[...] / whole

        mine, core, beside, beside_core = outs

        @pl.when(at == 0)
        def _():
            mine[0:128] = context[0:128].astype(BF16)
            core[0:128] = context[128:256].astype(BF16)
            beside[128:256] = context[256:384].astype(BF16)
            beside_core[128:256] = context[384:512].astype(BF16)

        @pl.when(at == 1)
        def _():
            beside[0:128] = context[0:128].astype(BF16)
            beside_core[0:128] = context[128:256].astype(BF16)
            mine[128:256] = context[256:384].astype(BF16)
            core[128:256] = context[384:512].astype(BF16)

        return 0

    lax.fori_loop(0, 2, one_block, 0)


def attend(keys, pieces, arrays, place, span_ids, ids_own, ids_low, key_ids, blocks):
    out = jax.ShapeDtypeStruct((256, HD), BF16)
    return pl.pallas_call(
        functools.partial(attend_kernel, pieces, keys),
        out_shape=(out,) * 4,
        in_specs=smem(2) + vmem(7 + len(arrays)),
        out_specs=tuple(vmem(4)),
        scratch_shapes=[
            pltpu.VMEM((2 * ATTEND_ROWS, HD), BF16),
            pltpu.VMEM((2 * ATTEND_ROWS, 128), jnp.int32),
            pltpu.VMEM((len(pieces), ATTEND_ROWS, keys), F32),
            pltpu.VMEM((ATTEND_ROWS, 128), F32),
            pltpu.VMEM((ATTEND_ROWS, 128), F32),
            pltpu.VMEM((ATTEND_ROWS, HD), F32),
        ],
        compiler_params=params(28),
        cost_estimate=pl.CostEstimate(
            flops=4 * 1024 * 4096 * 256, bytes_accessed=6 * MIB, transcendentals=1024 * 1024
        ),
        name="attend",
    )(place, span_ids, ids_own, ids_low, key_ids, *blocks, *arrays)


def output_kernel(row, first, place, c0, c1, c2, c3, w_own, w_core, *refs):
    residual, (out, weight, arrived) = refs[:-3], refs[-3:]
    pieces = out.shape[1] // 512
    copies = [
        [
            pltpu.make_async_copy(
                source.at[:, pl.ds(first + at * 512, 512)], weight.at[core, at], arrived.at[core, at]
            )
            for core, source in enumerate((w_own, w_core))
        ]
        for at in range(pieces)
    ]
    for pair in copies:
        for copy in pair:
            copy.start()
    span = slice(row, row + 128)
    low = place[1]
    left = jnp.concatenate([c0[span], c2[span]], axis=1)
    left_core = jnp.concatenate([c1[span], c3[span]], axis=1)
    swapped = jnp.concatenate([c2[span], c0[span]], axis=1)
    swapped_core = jnp.concatenate([c3[span], c1[span]], axis=1)
    left = jnp.where(low == 0, left, swapped)
    left_core = jnp.where(low == 0, left_core, swapped_core)
    for at, pair in enumerate(copies):
        columns = slice(at * 512, (at + 1) * 512)
        for copy in pair:
            copy.wait()
        summed = dot(left, weight[0, at]) + dot(left_core, weight[1, at])
        for rows in residual:
            summed = summed + rows[:, columns].astype(F32)
        out[:, columns] = summed.astype(out.dtype)


def outputs(place, contexts, w_own, w_core, row, part, parts, residual=()):
    width = 4096 // parts
    return pl.pallas_call(
        functools.partial(output_kernel, row, part * width),
        out_shape=jax.ShapeDtypeStruct((128, width), F32 if residual else BF16),
        in_specs=smem(1) + vmem(4) + hbm(2) + vmem(len(residual)),
        out_specs=vmem(1)[0],
        scratch_shapes=[
            pltpu.VMEM((2, width // 512, 512, 512), BF16),
            pltpu.SemaphoreType.DMA((2, width // 512)),
        ],
        compiler_params=params(48),
        cost_estimate=pl.CostEstimate(
            flops=2 * 256 * width * 1024, bytes_accessed=width * 2048, transcendentals=0
        ),
        name="outputs",
    )(place, *contexts, w_own, w_core, *residual)


def per_device(
    decoder_rows,
    encoder_panel,
    norm_gain,
    w_query,
    w_key,
    w_value,
    w_output,
    decoder_segments,
    encoder_segments,
):
    section = lax.axis_index("section")
    seq = lax.axis_index("seq")
    mp = lax.axis_index("mp")
    low, z = seq // 4, seq % 4
    place = jnp.stack([section, low, mp] + [(section + offset) % 4 for offset in X_ORDER] + [z]).astype(
        jnp.int32
    )

    def panel_of(offset, first, count):
        return lax.dynamic_slice(
            encoder_panel, ((section + offset) % 4, first, 0), (1, count, 256)
        )

    own = panel_of(0, 0, 512)
    own_far = send(own, Y_FAR)
    crossed = [
        send(panel_of(offset, 0, 512), pairs) for offset, pairs in ((1, X_UP), (3, X_DOWN), (2, X_TWO))
    ]
    crossed[0], own_far = lax.optimization_barrier((crossed[0], own_far))
    panels = [own] + crossed
    fars = [own_far] + [send(block, Y_FAR) for block in crossed]

    local_rows = decoder_rows[0]
    hidden = normed_rows(local_rows, norm_gain[0])
    near_mine, near_other = queries(place, (hidden, send(hidden, CORE)), w_query[0])

    ids_own = decoder_segments[0].reshape(4, 128)
    ids_low = send(ids_own, Y_LOW)
    ends = jnp.stack([jnp.stack([ids[0, 0], ids[3, 127]]) for ids in (ids_own, ids_low)])
    span_ids = jnp.concatenate([jnp.pad(ends, ((0, 0), (0, 4094))), encoder_segments])
    w_core = send(w_output[0], CORE)

    near_mine, near_other, ids_low, span_ids, fars[1] = lax.optimization_barrier(
        (near_mine, near_other, ids_low, span_ids, fars[1])
    )
    blocks = []
    for near, far in zip(panels, fars):
        blocks += [near, send(near, CORE), far, send(far, CORE)]
    mine, other = key_values(place, blocks, w_key[0], w_value[0])

    below_0, above_0 = send(mine, Z_UP), send(mine, Z_DOWN)
    theirs, below_0, above_0 = lax.optimization_barrier((send(other, Y_LOW), below_0, above_0))
    below_1, above_1 = send(theirs, Z_UP), send(theirs, Z_DOWN)
    across_0 = (send(below_0[0], Z_UP), send(above_0[1], Z_DOWN))
    hidden, _ = lax.optimization_barrier((hidden, fars[3]))
    hidden_cut = send(hidden, Y_CUT)
    hidden_cut, below_1, above_1 = lax.optimization_barrier((hidden_cut, below_1, above_1))

    across_1 = (send(below_1[0], Z_UP), send(above_1[1], Z_DOWN))

    far_mine, far_other = queries(place, (hidden_cut, send(hidden_cut, CORE)), w_query[0])
    blocks = (near_mine, send(far_other, Y_LOW), send(near_other, Y_LOW), far_mine)

    arrays, pieces = [], []
    for flip_low, (held, below, above, across) in enumerate(
        ((mine, below_0, above_0, across_0), (theirs, below_1, above_1, across_1))
    ):
        base = len(arrays)
        arrays.extend([held, below, above, *across])
        for turn, keys, values in (
            (0, (base, (0,)), (base, (1,))),
            (3, (base + 1, (0,)), (base + 1, (1,))),
            (1, (base + 2, (0,)), (base + 2, (1,))),
            (2, (base + 3, ()), (base + 4, ())),
        ):
            for row in range(0, 512, KEYS):
                pieces.append((flip_low, turn, keys, values, row))

    contexts = attend(
        KEYS, pieces, arrays, place, span_ids, ids_own, ids_low, encoder_segments, blocks
    )

    contexts = (contexts[0],) + tuple(
        send(context, pairs) for context, pairs in zip(contexts[1:], (CORE, Y_LOW, Y_LOW_CORE))
    )
    w_own = w_output[0]
    arrived = [
        send(outputs(place, contexts, w_own, w_core, 128, part, 2), Y_CUT) for part in range(2)
    ]
    near = outputs(place, contexts, w_own, w_core, 0, 0, 1, (local_rows,))
    return (near + jnp.concatenate(arrived, axis=1).astype(F32)).astype(BF16)[None]


def solution(mesh):
    in_specs = (
        P("section", ("seq", "mp"), None),
        P(None, "seq", ("section", "mp")),
        P("section", None),
        P("section", None, "mp"),
        P("section", None, "mp"),
        P("section", None, "mp"),
        P("section", "mp", None),
        P("section", "seq"),
        P("section", None),
    )
    out_specs = P("section", ("seq", "mp"), None)
    return jax.shard_map(
        per_device, mesh=mesh, in_specs=in_specs, out_specs=out_specs, check_vma=False
    )
```

time: 361 us -> 153 us (0.42)
  waiting for transfers between devices: 281 us -> 61.7 us
  starting transfers between devices: 0.17 us -> 46.3 us
  matrix products: 40.2 us -> 0 us
  Pallas kernels: 0 us -> 34.5 us
  between operations: 13.2 us -> 0.2 us
  local copies, waits for them, and re-layouts: 12.1 us -> 2.36 us
  other arithmetic: 13.3 us -> 7.87 us
    all_gather x4 -> x0, waiting for transfers between devices: 230 us -> none  [the longest x1 124 us: per_device(): lax.all_gather(encoder_panel, ('section', 'mp'), axis=2, tiled=True)]
    ppermute x0 -> x36, waiting for transfers between devices: none -> 61.7 us  [send(): return lax.ppermute(array, AXES, pairs)]
    reduce_scatter x1 -> x0, waiting for transfers between devices: 50.2 us -> none  [per_device(): lax.psum_scatter(jnp.dot(context, output_weight, preferred_element_type=j...]
    ppermute x0 -> x36, starting transfers between devices: none -> 46.3 us  [send(): return lax.ppermute(array, AXES, pairs)]
    dot_general x6 -> x0, matrix products: 40.2 us -> none  [the longest x1 9.12 us: attend_block(): jnp.einsum('hqk,khd->qhd', weights.astype(jnp.bfloat16), value_heads, pre...]
    pallas_call x0 -> x7, Pallas kernels: none -> 34.5 us  [the longest x3 10.4 us: outputs(): pl.pallas_call(functools.partial(output_kernel, row, part * width), out_s...]
    reshape x1 -> x0, local copies, waits for them, and re-layouts: 6.36 us -> none  [attend_block(): value_heads = value_block.reshape(key_count, head_count, HD)]
    unnamed x10, local copies, waits for them, and re-layouts: 5.73 us -> 0.03 us
  transfers between devices with their start and end apart: 5 -> 36, of which waited for: 5 -> 18; matrix products, arithmetic and copies ran while one was open for 10% -> 3% of each run, Pallas kernels for 0% -> 21%
where the time goes in v2:
time: 153 us
  waiting for transfers between devices  61.7 us (40%)
  starting transfers between devices  46.3 us (30%)
  Pallas kernels  34.5 us (23%)
  other arithmetic  7.87 us (5%)
  local copies, waits for them, and re-layouts  2.36 us (2%)
    ppermute x36, waiting for transfers between devices, send(): return lax.ppermute(array, AXES, pairs)  61.7 us
    ppermute x36, starting transfers between devices, send(): return lax.ppermute(array, AXES, pairs)  46.3 us
    pallas_call x3, Pallas kernels, outputs(): pl.pallas_call(functools.partial(output_kernel, row, part * width), out_s...  10.4 us
    pallas_call x1, Pallas kernels, attend(): pl.pallas_call(functools.partial(attend_kernel, pieces, keys), out_shape=...  9.7 us
    pallas_call x1, Pallas kernels, key_values(): pl.pallas_call(key_value_kernel, out_shape=(out, out), in_specs=smem(1) +...  7.91 us
    pallas_call x2, Pallas kernels, queries(): pl.pallas_call(query_kernel, out_shape=(out, out), in_specs=smem(1) + vme...  6.48 us
  transfers between devices with their start and end apart: 36, of which 18 were waited for; matrix products, arithmetic and copies ran while one was open for 3% of the time, Pallas kernels for 21%

profile of v2, /device:TPU:1, one launch (start us, length us, event | category | flops | bytes accessed | tf_op | source)
XLA Modules:
  0.0 152.9 jit_solution(2007824697133247458)
XLA Ops:
  0.0 1.6 %fusion = f32[128]{0:T(128)S(1)} fusion(bf16[1,128,4096]{2,1,0:T(8,128)(2,1)} %param.9), kind=kLoop, calls=%fused_computation.2 | loop fusion | flops 1572736 | bytes 1049088 | tf_op jit(solution)/shard_map/reduce_sum | solution.py:66
  2.4 1.6 %fusion.2.h0 = bf16[128,4096]{1,0:T(8,128)(2,1)S(1)} fusion(f32[4096]{0:T(1024)S(1)} %bitcast.45, f32[128]{0:T(128)S(1)} %add_rsqrt_fusion, bf16[1,128,4096]{2,1,0:T(8,128)(2,1)} %param.9), kind=kLoop, calls=%fused_computation.4 | loop fusion | flops 2097152 | bytes 2114048 | tf_op jit(solution)/shard_map/convert_element_type | solution.py:67
  3.9 1.5 collective-permute-start
  6.4 1.3 collective-permute-start.2
  7.7 2.9 %collective-permute-start.3 = (bf16[1,512,256]{2,1,0:T(8,128)(2,1)S(1)}, bf16[1,512,256]{2,1,0:T(8,128)(2,1)S(1)}, u32[]{:S(2)}, u32[]{:S(2)}) collective-permute-start(bf16[1,512,256]{2,1,0:T(8,128)(2,1)S(1)} %get-tuple-element.54.refs_0_), channel_id=1, source_target_pairs={{0,2},{1,3},{2,0},{3,1},{4,6},{5,7},{6,4},{7,5},{8,10},{9,11},{10,... | collective-permute-start | bytes 786440 | tf_op jit(solution)/shard_map/ppermute | solution.py:49
  10.6 1.5 collective-permute-start.12
  12.0 1.5 %collective-permute-start.5 = (bf16[1,512,256]{2,1,0:T(8,128)(2,1)}, bf16[1,512,256]{2,1,0:T(8,128)(2,1)S(1)}, u32[]{:S(2)}, u32[]{:S(2)}) collective-permute-start(bf16[1,512,256]{2,1,0:T(8,128)(2,1)} %get-tuple-element.56), channel_id=1, source_target_pairs={{0,64},{1,65},{2,66},{3,67},{4,68},{5,69},{6,70},{7,71},{8,72},{9,... | collective-permute-start | bytes 786440 | tf_op jit(solution)/shard_map/ppermute | solution.py:49
  14.2 1.4 collective-permute-done.2.refs_4_
  15.7 1.4 collective-permute-start.1
  17.1 1.2 collective-permute-start.8
  18.4 3.0 %collective-permute-start.4 = (bf16[1,512,256]{2,1,0:T(8,128)(2,1)S(1)}, bf16[1,512,256]{2,1,0:T(8,128)(2,1)S(1)}, u32[]{:S(2)}, u32[]{:S(2)}) collective-permute-start(bf16[1,512,256]{2,1,0:T(8,128)(2,1)S(1)} %collective-permute-done.2.refs_4_), channel_id=1, source_target_pairs={{0,2},{1,3},{2,0},{3,1},{4,6},{5,7},{6,4},{7,5},{8,10},{9,11},{10,... | collective-permute-start | bytes 786440 | tf_op jit(solution)/shard_map/ppermute | solution.py:49
  22.1 2.7 %add_bitcast_fusion = (s32[1,2]{1,0:T(1,128)S(1)}, s32[1,2]{1,0:T(1,128)S(1)}) fusion(s32[1]{0:T(128)} %bitcast.13, s32[1]{0:T(128)} %bitcast.12, s32[1]{0:T(128)} %bitcast.16, s32[1]{0:T(128)} %bitcast.15), kind=kLoop, calls=%fused_computation.17 | loop fusion | flops 4 | bytes 32 | tf_op jit(solution)/shard_map/stack | solution.py:372
  24.8 3.1 %collective-permute-start.33 = (bf16[512,4096]{1,0:T(8,128)(2,1)}, bf16[512,4096]{1,0:T(8,128)(2,1)}, u32[]{:S(2)}, u32[]{:S(2)}) collective-permute-start(bf16[512,4096]{1,0:T(8,128)(2,1)} %bitcast.35), channel_id=1, source_target_pairs={{0,1},{1,0},{2,3},{3,2},{4,5},{5,4},{6,7},{7,6},{8,9},{9,8},{10,11... | collective-permute-start | bytes 12582920 | tf_op jit(solution)/shard_map/ppermute | solution.py:49
  28.1 3.6 %collective-permute-done.14.refs_10_ = bf16[1,512,256]{2,1,0:T(8,128)(2,1)S(1)} collective-permute-done((bf16[1,512,256]{2,1,0:T(8,128)(2,1)S(1)}, bf16[1,512,256]{2,1,0:T(8,128)(2,1)S(1)}, u32[]{:S(2)}, u32[]{:S(2)}) %collective-permute-start.14) | collective-permute-done | bytes 262176 | tf_op jit(solution)/shard_map/ppermute | solution.py:49
  31.6 2.6 %collective-permute-start.13 = (bf16[1,512,256]{2,1,0:T(8,128)(2,1)S(1)}, bf16[1,512,256]{2,1,0:T(8,128)(2,1)S(1)}, u32[]{:S(2)}, u32[]{:S(2)}) collective-permute-start(bf16[1,512,256]{2,1,0:T(8,128)(2,1)S(1)} %collective-permute-done.12.refs_8_), channel_id=1, source_target_pairs={{0,1},{1,0},{2,3},{3,2},{4,5},{5,4},{6,7},{7,6},{8,9},{9,8},{10,11... | collective-permute-start | bytes 786440 | tf_op jit(solution)/shard_map/ppermute | solution.py:49
  34.3 3.0 %collective-permute-start.6 = (bf16[1,512,256]{2,1,0:T(8,128)(2,1)S(1)}, bf16[1,512,256]{2,1,0:T(8,128)(2,1)S(1)}, u32[]{:S(2)}, u32[]{:S(2)}) collective-permute-start(bf16[1,512,256]{2,1,0:T(8,128)(2,1)S(1)} %collective-permute-done.5.refs_12_), channel_id=1, source_target_pairs={{0,2},{1,3},{2,0},{3,1},{4,6},{5,7},{6,4},{7,5},{8,10},{9,11},{10,... | collective-permute-start | bytes 786440 | tf_op jit(solution)/shard_map/ppermute | solution.py:49
  37.3 3.2 %queries.2 = (bf16[256,256]{1,0:T(8,128)(2,1)S(1)}, bf16[256,256]{1,0:T(8,128)(2,1)S(1)}) custom-call(s32[8]{0:T(128)S(1)} %stack.50.place, bf16[128,4096]{1,0:T(8,128)(2,1)S(1)} %fusion.2.h0, bf16[128,4096]{1,0:T(8,128)(2,1)S(1)} %collective-permute-done.h1, bf16[4096,512]{1,0:T(8,128)(2,1)} %bitcast.43), custom_call_target="tpu_custom_call" | custom-call | flops 1073741824 | bytes 6291456 | tf_op jit(solution)/shard_map/queries/pallas_call | solution.py:155
  41.5 1.8 %collective-permute-done.6.refs_14_ = bf16[1,512,256]{2,1,0:T(8,128)(2,1)S(1)} collective-permute-done((bf16[1,512,256]{2,1,0:T(8,128)(2,1)S(1)}, bf16[1,512,256]{2,1,0:T(8,128)(2,1)S(1)}, u32[]{:S(2)}, u32[]{:S(2)}) %collective-permute-start.6) | collective-permute-done | bytes 262176 | tf_op jit(solution)/shard_map/ppermute | solution.py:49
  43.3 1.3 collective-permute-start.17
  44.6 1.1 collective-permute-done.17.refs_15_
  46.1 7.9 %key_values.1 = (bf16[2,512,256]{2,1,0:T(8,128)(2,1)S(1)}, bf16[2,512,256]{2,1,0:T(8,128)(2,1)S(1)}) custom-call(s32[8]{0:T(128)S(1)} %stack.50.place, bf16[1,512,256]{2,1,0:T(8,128)(2,1)S(1)} %get-tuple-element.54.refs_0_, bf16[1,512,256]{2,1,0:T(8,128)(2,1)S(1)} %collective-permute-done.8.refs_1_, bf16[1,512,256]{2,1,0:T(8,128)(2,1)S(1)} %collective-permute-done.3.refs_2_, ...), custom_call_target="tpu_custom_call" | custom-call | flops 4294967296 | bytes 12582912 | tf_op jit(solution)/shard_map/key_values/pallas_call | solution.py:117
  54.0 1.4 collective-permute-start.18
  55.5 3.8 %collective-permute-start.20 = (bf16[2,512,256]{2,1,0:T(8,128)(2,1)S(1)}, bf16[2,512,256]{2,1,0:T(8,128)(2,1)S(1)}, u32[]{:S(2)}, u32[]{:S(2)}) collective-permute-start(bf16[2,512,256]{2,1,0:T(8,128)(2,1)S(1)} %get-tuple-element.39.refs_7_), channel_id=1, source_target_pairs={{0,12},{1,13},{2,14},{3,15},{4,0},{5,1},{6,2},{7,3},{8,4},{9,5},{1... | collective-permute-start | bytes 1572872 | tf_op jit(solution)/shard_map/ppermute | solution.py:49
  59.2 1.9 %collective-permute-start.7 = (bf16[128,4096]{1,0:T(8,128)(2,1)S(1)}, bf16[128,4096]{1,0:T(8,128)(2,1)S(1)}, u32[]{:S(2)}, u32[]{:S(2)}) collective-permute-start(bf16[128,4096]{1,0:T(8,128)(2,1)S(1)} %fusion.2.h0), channel_id=1, source_target_pairs={{0,18},{1,19},{2,16},{3,17},{4,22},{5,23},{6,20},{7,21},{8,26},{9,... | collective-permute-start | bytes 3145736 | tf_op jit(solution)/shard_map/ppermute | solution.py:49
  61.1 6.1 %collective-permute-done.18.refs_12_ = bf16[2,512,256]{2,1,0:T(8,128)(2,1)S(1)} collective-permute-done((bf16[2,512,256]{2,1,0:T(8,128)(2,1)S(1)}, bf16[2,512,256]{2,1,0:T(8,128)(2,1)S(1)}, u32[]{:S(2)}, u32[]{:S(2)}) %collective-permute-start.18) | collective-permute-done | bytes 524320 | tf_op jit(solution)/shard_map/ppermute | solution.py:49
  67.3 2.6 %collective-permute-done.20.refs_9_ = bf16[2,512,256]{2,1,0:T(8,128)(2,1)S(1)} collective-permute-done((bf16[2,512,256]{2,1,0:T(8,128)(2,1)S(1)}, bf16[2,512,256]{2,1,0:T(8,128)(2,1)S(1)}, u32[]{:S(2)}, u32[]{:S(2)}) %collective-permute-start.20) | collective-permute-done | bytes 524320 | tf_op jit(solution)/shard_map/ppermute | solution.py:49
  69.8 3.1 %collective-permute-done.19.refs_8_ = bf16[2,512,256]{2,1,0:T(8,128)(2,1)S(1)} collective-permute-done((bf16[2,512,256]{2,1,0:T(8,128)(2,1)S(1)}, bf16[2,512,256]{2,1,0:T(8,128)(2,1)S(1)}, u32[]{:S(2)}, u32[]{:S(2)}) %collective-permute-start.19) | collective-permute-done | bytes 524320 | tf_op jit(solution)/shard_map/ppermute | solution.py:49
  73.3 1.1 collective-permute-start.21
  74.4 9.8 %collective-permute-done.7.h0 = bf16[128,4096]{1,0:T(8,128)(2,1)S(1)} collective-permute-done((bf16[128,4096]{1,0:T(8,128)(2,1)S(1)}, bf16[128,4096]{1,0:T(8,128)(2,1)S(1)}, u32[]{:S(2)}, u32[]{:S(2)}) %collective-permute-start.7) | collective-permute-done | bytes 1048608 | tf_op jit(solution)/shard_map/ppermute | solution.py:49
  84.5 1.6 %collective-permute-done.21.refs_13_ = bf16[2,512,256]{2,1,0:T(8,128)(2,1)S(1)} collective-permute-done((bf16[2,512,256]{2,1,0:T(8,128)(2,1)S(1)}, bf16[2,512,256]{2,1,0:T(8,128)(2,1)S(1)}, u32[]{:S(2)}, u32[]{:S(2)}) %collective-permute-start.21) | collective-permute-done | bytes 524320 | tf_op jit(solution)/shard_map/ppermute | solution.py:49
  86.1 2.7 %collective-permute-start.23 = (bf16[128,4096]{1,0:T(8,128)(2,1)S(1)}, bf16[128,4096]{1,0:T(8,128)(2,1)S(1)}, u32[]{:S(2)}, u32[]{:S(2)}) collective-permute-start(bf16[128,4096]{1,0:T(8,128)(2,1)S(1)} %collective-permute-done.7.h0), channel_id=1, source_target_pairs={{0,1},{1,0},{2,3},{3,2},{4,5},{5,4},{6,7},{7,6},{8,9},{9,8},{10,11... | collective-permute-start | bytes 3145736 | tf_op jit(solution)/shard_map/ppermute | solution.py:49
  89.1 1.5 collective-permute-start.26
  90.7 3.3 %collective-permute-done.25.refs_5_ = bf16[256,256]{1,0:T(8,128)(2,1)S(1)} collective-permute-done((bf16[256,256]{1,0:T(8,128)(2,1)S(1)}, bf16[256,256]{1,0:T(8,128)(2,1)S(1)}, u32[]{:S(2)}, u32[]{:S(2)}) %collective-permute-start.25) | collective-permute-done | bytes 131104 | tf_op jit(solution)/shard_map/ppermute | solution.py:49
  93.9 1.5 collective-permute-start.28
  95.4 3.2 %queries.3 = (bf16[256,256]{1,0:T(8,128)(2,1)S(1)}, bf16[256,256]{1,0:T(8,128)(2,1)S(1)}) custom-call(s32[8]{0:T(128)S(1)} %stack.50.place, bf16[128,4096]{1,0:T(8,128)(2,1)S(1)} %collective-permute-done.7.h0, bf16[128,4096]{1,0:T(8,128)(2,1)S(1)} %collective-permute-done.23.h1, bf16[4096,512]{1,0:T(8,128)(2,1)} %bitcast.44), custom_call_target="tpu_custom_call" | custom-call | flops 1073741824 | bytes 6291456 | tf_op jit(solution)/shard_map/queries/pallas_call | solution.py:155
  98.9 3.4 %collective-permute-done.29.refs_16_ = bf16[512,256]{1,0:T(8,128)(2,1)S(1)} collective-permute-done((bf16[512,256]{1,0:T(8,128)(2,1)S(1)}, bf16[512,256]{1,0:T(8,128)(2,1)S(1)}, u32[]{:S(2)}, u32[]{:S(2)}) %collective-permute-start.29) | collective-permute-done | bytes 262176 | tf_op jit(solution)/shard_map/ppermute | solution.py:49
  102.3 1.2 collective-permute-done.28.refs_15_
  103.5 9.7 %attend.1 = (bf16[256,256]{1,0:T(8,128)(2,1)S(1)}, bf16[256,256]{1,0:T(8,128)(2,1)S(1)}, bf16[256,256]{1,0:T(8,128)(2,1)S(1)}, bf16[256,256]{1,0:T(8,128)(2,1)S(1)}) custom-call(s32[8]{0:T(128)S(1)} %stack.50.place, s32[3,4096]{1,0:T(4,128)S(1)} %pad_add_fusion.span_ids, s32[4,128]{1,0:T(4,128)S(1)} %bitcast.42, ...), custom_call_target="tpu_custom_call" | custom-call | flops 4294967296 | bytes 6291456 | tf_op jit(solution)/shard_map/attend/pallas_call | solution.py:260
  113.3 1.6 %collective-permute-start.30 = (bf16[256,256]{1,0:T(8,128)(2,1)S(1)}, bf16[256,256]{1,0:T(8,128)(2,1)S(1)}, u32[]{:S(2)}, u32[]{:S(2)}) collective-permute-start(bf16[256,256]{1,0:T(8,128)(2,1)S(1)} %get-tuple-element.50), channel_id=1, source_target_pairs={{0,1},{1,0},{2,3},{3,2},{4,5},{5,4},{6,7},{7,6},{8,9},{9,8},{10,11... | collective-permute-start | bytes 393224 | tf_op jit(solution)/shard_map/ppermute | solution.py:49
  116.6 3.3 %collective-permute-done.31.c2 = bf16[256,256]{1,0:T(8,128)(2,1)S(1)} collective-permute-done((bf16[256,256]{1,0:T(8,128)(2,1)S(1)}, bf16[256,256]{1,0:T(8,128)(2,1)S(1)}, u32[]{:S(2)}, u32[]{:S(2)}) %collective-permute-start.31) | collective-permute-done | bytes 131104 | tf_op jit(solution)/shard_map/ppermute | solution.py:49
  119.9 3.0 %collective-permute-done.32.c3 = bf16[256,256]{1,0:T(8,128)(2,1)S(1)} collective-permute-done((bf16[256,256]{1,0:T(8,128)(2,1)S(1)}, bf16[256,256]{1,0:T(8,128)(2,1)S(1)}, u32[]{:S(2)}, u32[]{:S(2)}) %collective-permute-start.32) | collective-permute-done | bytes 131104 | tf_op jit(solution)/shard_map/ppermute | solution.py:49
  122.9 3.0 %outputs.4 = bf16[128,2048]{1,0:T(8,128)(2,1)S(1)} custom-call(s32[8]{0:T(128)S(1)} %stack.50.place, bf16[256,256]{1,0:T(8,128)(2,1)S(1)} %get-tuple-element.49.c0, bf16[256,256]{1,0:T(8,128)(2,1)S(1)} %collective-permute-done.30.c1, bf16[256,256]{1,0:T(8,128)(2,1)S(1)} %collective-permute-done.31.c2, bf16[256,256]{1,0:T(8,128)(2,1)S(1)} %collective-permute-done.32.c3, ...), custom_call_target="tpu_custom_call" | custom-call | flops 1073741824 | bytes 4194304 | tf_op jit(solution)/shard_map/outputs/pallas_call | solution.py:316
  125.9 2.5 %collective-permute-start.34 = (bf16[128,2048]{1,0:T(8,128)(2,1)S(1)}, bf16[128,2048]{1,0:T(8,128)(2,1)S(1)}, u32[]{:S(2)}, u32[]{:S(2)}) collective-permute-start(bf16[128,2048]{1,0:T(8,128)(2,1)S(1)} %outputs.4), channel_id=1, source_target_pairs={{0,18},{1,19},{2,16},{3,17},{4,22},{5,23},{6,20},{7,21},{8,26},{9,... | collective-permute-start | bytes 1572872 | tf_op jit(solution)/shard_map/ppermute | solution.py:49
  128.4 3.0 %outputs.5 = bf16[128,2048]{1,0:T(8,128)(2,1)S(1)} custom-call(s32[8]{0:T(128)S(1)} %stack.50.place, bf16[256,256]{1,0:T(8,128)(2,1)S(1)} %get-tuple-element.49.c0, bf16[256,256]{1,0:T(8,128)(2,1)S(1)} %collective-permute-done.30.c1, bf16[256,256]{1,0:T(8,128)(2,1)S(1)} %collective-permute-done.31.c2, bf16[256,256]{1,0:T(8,128)(2,1)S(1)} %collective-permute-done.32.c3, ...), custom_call_target="tpu_custom_call" | custom-call | flops 1073741824 | bytes 4194304 | tf_op jit(solution)/shard_map/outputs/pallas_call | solution.py:316
  131.7 4.4 %outputs.3 = f32[128,4096]{1,0:T(8,128)S(1)} custom-call(s32[8]{0:T(128)S(1)} %stack.50.place, bf16[256,256]{1,0:T(8,128)(2,1)S(1)} %get-tuple-element.49.c0, bf16[256,256]{1,0:T(8,128)(2,1)S(1)} %collective-permute-done.30.c1, bf16[256,256]{1,0:T(8,128)(2,1)S(1)} %collective-permute-done.31.c2, bf16[256,256]{1,0:T(8,128)(2,1)S(1)} %collective-permute-done.32.c3, ...), custom_call_target="tpu_custom_call" | custom-call | flops 2147483648 | bytes 8388608 | tf_op jit(solution)/shard_map/outputs/pallas_call | solution.py:316
  136.1 4.4 %collective-permute-done.34 = bf16[128,2048]{1,0:T(8,128)(2,1)S(1)} collective-permute-done((bf16[128,2048]{1,0:T(8,128)(2,1)S(1)}, bf16[128,2048]{1,0:T(8,128)(2,1)S(1)}, u32[]{:S(2)}, u32[]{:S(2)}) %collective-permute-start.34) | collective-permute-done | bytes 524320 | tf_op jit(solution)/shard_map/ppermute | solution.py:49
  140.5 11.2 %collective-permute-done.35 = bf16[128,2048]{1,0:T(8,128)(2,1)S(1)} collective-permute-done((bf16[128,2048]{1,0:T(8,128)(2,1)S(1)}, bf16[128,2048]{1,0:T(8,128)(2,1)S(1)}, u32[]{:S(2)}, u32[]{:S(2)}) %collective-permute-start.35) | collective-permute-done | bytes 524320 | tf_op jit(solution)/shard_map/ppermute | solution.py:49
  151.7 1.2 fusion.3
  (57 shorter events, 7.8 us)
Async XLA Ops:
  0.0 5.5 %copy-start.4 = (bf16[4,512,256]{2,1,0:T(8,128)(2,1)S(1)}, bf16[4,512,256]{2,1,0:T(8,128)(2,1)}, u32[]{:S(2)}) copy-start(bf16[4,512,256]{2,1,0:T(8,128)(2,1)} %param.10) | copy-start | bytes 3145732
  2.4 11.2 %copy-start.3 = (s32[1,512]{1,0:T(1,128)S(1)}, s32[1,512]{1,0:T(1,128)}, u32[]{:S(2)}) copy-start(s32[1,512]{1,0:T(1,128)} %param.16) | copy-start | bytes 6148
  2.4 34.9 %copy-start.2 = (s32[1,4096]{1,0:T(1,128)S(1)}, s32[1,4096]{1,0:T(1,128)}, u32[]{:S(2)}) copy-start(s32[1,4096]{1,0:T(1,128)} %refs_2_.1) | copy-start | bytes 49156
  3.9 30.3 %collective-permute-start = (bf16[128,4096]{1,0:T(8,128)(2,1)S(1)}, bf16[128,4096]{1,0:T(8,128)(2,1)S(1)}, u32[]{:S(2)}, u32[]{:S(2)}) collective-permute-start(bf16[128,4096]{1,0:T(8,128)(2,1)S(1)} %fusion.2.h0), channel_id=1, source_target_pairs={{0,1},{1,0},{2,3},{3,2},{4,5},{5,4},{6,7},{7,6},{8,9},{9,8},{10,11... | collective-permute-start | bytes 3145736 | tf_op jit(solution)/shard_map/ppermute | solution.py:49
  6.4 9.3 %collective-permute-start.2 = (bf16[1,512,256]{2,1,0:T(8,128)(2,1)}, bf16[1,512,256]{2,1,0:T(8,128)(2,1)S(1)}, u32[]{:S(2)}, u32[]{:S(2)}) collective-permute-start(bf16[1,512,256]{2,1,0:T(8,128)(2,1)} %get-tuple-element.55), channel_id=1, source_target_pairs={{0,32},{1,33},{2,34},{3,35},{4,36},{5,37},{6,38},{7,39},{8,40},{9,... | collective-permute-start | bytes 786440 | tf_op jit(solution)/shard_map/ppermute | solution.py:49
  7.7 9.4 %collective-permute-start.3 = (bf16[1,512,256]{2,1,0:T(8,128)(2,1)S(1)}, bf16[1,512,256]{2,1,0:T(8,128)(2,1)S(1)}, u32[]{:S(2)}, u32[]{:S(2)}) collective-permute-start(bf16[1,512,256]{2,1,0:T(8,128)(2,1)S(1)} %get-tuple-element.54.refs_0_), channel_id=1, source_target_pairs={{0,2},{1,3},{2,0},{3,1},{4,6},{5,7},{6,4},{7,5},{8,10},{9,11},{10,... | collective-permute-start | bytes 786440 | tf_op jit(solution)/shard_map/ppermute | solution.py:49
  10.6 10.8 %collective-permute-start.12 = (bf16[1,512,256]{2,1,0:T(8,128)(2,1)}, bf16[1,512,256]{2,1,0:T(8,128)(2,1)S(1)}, u32[]{:S(2)}, u32[]{:S(2)}) collective-permute-start(bf16[1,512,256]{2,1,0:T(8,128)(2,1)} %get-tuple-element.53), channel_id=1, source_target_pairs={{0,96},{1,97},{2,98},{3,99},{4,100},{5,101},{6,102},{7,103},{8,104... | collective-permute-start | bytes 786440 | tf_op jit(solution)/shard_map/ppermute | solution.py:49
  12.0 12.8 %collective-permute-start.5 = (bf16[1,512,256]{2,1,0:T(8,128)(2,1)}, bf16[1,512,256]{2,1,0:T(8,128)(2,1)S(1)}, u32[]{:S(2)}, u32[]{:S(2)}) collective-permute-start(bf16[1,512,256]{2,1,0:T(8,128)(2,1)} %get-tuple-element.56), channel_id=1, source_target_pairs={{0,64},{1,65},{2,66},{3,67},{4,68},{5,69},{6,70},{7,71},{8,72},{9,... | collective-permute-start | bytes 786440 | tf_op jit(solution)/shard_map/ppermute | solution.py:49
  15.7 2.7 %collective-permute-start.1 = (s32[4,128]{1,0:T(4,128)S(1)}, s32[4,128]{1,0:T(4,128)S(1)}, u32[]{:S(2)}, u32[]{:S(2)}) collective-permute-start(s32[4,128]{1,0:T(4,128)S(1)} %bitcast.41), channel_id=1, source_target_pairs={{0,16},{1,17},{2,18},{3,19},{4,20},{5,21},{6,22},{7,23},{8,24},{9,... | collective-permute-start | bytes 6152 | tf_op jit(solution)/shard_map/ppermute | solution.py:49
  17.1 10.8 %collective-permute-start.8 = (bf16[1,512,256]{2,1,0:T(8,128)(2,1)S(1)}, bf16[1,512,256]{2,1,0:T(8,128)(2,1)S(1)}, u32[]{:S(2)}, u32[]{:S(2)}) collective-permute-start(bf16[1,512,256]{2,1,0:T(8,128)(2,1)S(1)} %get-tuple-element.54.refs_0_), channel_id=1, source_target_pairs={{0,1},{1,0},{2,3},{3,2},{4,5},{5,4},{6,7},{7,6},{8,9},{9,8},{10,11... | collective-permute-start | bytes 786440 | tf_op jit(solution)/shard_map/ppermute | solution.py:49
  18.4 15.9 %collective-permute-start.4 = (bf16[1,512,256]{2,1,0:T(8,128)(2,1)S(1)}, bf16[1,512,256]{2,1,0:T(8,128)(2,1)S(1)}, u32[]{:S(2)}, u32[]{:S(2)}) collective-permute-start(bf16[1,512,256]{2,1,0:T(8,128)(2,1)S(1)} %collective-permute-done.2.refs_4_), channel_id=1, source_target_pairs={{0,2},{1,3},{2,0},{3,1},{4,6},{5,7},{6,4},{7,5},{8,10},{9,11},{10,... | collective-permute-start | bytes 786440 | tf_op jit(solution)/shard_map/ppermute | solution.py:49
  21.4 10.3 %collective-permute-start.14 = (bf16[1,512,256]{2,1,0:T(8,128)(2,1)S(1)}, bf16[1,512,256]{2,1,0:T(8,128)(2,1)S(1)}, u32[]{:S(2)}, u32[]{:S(2)}) collective-permute-start(bf16[1,512,256]{2,1,0:T(8,128)(2,1)S(1)} %collective-permute-done.12.refs_8_), channel_id=1, source_target_pairs={{0,2},{1,3},{2,0},{3,1},{4,6},{5,7},{6,4},{7,5},{8,10},{9,11},{10,... | collective-permute-start | bytes 786440 | tf_op jit(solution)/shard_map/ppermute | solution.py:49
  24.8 98.1 %collective-permute-start.33 = (bf16[512,4096]{1,0:T(8,128)(2,1)}, bf16[512,4096]{1,0:T(8,128)(2,1)}, u32[]{:S(2)}, u32[]{:S(2)}) collective-permute-start(bf16[512,4096]{1,0:T(8,128)(2,1)} %bitcast.35), channel_id=1, source_target_pairs={{0,1},{1,0},{2,3},{3,2},{4,5},{5,4},{6,7},{7,6},{8,9},{9,8},{10,11... | collective-permute-start | bytes 12582920 | tf_op jit(solution)/shard_map/ppermute | solution.py:49
  28.0 16.6 %collective-permute-start.9 = (bf16[1,512,256]{2,1,0:T(8,128)(2,1)S(1)}, bf16[1,512,256]{2,1,0:T(8,128)(2,1)S(1)}, u32[]{:S(2)}, u32[]{:S(2)}) collective-permute-start(bf16[1,512,256]{2,1,0:T(8,128)(2,1)S(1)} %collective-permute-done.3.refs_2_), channel_id=1, source_target_pairs={{0,1},{1,0},{2,3},{3,2},{4,5},{5,4},{6,7},{7,6},{8,9},{9,8},{10,11... | collective-permute-start | bytes 786440 | tf_op jit(solution)/shard_map/ppermute | solution.py:49
  31.6 9.0 %collective-permute-start.13 = (bf16[1,512,256]{2,1,0:T(8,128)(2,1)S(1)}, bf16[1,512,256]{2,1,0:T(8,128)(2,1)S(1)}, u32[]{:S(2)}, u32[]{:S(2)}) collective-permute-start(bf16[1,512,256]{2,1,0:T(8,128)(2,1)S(1)} %collective-permute-done.12.refs_8_), channel_id=1, source_target_pairs={{0,1},{1,0},{2,3},{3,2},{4,5},{5,4},{6,7},{7,6},{8,9},{9,8},{10,11... | collective-permute-start | bytes 786440 | tf_op jit(solution)/shard_map/ppermute | solution.py:49
  34.3 7.1 %collective-permute-start.16 = (bf16[1,512,256]{2,1,0:T(8,128)(2,1)S(1)}, bf16[1,512,256]{2,1,0:T(8,128)(2,1)S(1)}, u32[]{:S(2)}, u32[]{:S(2)}) collective-permute-start(bf16[1,512,256]{2,1,0:T(8,128)(2,1)S(1)} %collective-permute-done.5.refs_12_), channel_id=1, source_target_pairs={{0,1},{1,0},{2,3},{3,2},{4,5},{5,4},{6,7},{7,6},{8,9},{9,8},{10,11... | collective-permute-start | bytes 786440 | tf_op jit(solution)/shard_map/ppermute | solution.py:49
  34.3 9.0 %collective-permute-start.6 = (bf16[1,512,256]{2,1,0:T(8,128)(2,1)S(1)}, bf16[1,512,256]{2,1,0:T(8,128)(2,1)S(1)}, u32[]{:S(2)}, u32[]{:S(2)}) collective-permute-start(bf16[1,512,256]{2,1,0:T(8,128)(2,1)S(1)} %collective-permute-done.5.refs_12_), channel_id=1, source_target_pairs={{0,2},{1,3},{2,0},{3,1},{4,6},{5,7},{6,4},{7,5},{8,10},{9,11},{10,... | collective-permute-start | bytes 786440 | tf_op jit(solution)/shard_map/ppermute | solution.py:49
  40.6 4.0 %collective-permute-start.10 = (bf16[1,512,256]{2,1,0:T(8,128)(2,1)S(1)}, bf16[1,512,256]{2,1,0:T(8,128)(2,1)S(1)}, u32[]{:S(2)}, u32[]{:S(2)}) collective-permute-start(bf16[1,512,256]{2,1,0:T(8,128)(2,1)S(1)} %collective-permute-done.2.refs_4_), channel_id=1, source_target_pairs={{0,1},{1,0},{2,3},{3,2},{4,5},{5,4},{6,7},{7,6},{8,9},{9,8},{10,11... | collective-permute-start | bytes 786440 | tf_op jit(solution)/shard_map/ppermute | solution.py:49
  41.4 3.2 %collective-permute-start.15 = (bf16[1,512,256]{2,1,0:T(8,128)(2,1)S(1)}, bf16[1,512,256]{2,1,0:T(8,128)(2,1)S(1)}, u32[]{:S(2)}, u32[]{:S(2)}) collective-permute-start(bf16[1,512,256]{2,1,0:T(8,128)(2,1)S(1)} %collective-permute-done.14.refs_10_), channel_id=1, source_target_pairs={{0,1},{1,0},{2,3},{3,2},{4,5},{5,4},{6,7},{7,6},{8,9},{9,8},{10,11... | collective-permute-start | bytes 786440 | tf_op jit(solution)/shard_map/ppermute | solution.py:49
  43.3 2.4 %collective-permute-start.17 = (bf16[1,512,256]{2,1,0:T(8,128)(2,1)S(1)}, bf16[1,512,256]{2,1,0:T(8,128)(2,1)S(1)}, u32[]{:S(2)}, u32[]{:S(2)}) collective-permute-start(bf16[1,512,256]{2,1,0:T(8,128)(2,1)S(1)} %collective-permute-done.6.refs_14_), channel_id=1, source_target_pairs={{0,1},{1,0},{2,3},{3,2},{4,5},{5,4},{6,7},{7,6},{8,9},{9,8},{10,11... | collective-permute-start | bytes 786440 | tf_op jit(solution)/shard_map/ppermute | solution.py:49
  44.6 1.5 %collective-permute-start.11 = (bf16[1,512,256]{2,1,0:T(8,128)(2,1)S(1)}, bf16[1,512,256]{2,1,0:T(8,128)(2,1)S(1)}, u32[]{:S(2)}, u32[]{:S(2)}) collective-permute-start(bf16[1,512,256]{2,1,0:T(8,128)(2,1)S(1)} %collective-permute-done.4.refs_6_), channel_id=1, source_target_pairs={{0,1},{1,0},{2,3},{3,2},{4,5},{5,4},{6,7},{7,6},{8,9},{9,8},{10,11... | collective-permute-start | bytes 786440 | tf_op jit(solution)/shard_map/ppermute | solution.py:49
  54.0 13.2 %collective-permute-start.18 = (bf16[2,512,256]{2,1,0:T(8,128)(2,1)S(1)}, bf16[2,512,256]{2,1,0:T(8,128)(2,1)S(1)}, u32[]{:S(2)}, u32[]{:S(2)}) collective-permute-start(bf16[2,512,256]{2,1,0:T(8,128)(2,1)S(1)} %get-tuple-element.38), channel_id=1, source_target_pairs={{0,16},{1,17},{2,18},{3,19},{4,20},{5,21},{6,22},{7,23},{8,24},{9,... | collective-permute-start | bytes 1572872 | tf_op jit(solution)/shard_map/ppermute | solution.py:49
  55.5 14.4 %collective-permute-start.20 = (bf16[2,512,256]{2,1,0:T(8,128)(2,1)S(1)}, bf16[2,512,256]{2,1,0:T(8,128)(2,1)S(1)}, u32[]{:S(2)}, u32[]{:S(2)}) collective-permute-start(bf16[2,512,256]{2,1,0:T(8,128)(2,1)S(1)} %get-tuple-element.39.refs_7_), channel_id=1, source_target_pairs={{0,12},{1,13},{2,14},{3,15},{4,0},{5,1},{6,2},{7,3},{8,4},{9,5},{1... | collective-permute-start | bytes 1572872 | tf_op jit(solution)/shard_map/ppermute | solution.py:49
  59.2 13.7 %collective-permute-start.19 = (bf16[2,512,256]{2,1,0:T(8,128)(2,1)S(1)}, bf16[2,512,256]{2,1,0:T(8,128)(2,1)S(1)}, u32[]{:S(2)}, u32[]{:S(2)}) collective-permute-start(bf16[2,512,256]{2,1,0:T(8,128)(2,1)S(1)} %get-tuple-element.39.refs_7_), channel_id=1, source_target_pairs={{0,4},{1,5},{2,6},{3,7},{4,8},{5,9},{6,10},{7,11},{8,12},{9,13},{1... | collective-permute-start | bytes 1572872 | tf_op jit(solution)/shard_map/ppermute | solution.py:49
  59.2 24.9 %collective-permute-start.7 = (bf16[128,4096]{1,0:T(8,128)(2,1)S(1)}, bf16[128,4096]{1,0:T(8,128)(2,1)S(1)}, u32[]{:S(2)}, u32[]{:S(2)}) collective-permute-start(bf16[128,4096]{1,0:T(8,128)(2,1)S(1)} %fusion.2.h0), channel_id=1, source_target_pairs={{0,18},{1,19},{2,16},{3,17},{4,22},{5,23},{6,20},{7,21},{8,26},{9,... | collective-permute-start | bytes 3145736 | tf_op jit(solution)/shard_map/ppermute | solution.py:49
  72.9 11.6 %collective-permute-start.22 = (bf16[2,512,256]{2,1,0:T(8,128)(2,1)S(1)}, bf16[2,512,256]{2,1,0:T(8,128)(2,1)S(1)}, u32[]{:S(2)}, u32[]{:S(2)}) collective-permute-start(bf16[2,512,256]{2,1,0:T(8,128)(2,1)S(1)} %collective-permute-done.18.refs_12_), channel_id=1, source_target_pairs={{0,12},{1,13},{2,14},{3,15},{4,0},{5,1},{6,2},{7,3},{8,4},{9,5},{1... | collective-permute-start | bytes 1572872 | tf_op jit(solution)/shard_map/ppermute | solution.py:49
  73.3 12.8 %collective-permute-start.21 = (bf16[2,512,256]{2,1,0:T(8,128)(2,1)S(1)}, bf16[2,512,256]{2,1,0:T(8,128)(2,1)S(1)}, u32[]{:S(2)}, u32[]{:S(2)}) collective-permute-start(bf16[2,512,256]{2,1,0:T(8,128)(2,1)S(1)} %collective-permute-done.18.refs_12_), channel_id=1, source_target_pairs={{0,4},{1,5},{2,6},{3,7},{4,8},{5,9},{6,10},{7,11},{8,12},{9,13},{1... | collective-permute-start | bytes 1572872 | tf_op jit(solution)/shard_map/ppermute | solution.py:49
  86.1 7.9 %collective-permute-start.23 = (bf16[128,4096]{1,0:T(8,128)(2,1)S(1)}, bf16[128,4096]{1,0:T(8,128)(2,1)S(1)}, u32[]{:S(2)}, u32[]{:S(2)}) collective-permute-start(bf16[128,4096]{1,0:T(8,128)(2,1)S(1)} %collective-permute-done.7.h0), channel_id=1, source_target_pairs={{0,1},{1,0},{2,3},{3,2},{4,5},{5,4},{6,7},{7,6},{8,9},{9,8},{10,11... | collective-permute-start | bytes 3145736 | tf_op jit(solution)/shard_map/ppermute | solution.py:49
  88.8 5.1 %collective-permute-start.25 = (bf16[256,256]{1,0:T(8,128)(2,1)S(1)}, bf16[256,256]{1,0:T(8,128)(2,1)S(1)}, u32[]{:S(2)}, u32[]{:S(2)}) collective-permute-start(bf16[256,256]{1,0:T(8,128)(2,1)S(1)} %get-tuple-element.43), channel_id=1, source_target_pairs={{0,16},{1,17},{2,18},{3,19},{4,20},{5,21},{6,22},{7,23},{8,24},{9,... | collective-permute-start | bytes 393224 | tf_op jit(solution)/shard_map/ppermute | solution.py:49
  89.0 9.7 %collective-permute-start.27 = (bf16[512,256]{1,0:T(8,128)(2,1)S(1)}, bf16[512,256]{1,0:T(8,128)(2,1)S(1)}, u32[]{:S(2)}, u32[]{:S(2)}) collective-permute-start(bf16[512,256]{1,0:T(8,128)(2,1)S(1)} %slice_bitcast_fusion.2), channel_id=1, source_target_pairs={{0,12},{1,13},{2,14},{3,15},{4,0},{5,1},{6,2},{7,3},{8,4},{9,5},{1... | collective-permute-start | bytes 786440 | tf_op jit(solution)/shard_map/ppermute | solution.py:49
  89.1 9.8 %collective-permute-start.26 = (bf16[512,256]{1,0:T(8,128)(2,1)S(1)}, bf16[512,256]{1,0:T(8,128)(2,1)S(1)}, u32[]{:S(2)}, u32[]{:S(2)}) collective-permute-start(bf16[512,256]{1,0:T(8,128)(2,1)S(1)} %slice_bitcast_fusion.3), channel_id=1, source_target_pairs={{0,4},{1,5},{2,6},{3,7},{4,8},{5,9},{6,10},{7,11},{8,12},{9,13},{1... | collective-permute-start | bytes 786440 | tf_op jit(solution)/shard_map/ppermute | solution.py:49
  93.9 8.4 %collective-permute-start.29 = (bf16[512,256]{1,0:T(8,128)(2,1)S(1)}, bf16[512,256]{1,0:T(8,128)(2,1)S(1)}, u32[]{:S(2)}, u32[]{:S(2)}) collective-permute-start(bf16[512,256]{1,0:T(8,128)(2,1)S(1)} %slice_bitcast_fusion), channel_id=1, source_target_pairs={{0,12},{1,13},{2,14},{3,15},{4,0},{5,1},{6,2},{7,3},{8,4},{9,5},{1... | collective-permute-start | bytes 786440 | tf_op jit(solution)/shard_map/ppermute | solution.py:49
  93.9 9.6 %collective-permute-start.28 = (bf16[512,256]{1,0:T(8,128)(2,1)S(1)}, bf16[512,256]{1,0:T(8,128)(2,1)S(1)}, u32[]{:S(2)}, u32[]{:S(2)}) collective-permute-start(bf16[512,256]{1,0:T(8,128)(2,1)S(1)} %slice_bitcast_fusion.1), channel_id=1, source_target_pairs={{0,4},{1,5},{2,6},{3,7},{4,8},{5,9},{6,10},{7,11},{8,12},{9,13},{1... | collective-permute-start | bytes 786440 | tf_op jit(solution)/shard_map/ppermute | solution.py:49
  98.7 4.9 %collective-permute-start.24 = (bf16[256,256]{1,0:T(8,128)(2,1)S(1)}, bf16[256,256]{1,0:T(8,128)(2,1)S(1)}, u32[]{:S(2)}, u32[]{:S(2)}) collective-permute-start(bf16[256,256]{1,0:T(8,128)(2,1)S(1)} %get-tuple-element.42), channel_id=1, source_target_pairs={{0,16},{1,17},{2,18},{3,19},{4,20},{5,21},{6,22},{7,23},{8,24},{9,... | collective-permute-start | bytes 393224 | tf_op jit(solution)/shard_map/ppermute | solution.py:49
  103.5 19.4 %copy-start = (bf16[1,512,4096]{2,1,0:T(8,128)(2,1)S(1)}, bf16[1,512,4096]{2,1,0:T(8,128)(2,1)}, u32[]{:S(2)}) copy-start(bf16[1,512,4096]{2,1,0:T(8,128)(2,1)} %param.15) | copy-start | bytes 12582916
  113.3 3.3 %collective-permute-start.30 = (bf16[256,256]{1,0:T(8,128)(2,1)S(1)}, bf16[256,256]{1,0:T(8,128)(2,1)S(1)}, u32[]{:S(2)}, u32[]{:S(2)}) collective-permute-start(bf16[256,256]{1,0:T(8,128)(2,1)S(1)} %get-tuple-element.50), channel_id=1, source_target_pairs={{0,1},{1,0},{2,3},{3,2},{4,5},{5,4},{6,7},{7,6},{8,9},{9,8},{10,11... | collective-permute-start | bytes 393224 | tf_op jit(solution)/shard_map/ppermute | solution.py:49
  114.9 5.1 %collective-permute-start.31 = (bf16[256,256]{1,0:T(8,128)(2,1)S(1)}, bf16[256,256]{1,0:T(8,128)(2,1)S(1)}, u32[]{:S(2)}, u32[]{:S(2)}) collective-permute-start(bf16[256,256]{1,0:T(8,128)(2,1)S(1)} %get-tuple-element.51), channel_id=1, source_target_pairs={{0,16},{1,17},{2,18},{3,19},{4,20},{5,21},{6,22},{7,23},{8,24},{9,... | collective-permute-start | bytes 393224 | tf_op jit(solution)/shard_map/ppermute | solution.py:49
  115.8 7.1 %collective-permute-start.32 = (bf16[256,256]{1,0:T(8,128)(2,1)S(1)}, bf16[256,256]{1,0:T(8,128)(2,1)S(1)}, u32[]{:S(2)}, u32[]{:S(2)}) collective-permute-start(bf16[256,256]{1,0:T(8,128)(2,1)S(1)} %get-tuple-element.52), channel_id=1, source_target_pairs={{0,17},{1,16},{2,19},{3,18},{4,21},{5,20},{6,23},{7,22},{8,25},{9,... | collective-permute-start | bytes 393224 | tf_op jit(solution)/shard_map/ppermute | solution.py:49
  125.9 5.8 %copy-start.1 = (bf16[1,128,4096]{2,1,0:T(8,128)(2,1)S(1)}, bf16[1,128,4096]{2,1,0:T(8,128)(2,1)}, u32[]{:S(2)}) copy-start(bf16[1,128,4096]{2,1,0:T(8,128)(2,1)} %param.9) | copy-start | bytes 3145732
  125.9 14.6 %collective-permute-start.34 = (bf16[128,2048]{1,0:T(8,128)(2,1)S(1)}, bf16[128,2048]{1,0:T(8,128)(2,1)S(1)}, u32[]{:S(2)}, u32[]{:S(2)}) collective-permute-start(bf16[128,2048]{1,0:T(8,128)(2,1)S(1)} %outputs.4), channel_id=1, source_target_pairs={{0,18},{1,19},{2,16},{3,17},{4,22},{5,23},{6,20},{7,21},{8,26},{9,... | collective-permute-start | bytes 1572872 | tf_op jit(solution)/shard_map/ppermute | solution.py:49
  131.4 20.4 %collective-permute-start.35 = (bf16[128,2048]{1,0:T(8,128)(2,1)S(1)}, bf16[128,2048]{1,0:T(8,128)(2,1)S(1)}, u32[]{:S(2)}, u32[]{:S(2)}) collective-permute-start(bf16[128,2048]{1,0:T(8,128)(2,1)S(1)} %outputs.5), channel_id=1, source_target_pairs={{0,18},{1,19},{2,16},{3,17},{4,22},{5,23},{6,20},{7,21},{8,26},{9,... | collective-permute-start | bytes 1572872 | tf_op jit(solution)/shard_map/ppermute | solution.py:49

commit v3 on v2

--- a/solution.py
+++ b/solution.py
@@ -43,6 +43,18 @@
 X_DOWN = route(lambda x, l, z, h, c: (x - 1, l, z, h, c))
 X_TWO = route(lambda x, l, z, h, c: (x + 2, l, z, h, c))
 X_ORDER = (0, -1, 1, 2)
+W_PIECES = (
+    (0, 0, 0, 64, 0),
+    (0, 0, 3, 64, 1),
+    (0, 0, 1, 64, 2),
+    (0, 0, 2, 32, 3),
+    (0, 32, 2, 32, 4),
+    (1, 0, 0, 64, 5),
+    (1, 0, 3, 64, 6),
+    (1, 0, 1, 64, 7),
+    (1, 0, 2, 64, 8),
+)
+X_GROUPS = ((0,), (1, 2), (3,))
 
 
 def send(array, pairs):
@@ -86,13 +98,14 @@
 
 
 def key_value_kernel(place, *refs):
-    blocks, (w_key, w_value, mine, other, panel, keys, values, sums, arrived) = refs[:16], refs[16:]
+    blocks, (w_key, w_value, mine, other, panel, keys, values, sums, arrived) = refs[:12], refs[12:]
     wait_key = fetch(w_key, keys, arrived.at[0], 4, row_piece)
     wait_value = fetch(w_value, values, arrived.at[1], 4, row_piece)
     for at, block in enumerate(blocks):
-        step, flip = divmod(at, 4)
-        column = place[3 + step] * 1024 + jnp.bitwise_xor(place[2], flip) * 256
-        panel[:, pl.ds(pl.multiple_of(column, 256), 256)] = block[0]
+        group, flip = divmod(at, 4)
+        for lead, step in enumerate(X_GROUPS[group]):
+            column = place[3 + step] * 1024 + jnp.bitwise_xor(place[2], flip) * 256
+            panel[:, pl.ds(pl.multiple_of(column, 256), 256)] = block[lead]
     for step in range(4):
         block = panel[:, step * 1024 : (step + 1) * 1024]
         for at, (wait, held) in enumerate(((wait_key, keys), (wait_value, values))):
@@ -117,7 +130,7 @@
     return pl.pallas_call(
         key_value_kernel,
         out_shape=(out, out),
-        in_specs=smem(1) + vmem(16) + hbm(2),
+        in_specs=smem(1) + vmem(12) + hbm(2),
         out_specs=tuple(vmem(2)),
         scratch_shapes=[
             pltpu.VMEM((rows, 4096), BF16),
@@ -164,13 +177,13 @@
         ],
         compiler_params=params(48),
         cost_estimate=pl.CostEstimate(
-            flops=4 * rows * 4096 * 512, bytes_accessed=4 * MIB + rows * 16384, transcendentals=0
+            flops=4 * rows * 4096 * 512, bytes_accessed=8 * MIB, transcendentals=0
         ),
         name="queries",
     )(place, *blocks, w_query)
 
 
-def attend_kernel(pieces, keys, place, span_ids, *refs):
+def attend_kernel(pieces, keys, place, own_span, low_span, key_span, *refs):
     ids_own, ids_low, key_ids, near, far_low, near_low, far = refs[:7]
     arrays, outs, (query, ids, scores, peak, total, context) = refs[7:-10], refs[-10:-6], refs[-6:]
     block = ATTEND_ROWS
@@ -187,23 +200,22 @@
 
     def one_block(at, _):
         rows = pl.ds(pl.multiple_of(at * block, block), block)
-        lowest, highest_id = span_ids[at, 0], span_ids[at, 1]
+        lowest = jnp.where(at == 0, own_span[0, 0], low_span[0, 0])
+        highest_id = jnp.where(at == 0, own_span[3, 127], low_span[3, 127])
         peak[...] = jnp.full_like(peak, -1e30)
         total[...] = jnp.zeros_like(total)
         context[...] = jnp.zeros_like(context)
 
-        def rows_of(held, row):
-            array, lead = held
+        def rows_of(held):
+            array, lead, row = held
             return arrays[array].at[lead + (pl.ds(row, keys),)]
 
         def for_each_part(step):
-            for part, (flip_low, turn, piece_keys, piece_values, row) in enumerate(pieces):
+            for part, (flip_low, turn, row, piece_keys, piece_values) in enumerate(pieces):
                 first = (jnp.bitwise_xor(low, flip_low) * 4 + (z + turn) % 4) * 512 + row
-                meets = (span_ids[2, first] <= highest_id) & (span_ids[2, first + keys - 1] >= lowest)
+                meets = (key_span[0, first] <= highest_id) & (key_span[0, first + keys - 1] >= lowest)
                 pl.when(meets)(
-                    functools.partial(
-                        step, part, rows_of(piece_keys, row), rows_of(piece_values, row), first
-                    )
+                    functools.partial(step, part, rows_of(piece_keys), rows_of(piece_values), first)
                 )
 
         def score(part, part_keys, part_values, first):
@@ -234,33 +246,24 @@
         whole = jnp.sum(total[...], axis=-1, keepdims=True)
         context[...] = context[...] / whole
 
-        mine, core, beside, beside_core = outs
-
-        @pl.when(at == 0)
-        def _():
-            mine[0:128] = context[0:128].astype(BF16)
-            core[0:128] = context[128:256].astype(BF16)
-            beside[128:256] = context[256:384].astype(BF16)
-            beside_core[128:256] = context[384:512].astype(BF16)
-
-        @pl.when(at == 1)
-        def _():
-            beside[0:128] = context[0:128].astype(BF16)
-            beside_core[0:128] = context[128:256].astype(BF16)
-            mine[128:256] = context[256:384].astype(BF16)
-            core[128:256] = context[384:512].astype(BF16)
+        for tile in range(2):
+
+            @pl.when(at == tile)
+            def _():
+                outs[2 * tile][...] = context[0:256].astype(BF16)
+                outs[2 * tile + 1][...] = context[256:512].astype(BF16)
 
         return 0
 
     lax.fori_loop(0, 2, one_block, 0)
 
 
-def attend(keys, pieces, arrays, place, span_ids, ids_own, ids_low, key_ids, blocks):
+def attend(keys, pieces, arrays, place, ids_own, ids_low, key_ids, blocks):
     out = jax.ShapeDtypeStruct((256, HD), BF16)
     return pl.pallas_call(
         functools.partial(attend_kernel, pieces, keys),
         out_shape=(out,) * 4,
-        in_specs=smem(2) + vmem(7 + len(arrays)),
+        in_specs=smem(4) + vmem(7 + len(arrays)),
         out_specs=tuple(vmem(4)),
         scratch_shapes=[
             pltpu.VMEM((2 * ATTEND_ROWS, HD), BF16),
@@ -275,59 +278,56 @@
             flops=4 * 1024 * 4096 * 256, bytes_accessed=6 * MIB, transcendentals=1024 * 1024
         ),
         name="attend",
-    )(place, span_ids, ids_own, ids_low, key_ids, *blocks, *arrays)
-
-
-def output_kernel(row, first, place, c0, c1, c2, c3, w_own, w_core, *refs):
-    residual, (out, weight, arrived) = refs[:-3], refs[-3:]
-    pieces = out.shape[1] // 512
-    copies = [
-        [
-            pltpu.make_async_copy(
-                source.at[:, pl.ds(first + at * 512, 512)], weight.at[core, at], arrived.at[core, at]
-            )
-            for core, source in enumerate((w_own, w_core))
-        ]
-        for at in range(pieces)
-    ]
-    for pair in copies:
-        for copy in pair:
+    )(place, ids_own, ids_low, key_ids, ids_own, ids_low, key_ids, *blocks, *arrays)
+
+
+def output_kernel(first, place, c0, c1, c2, c3, w_own, *refs):
+    pieces, (out, weight, arrived) = refs[:-3], refs[-3:]
+    low, z, width = place[1], place[7], weight.shape[3]
+    steps = out.shape[1] // width
+    copies = []
+    for step in range(steps):
+        columns = pl.ds(first + step * width, width)
+        moves = [(w_own.at[:, columns], weight.at[step, 0])]
+        for head, row, turn, count, at in W_PIECES:
+            start = jnp.bitwise_xor(low, head) * HD + (z + turn) % 4 * 64 + row
+            target = weight.at[step, 1, pl.ds(pl.multiple_of(start, 32), count)]
+            moves.append((pieces[at].at[:, columns], target))
+        copies.append(
+            [
+                pltpu.make_async_copy(source, target, arrived.at[step, at])
+                for at, (source, target) in enumerate(moves)
+            ]
+        )
+    for moves in copies:
+        for copy in moves:
             copy.start()
-    span = slice(row, row + 128)
-    low = place[1]
-    left = jnp.concatenate([c0[span], c2[span]], axis=1)
-    left_core = jnp.concatenate([c1[span], c3[span]], axis=1)
-    swapped = jnp.concatenate([c2[span], c0[span]], axis=1)
-    swapped_core = jnp.concatenate([c3[span], c1[span]], axis=1)
-    left = jnp.where(low == 0, left, swapped)
-    left_core = jnp.where(low == 0, left_core, swapped_core)
-    for at, pair in enumerate(copies):
-        columns = slice(at * 512, (at + 1) * 512)
-        for copy in pair:
+    near = jnp.where(low == 0, jnp.concatenate([c0[...], c2[...]], 1), jnp.concatenate([c2[...], c0[...]], 1))
+    far = jnp.where(low == 0, jnp.concatenate([c1[...], c3[...]], 1), jnp.concatenate([c3[...], c1[...]], 1))
+    for step, moves in enumerate(copies):
+        for copy in moves:
             copy.wait()
-        summed = dot(left, weight[0, at]) + dot(left_core, weight[1, at])
-        for rows in residual:
-            summed = summed + rows[:, columns].astype(F32)
-        out[:, columns] = summed.astype(out.dtype)
-
-
-def outputs(place, contexts, w_own, w_core, row, part, parts, residual=()):
-    width = 4096 // parts
+        summed = dot(near, weight[step, 0]) + dot(far, weight[step, 1])
+        out[:, step * width : (step + 1) * width] = summed.astype(out.dtype)
+
+
+def outputs(place, contexts, w_own, pieces, part, parts):
+    width, step = 4096 // parts, 512
     return pl.pallas_call(
-        functools.partial(output_kernel, row, part * width),
-        out_shape=jax.ShapeDtypeStruct((128, width), F32 if residual else BF16),
-        in_specs=smem(1) + vmem(4) + hbm(2) + vmem(len(residual)),
+        functools.partial(output_kernel, part * width),
+        out_shape=jax.ShapeDtypeStruct((256, width), BF16),
+        in_specs=smem(1) + vmem(4) + hbm(1 + len(pieces)),
         out_specs=vmem(1)[0],
         scratch_shapes=[
-            pltpu.VMEM((2, width // 512, 512, 512), BF16),
-            pltpu.SemaphoreType.DMA((2, width // 512)),
+            pltpu.VMEM((width // step, 2, 512, step), BF16),
+            pltpu.SemaphoreType.DMA((width // step, 1 + len(pieces))),
         ],
         compiler_params=params(48),
         cost_estimate=pl.CostEstimate(
             flops=2 * 256 * width * 1024, bytes_accessed=width * 2048, transcendentals=0
         ),
         name="outputs",
-    )(place, *contexts, w_own, w_core, *residual)
+    )(place, *contexts, w_own, *pieces)
 
 
 def per_device(
@@ -349,79 +349,97 @@
         jnp.int32
     )
 
+    ids_own = decoder_segments[0].reshape(4, 128)
+
     def panel_of(offset, first, count):
         return lax.dynamic_slice(
             encoder_panel, ((section + offset) % 4, first, 0), (1, count, 256)
         )
 
+    w_own = w_output[0]
+
+    def rows_for_cut(head, turn):
+        return lax.dynamic_slice(w_own, (head * HD + (z + turn) % 4 * 64, 0), (64, 4096))
+
+    piece = send(rows_for_cut(1 - low, 0), Y_CUT)
     own = panel_of(0, 0, 512)
-    own_far = send(own, Y_FAR)
-    crossed = [
-        send(panel_of(offset, 0, 512), pairs) for offset, pairs in ((1, X_UP), (3, X_DOWN), (2, X_TWO))
-    ]
-    crossed[0], own_far = lax.optimization_barrier((crossed[0], own_far))
-    panels = [own] + crossed
-    fars = [own_far] + [send(block, Y_FAR) for block in crossed]
-
+    up, down = send(panel_of(1, 0, 512), X_UP), send(panel_of(3, 0, 512), X_DOWN)
     local_rows = decoder_rows[0]
     hidden = normed_rows(local_rows, norm_gain[0])
+    up, down, own_far, two, hidden, piece, w_own = lax.optimization_barrier(
+        (up, down, send(own, Y_FAR), panel_of(2, 0, 512), hidden, piece, w_own)
+    )
+    pair = jnp.concatenate([up, down])
+    two, pair_far, piece_below, piece_above, cut_1, cut_2 = lax.optimization_barrier(
+        (
+            send(two, X_TWO),
+            send(pair, Y_FAR),
+            send(piece, Z_UP),
+            send(piece, Z_DOWN),
+            rows_for_cut(low, 1),
+            rows_for_cut(low, 2),
+        )
+    )
     near_mine, near_other = queries(place, (hidden, send(hidden, CORE)), w_query[0])
-
-    ids_own = decoder_segments[0].reshape(4, 128)
-    ids_low = send(ids_own, Y_LOW)
-    ends = jnp.stack([jnp.stack([ids[0, 0], ids[3, 127]]) for ids in (ids_own, ids_low)])
-    span_ids = jnp.concatenate([jnp.pad(ends, ((0, 0), (0, 4094))), encoder_segments])
-    w_core = send(w_output[0], CORE)
-
-    near_mine, near_other, ids_low, span_ids, fars[1] = lax.optimization_barrier(
-        (near_mine, near_other, ids_low, span_ids, fars[1])
-    )
+    far_rows = [piece, piece_below, piece_above]
+    far_rows += [send(piece_below[:32], Z_UP), send(piece_above[32:], Z_DOWN)]
+    two_far, ids_low, near_mine, near_other, *far_rows = lax.optimization_barrier(
+        (send(two, Y_FAR), send(ids_own, Y_LOW), near_mine, near_other, *far_rows)
+    )
+    panels, fars = [own, pair, two], [own_far, pair_far, two_far]
+
+
     blocks = []
     for near, far in zip(panels, fars):
         blocks += [near, send(near, CORE), far, send(far, CORE)]
     mine, other = key_values(place, blocks, w_key[0], w_value[0])
 
+    hidden, _ = lax.optimization_barrier((hidden, two_far))
+    hidden_cut = send(hidden, Y_CUT)
     below_0, above_0 = send(mine, Z_UP), send(mine, Z_DOWN)
-    theirs, below_0, above_0 = lax.optimization_barrier((send(other, Y_LOW), below_0, above_0))
+    theirs, below_0, above_0, hidden_cut, piece, cut_1 = lax.optimization_barrier(
+        (send(other, Y_LOW), below_0, above_0, hidden_cut, far_rows[0], cut_1)
+    )
     below_1, above_1 = send(theirs, Z_UP), send(theirs, Z_DOWN)
-    across_0 = (send(below_0[0], Z_UP), send(above_0[1], Z_DOWN))
-    hidden, _ = lax.optimization_barrier((hidden, fars[3]))
-    hidden_cut = send(hidden, Y_CUT)
-    hidden_cut, below_1, above_1 = lax.optimization_barrier((hidden_cut, below_1, above_1))
-
-    across_1 = (send(below_1[0], Z_UP), send(above_1[1], Z_DOWN))
 
     far_mine, far_other = queries(place, (hidden_cut, send(hidden_cut, CORE)), w_query[0])
+    other_0, other_1 = send(piece, Y_LOW), send(cut_1, Y_CUT)
+    below_1, above_1, far_mine, far_other, other_0, other_1, piece, cut_2 = (
+        lax.optimization_barrier(
+            (below_1, above_1, far_mine, far_other, other_0, other_1, far_rows[1], cut_2)
+        )
+    )
+    across_keys = send(jnp.concatenate([below_0[0], below_1[0]]), Z_UP)
+    across_values = send(jnp.concatenate([above_0[1], above_1[1]]), Z_DOWN)
+    far_rows += [other_0, send(piece, Y_LOW), other_1, send(cut_2, Y_CUT)]
+
     blocks = (near_mine, send(far_other, Y_LOW), send(near_other, Y_LOW), far_mine)
 
-    arrays, pieces = [], []
-    for flip_low, (held, below, above, across) in enumerate(
-        ((mine, below_0, above_0, across_0), (theirs, below_1, above_1, across_1))
+    arrays, pieces = [across_keys, across_values], []
+    for flip_low, (held, below, above) in enumerate(
+        ((mine, below_0, above_0), (theirs, below_1, above_1))
     ):
-        base = len(arrays)
-        arrays.extend([held, below, above, *across])
-        for turn, keys, values in (
-            (0, (base, (0,)), (base, (1,))),
-            (3, (base + 1, (0,)), (base + 1, (1,))),
-            (1, (base + 2, (0,)), (base + 2, (1,))),
-            (2, (base + 3, ()), (base + 4, ())),
-        ):
+        for turn, whole in ((0, held), (3, below), (1, above)):
+            at = len(arrays)
+            arrays.append(whole)
             for row in range(0, 512, KEYS):
-                pieces.append((flip_low, turn, keys, values, row))
+                pieces.append((flip_low, turn, row, (at, (0,), row), (at, (1,), row)))
+        for row in range(0, 512, KEYS):
+            held_row = flip_low * 512 + row
+            pieces.append((flip_low, 2, row, (0, (), held_row), (1, (), held_row)))
 
     contexts = attend(
-        KEYS, pieces, arrays, place, span_ids, ids_own, ids_low, encoder_segments, blocks
+        KEYS, pieces, arrays, place, ids_own, ids_low, encoder_segments, blocks
     )
 
     contexts = (contexts[0],) + tuple(
-        send(context, pairs) for context, pairs in zip(contexts[1:], (CORE, Y_LOW, Y_LOW_CORE))
-    )
-    w_own = w_output[0]
-    arrived = [
-        send(outputs(place, contexts, w_own, w_core, 128, part, 2), Y_CUT) for part in range(2)
-    ]
-    near = outputs(place, contexts, w_own, w_core, 0, 0, 1, (local_rows,))
-    return (near + jnp.concatenate(arrived, axis=1).astype(F32)).astype(BF16)[None]
+        send(context, pairs) for context, pairs in zip(contexts[1:], (Y_FAR, Y_LOW, Y_CUT))
+    )
+    summed = []
+    for part in range(2):
+        both = outputs(place, contexts, w_own, far_rows, part, 2)
+        summed.append(both[:128].astype(F32) + send(both[128:], CORE).astype(F32))
+    return (jnp.concatenate(summed, axis=1) + local_rows.astype(F32)).astype(BF16)[None]
 
 
 def solution(mesh):

time: 153 us -> 149 us (0.974); the launches traced: 153 us -> 151 us
  waiting for transfers between devices: 61.7 us -> 55.6 us
  other arithmetic: 7.87 us -> 2.17 us
  starting transfers between devices: 46.3 us -> 50.1 us
  local copies, waits for them, and re-layouts: 2.36 us -> 5.76 us
  Pallas kernels: 34.5 us -> 37.1 us
    ppermute x36 -> x39, waiting for transfers between devices: 61.7 us -> 55.6 us  [send(): return lax.ppermute(array, AXES, pairs)]
    ppermute x36 -> x39, starting transfers between devices: 46.3 us -> 50.1 us  [send(): return lax.ppermute(array, AXES, pairs)]
    pallas_call x1, Pallas kernels: 9.7 us -> 13.2 us  [attend(): pl.pallas_call(functools.partial(attend_kernel, pieces, keys), out_shape=...]
    dynamic_slice x0 -> x2, local copies, waits for them, and re-layouts: none -> 3.45 us  [rows_for_cut(): lax.dynamic_slice(w_own, (head * HD + (z + turn) % 4 * 64, 0), (64, 4096))]
    pallas_call x3 -> x2, Pallas kernels: 10.4 us -> 7.5 us  [outputs(): pl.pallas_call(functools.partial(output_kernel, part * width), out_shape=...]
    another operation x2 -> x0, other arithmetic: 2.73 us -> none  [per_device(): jnp.stack([jnp.stack([ids[0, 0], ids[3, 127]]) for ids in (ids_own, ids_l...]
  transfers between devices with their start and end apart: 36 -> 39, of which waited for: 18 -> 21; matrix products, arithmetic and copies ran while one was open for 3% -> 4% of each run, Pallas kernels for 21% -> 22%
where the time goes in v3:
time: 149 us; the launch traced here: 151 us
  waiting for transfers between devices  55.6 us (37%)
  starting transfers between devices  50.1 us (34%)
  Pallas kernels  37.1 us (25%)
  local copies, waits for them, and re-layouts  5.76 us (4%)
  other arithmetic  2.17 us (1%)
    ppermute x39, waiting for transfers between devices, send(): return lax.ppermute(array, AXES, pairs)  55.6 us
    ppermute x39, starting transfers between devices, send(): return lax.ppermute(array, AXES, pairs)  50.1 us
    pallas_call x1, Pallas kernels, attend(): pl.pallas_call(functools.partial(attend_kernel, pieces, keys), out_shape=...  13.2 us
    pallas_call x1, Pallas kernels, key_values(): pl.pallas_call(key_value_kernel, out_shape=(out, out), in_specs=smem(1) +...  9.18 us
    pallas_call x2, Pallas kernels, outputs(): pl.pallas_call(functools.partial(output_kernel, part * width), out_shape=...  7.5 us
    pallas_call x2, Pallas kernels, queries(): pl.pallas_call(query_kernel, out_shape=(out, out), in_specs=smem(1) + vme...  7.24 us
    dynamic_slice x2, local copies, waits for them, and re-layouts, rows_for_cut(): lax.dynamic_slice(w_own, (head * HD + (z + turn) % 4 * 64, 0), (64, 4096))  3.45 us
  transfers between devices with their start and end apart: 39, of which 21 were waited for; matrix products, arithmetic and copies ran while one was open for 4% of the time, Pallas kernels for 22%

profile of v3, /device:TPU:1, one launch (start us, length us, event | category | flops | bytes accessed | tf_op | source)
XLA Modules:
  0.0 151.0 jit_solution(13749671209210476231)
XLA Ops:
  0.0 1.2 dynamic-slice_bitcast_fusion
  1.2 3.6 %collective-permute-start.3 = (bf16[64,4096]{1,0:T(8,128)(2,1)S(1)}, bf16[64,4096]{1,0:T(8,128)(2,1)S(1)}, u32[]{:S(2)}, u32[]{:S(2)}) collective-permute-start(bf16[64,4096]{1,0:T(8,128)(2,1)S(1)} %dynamic-slice_bitcast_fusion), channel_id=1, source_target_pairs={{0,18},{1,19},{2,16},{3,17},{4,22},{5,23},{6,20},{7,21},{8,26},{9,... | collective-permute-start | bytes 1572872 | tf_op jit(solution)/shard_map/ppermute | solution.py:61
  4.8 2.0 %constant_dynamic-slice_fusion.2 = (bf16[1,512,256]{2,1,0:T(8,128)(2,1)}, bf16[1,512,256]{2,1,0:T(8,128)(2,1)S(1)}, bf16[1,512,256]{2,1,0:T(8,128)(2,1)S(1)}, bf16[1,512,256]{2,1,0:T(8,128)(2,1)S(1)}) fusion(bf16[4,512,256]{2,1,0:T(8,128)(2,1)} %param.10, s32[]{:T(128)S(6)} %select_n.80, s32[]{:T(128)S(6)} %select_n.78, s32[]{:T(128)S(6)} %select_n.76, ...), kind=kLoop, calls=%fused_computation.21 | loop fusion | bytes 2097168 | tf_op jit(solution)/shard_map/dynamic_slice | solution.py:355
  6.8 1.2 collective-permute-start
  8.0 1.5 collective-permute-start.1
  10.5 4.3 %collective-permute-done = bf16[1,512,256]{2,1,0:T(8,128)(2,1)S(1)} collective-permute-done((bf16[1,512,256]{2,1,0:T(8,128)(2,1)S(1)}, bf16[1,512,256]{2,1,0:T(8,128)(2,1)S(1)}, u32[]{:S(2)}, u32[]{:S(2)}) %collective-permute-start) | collective-permute-done | bytes 262176 | tf_op jit(solution)/shard_map/ppermute | solution.py:61
  14.8 2.6 %collective-permute-done.2.refs_2_ = bf16[1,512,256]{2,1,0:T(8,128)(2,1)} collective-permute-done((bf16[1,512,256]{2,1,0:T(8,128)(2,1)S(1)}, bf16[1,512,256]{2,1,0:T(8,128)(2,1)}, u32[]{:S(2)}, u32[]{:S(2)}) %collective-permute-start.2) | collective-permute-done | bytes 262176 | tf_op jit(solution)/shard_map/ppermute | solution.py:61
  17.4 4.5 %collective-permute-done.3.refs_0_ = bf16[64,4096]{1,0:T(8,128)(2,1)S(1)} collective-permute-done((bf16[64,4096]{1,0:T(8,128)(2,1)S(1)}, bf16[64,4096]{1,0:T(8,128)(2,1)S(1)}, u32[]{:S(2)}, u32[]{:S(2)}) %collective-permute-start.3) | collective-permute-done | bytes 524320 | tf_op jit(solution)/shard_map/ppermute | solution.py:61
  21.9 1.4 collective-permute-start.10
  23.4 1.7 %collective-permute-start.5 = (bf16[2,512,256]{2,1,0:T(8,128)(2,1)S(1)}, bf16[2,512,256]{2,1,0:T(8,128)(2,1)}, u32[]{:S(2)}, u32[]{:S(2)}) collective-permute-start(bf16[2,512,256]{2,1,0:T(8,128)(2,1)S(1)} %constant_dynamic-update-slice_fusion.refs_4_), channel_id=1, source_target_pairs={{0,2},{1,3},{2,0},{3,1},{4,6},{5,7},{6,4},{7,5},{8,10},{9,11},{10,... | collective-permute-start | bytes 1572872 | tf_op jit(solution)/shard_map/ppermute | solution.py:61
  25.1 1.6 %collective-permute-start.6 = (bf16[64,4096]{1,0:T(8,128)(2,1)S(1)}, bf16[64,4096]{1,0:T(8,128)(2,1)S(1)}, u32[]{:S(2)}, u32[]{:S(2)}) collective-permute-start(bf16[64,4096]{1,0:T(8,128)(2,1)S(1)} %collective-permute-done.3.refs_0_), channel_id=1, source_target_pairs={{0,4},{1,5},{2,6},{3,7},{4,8},{5,9},{6,10},{7,11},{8,12},{9,13},{1... | collective-permute-start | bytes 1572872 | tf_op jit(solution)/shard_map/ppermute | solution.py:61
  26.7 2.1 %collective-permute-start.7 = (bf16[64,4096]{1,0:T(8,128)(2,1)S(1)}, bf16[64,4096]{1,0:T(8,128)(2,1)S(1)}, u32[]{:S(2)}, u32[]{:S(2)}) collective-permute-start(bf16[64,4096]{1,0:T(8,128)(2,1)S(1)} %collective-permute-done.3.refs_0_), channel_id=1, source_target_pairs={{0,12},{1,13},{2,14},{3,15},{4,0},{5,1},{6,2},{7,3},{8,4},{9,5},{1... | collective-permute-start | bytes 1572872 | tf_op jit(solution)/shard_map/ppermute | solution.py:61
  28.9 2.7 %collective-permute-start.4 = (bf16[1,512,256]{2,1,0:T(8,128)(2,1)}, bf16[1,512,256]{2,1,0:T(8,128)(2,1)}, u32[]{:S(2)}, u32[]{:S(2)}) collective-permute-start(bf16[1,512,256]{2,1,0:T(8,128)(2,1)} %get-tuple-element.52), channel_id=1, source_target_pairs={{0,64},{1,65},{2,66},{3,67},{4,68},{5,69},{6,70},{7,71},{8,72},{9,... | collective-permute-start | bytes 786440 | tf_op jit(solution)/shard_map/ppermute | solution.py:61
  31.6 2.3 %constant_dynamic-slice_fusion = (bf16[64,4096]{1,0:T(8,128)(2,1)}, bf16[64,4096]{1,0:T(8,128)(2,1)}) fusion(bf16[512,4096]{1,0:T(8,128)(2,1)} %bitcast.43, s32[]{:T(128)S(6)} %select_n.86, s32[]{:T(128)S(6)} %select_n.84), kind=kLoop, calls=%fused_computation.19 | loop fusion | bytes 2097160 | tf_op jit(solution)/shard_map/dynamic_slice | solution.py:362
  33.9 4.1 %collective-permute-done.4.refs_8_ = bf16[1,512,256]{2,1,0:T(8,128)(2,1)} collective-permute-done((bf16[1,512,256]{2,1,0:T(8,128)(2,1)}, bf16[1,512,256]{2,1,0:T(8,128)(2,1)}, u32[]{:S(2)}, u32[]{:S(2)}) %collective-permute-start.4) | collective-permute-done | bytes 262176 | tf_op jit(solution)/shard_map/ppermute | solution.py:61
  38.6 2.3 %collective-permute-done.6.refs_1_ = bf16[64,4096]{1,0:T(8,128)(2,1)S(1)} collective-permute-done((bf16[64,4096]{1,0:T(8,128)(2,1)S(1)}, bf16[64,4096]{1,0:T(8,128)(2,1)S(1)}, u32[]{:S(2)}, u32[]{:S(2)}) %collective-permute-start.6) | collective-permute-done | bytes 524320 | tf_op jit(solution)/shard_map/ppermute | solution.py:61
  41.4 2.4 %collective-permute-start.12 = (bf16[32,4096]{1,0:T(8,128)(2,1)S(1)}, bf16[32,4096]{1,0:T(8,128)(2,1)S(1)}, u32[]{:S(2)}, u32[]{:S(2)}) collective-permute-start(bf16[32,4096]{1,0:T(8,128)(2,1)S(1)} %slice.31), channel_id=1, source_target_pairs={{0,12},{1,13},{2,14},{3,15},{4,0},{5,1},{6,2},{7,3},{8,4},{9,5},{1... | collective-permute-start | bytes 786440 | tf_op jit(solution)/shard_map/ppermute | solution.py:61
  43.8 1.6 %collective-permute-start.9 = (s32[4,128]{1,0:T(4,128)S(1)}, s32[4,128]{1,0:T(4,128)S(1)}, u32[]{:S(2)}, u32[]{:S(2)}) collective-permute-start(s32[4,128]{1,0:T(4,128)S(1)} %bitcast.40), channel_id=1, source_target_pairs={{0,16},{1,17},{2,18},{3,19},{4,20},{5,21},{6,22},{7,23},{8,24},{9,... | collective-permute-start | bytes 6152 | tf_op jit(solution)/shard_map/ppermute | solution.py:61
  46.7 2.1 %collective-permute-start.13 = (bf16[1,512,256]{2,1,0:T(8,128)(2,1)S(1)}, bf16[1,512,256]{2,1,0:T(8,128)(2,1)}, u32[]{:S(2)}, u32[]{:S(2)}) collective-permute-start(bf16[1,512,256]{2,1,0:T(8,128)(2,1)S(1)} %get-tuple-element.104.refs_0_), channel_id=1, source_target_pairs={{0,1},{1,0},{2,3},{3,2},{4,5},{5,4},{6,7},{7,6},{8,9},{9,8},{10,11... | collective-permute-start | bytes 786440 | tf_op jit(solution)/shard_map/ppermute | solution.py:61
  49.3 1.7 %collective-permute-start.15 = (bf16[2,512,256]{2,1,0:T(8,128)(2,1)}, bf16[2,512,256]{2,1,0:T(8,128)(2,1)}, u32[]{:S(2)}, u32[]{:S(2)}) collective-permute-start(bf16[2,512,256]{2,1,0:T(8,128)(2,1)} %copy-done), channel_id=1, source_target_pairs={{0,1},{1,0},{2,3},{3,2},{4,5},{5,4},{6,7},{7,6},{8,9},{9,8},{10,11... | collective-permute-start | bytes 1572872 | tf_op jit(solution)/shard_map/ppermute | solution.py:61
  51.6 4.0 %queries.2 = (bf16[256,256]{1,0:T(8,128)(2,1)S(1)}, bf16[256,256]{1,0:T(8,128)(2,1)S(1)}) custom-call(s32[8]{0:T(128)S(1)} %stack.35.place, bf16[128,4096]{1,0:T(8,128)(2,1)S(1)} %fusion.4.h0, bf16[128,4096]{1,0:T(8,128)(2,1)} %collective-permute-done.10.h1, bf16[4096,512]{1,0:T(8,128)(2,1)} %bitcast.46), custom_call_target="tpu_custom_call" | custom-call | flops 1073741824 | bytes 8388608 | tf_op jit(solution)/shard_map/queries/pallas_call | solution.py:168
  56.2 1.5 collective-permute-start.22
  57.8 9.2 %key_values.1 = (bf16[2,512,256]{2,1,0:T(8,128)(2,1)S(1)}, bf16[2,512,256]{2,1,0:T(8,128)(2,1)S(1)}) custom-call(s32[8]{0:T(128)S(1)} %stack.35.place, bf16[1,512,256]{2,1,0:T(8,128)(2,1)S(1)} %get-tuple-element.104.refs_0_, bf16[1,512,256]{2,1,0:T(8,128)(2,1)} %collective-permute-done.13.refs_1_, bf16[1,512,256]{2,1,0:T(8,128)(2,1)} %collective-permute-done.2.refs_2_, ...), custom_call_target="tpu_custom_call" | custom-call | flops 4294967296 | bytes 12582912 | tf_op jit(solution)/shard_map/key_values/pallas_call | solution.py:130
  67.0 1.7 %collective-permute-start.19 = (bf16[2,512,256]{2,1,0:T(8,128)(2,1)S(1)}, bf16[2,512,256]{2,1,0:T(8,128)(2,1)S(1)}, u32[]{:S(2)}, u32[]{:S(2)}) collective-permute-start(bf16[2,512,256]{2,1,0:T(8,128)(2,1)S(1)} %get-tuple-element.68), channel_id=1, source_target_pairs={{0,16},{1,17},{2,18},{3,19},{4,20},{5,21},{6,22},{7,23},{8,24},{9,... | collective-permute-start | bytes 1572872 | tf_op jit(solution)/shard_map/ppermute | solution.py:61
  68.9 2.4 %collective-permute-start.21 = (bf16[2,512,256]{2,1,0:T(8,128)(2,1)S(1)}, bf16[2,512,256]{2,1,0:T(8,128)(2,1)S(1)}, u32[]{:S(2)}, u32[]{:S(2)}) collective-permute-start(bf16[2,512,256]{2,1,0:T(8,128)(2,1)S(1)} %get-tuple-element.69.refs_9_), channel_id=1, source_target_pairs={{0,12},{1,13},{2,14},{3,15},{4,0},{5,1},{6,2},{7,3},{8,4},{9,5},{1... | collective-permute-start | bytes 1572872 | tf_op jit(solution)/shard_map/ppermute | solution.py:61
  71.4 9.3 %collective-permute-done.19.refs_12_ = bf16[2,512,256]{2,1,0:T(8,128)(2,1)S(1)} collective-permute-done((bf16[2,512,256]{2,1,0:T(8,128)(2,1)S(1)}, bf16[2,512,256]{2,1,0:T(8,128)(2,1)S(1)}, u32[]{:S(2)}, u32[]{:S(2)}) %collective-permute-start.19) | collective-permute-done | bytes 524320 | tf_op jit(solution)/shard_map/ppermute | solution.py:61
  80.6 2.3 %collective-permute-done.20.refs_10_ = bf16[2,512,256]{2,1,0:T(8,128)(2,1)S(1)} collective-permute-done((bf16[2,512,256]{2,1,0:T(8,128)(2,1)S(1)}, bf16[2,512,256]{2,1,0:T(8,128)(2,1)S(1)}, u32[]{:S(2)}, u32[]{:S(2)}) %collective-permute-start.20) | collective-permute-done | bytes 524320 | tf_op jit(solution)/shard_map/ppermute | solution.py:61
  83.0 1.3 collective-permute-start.25
  84.8 2.1 %collective-permute-start.24 = (bf16[2,512,256]{2,1,0:T(8,128)(2,1)S(1)}, bf16[2,512,256]{2,1,0:T(8,128)(2,1)S(1)}, u32[]{:S(2)}, u32[]{:S(2)}) collective-permute-start(bf16[2,512,256]{2,1,0:T(8,128)(2,1)S(1)} %collective-permute-done.19.refs_12_), channel_id=1, source_target_pairs={{0,12},{1,13},{2,14},{3,15},{4,0},{5,1},{6,2},{7,3},{8,4},{9,5},{1... | collective-permute-start | bytes 1572872 | tf_op jit(solution)/shard_map/ppermute | solution.py:61
  87.2 1.0 collective-permute-start.27
  88.3 3.2 %queries.3 = (bf16[256,256]{1,0:T(8,128)(2,1)S(1)}, bf16[256,256]{1,0:T(8,128)(2,1)S(1)}) custom-call(s32[8]{0:T(128)S(1)} %stack.35.place, bf16[128,4096]{1,0:T(8,128)(2,1)S(1)} %collective-permute-done.22.h0, bf16[128,4096]{1,0:T(8,128)(2,1)S(1)} %collective-permute-done.25.h1, bf16[4096,512]{1,0:T(8,128)(2,1)} %bitcast.47), custom_call_target="tpu_custom_call" | custom-call | flops 1073741824 | bytes 8388608 | tf_op jit(solution)/shard_map/queries/pallas_call | solution.py:168
  91.6 7.4 %collective-permute-done.23.refs_13_ = bf16[2,512,256]{2,1,0:T(8,128)(2,1)S(1)} collective-permute-done((bf16[2,512,256]{2,1,0:T(8,128)(2,1)S(1)}, bf16[2,512,256]{2,1,0:T(8,128)(2,1)S(1)}, u32[]{:S(2)}, u32[]{:S(2)}) %collective-permute-start.23) | collective-permute-done | bytes 524320 | tf_op jit(solution)/shard_map/ppermute | solution.py:61
  99.8 1.2 collective-permute-done.27.refs_7_
  101.0 1.6 %collective-permute-start.31 = (bf16[1024,256]{1,0:T(8,128)(2,1)S(1)}, bf16[1024,256]{1,0:T(8,128)(2,1)S(1)}, u32[]{:S(2)}, u32[]{:S(2)}) collective-permute-start(bf16[1024,256]{1,0:T(8,128)(2,1)S(1)} %pad_maximum_fusion.1), channel_id=1, source_target_pairs={{0,12},{1,13},{2,14},{3,15},{4,0},{5,1},{6,2},{7,3},{8,4},{9,5},{1... | collective-permute-start | bytes 1572872 | tf_op jit(solution)/shard_map/ppermute | solution.py:61
  102.8 1.5 collective-permute-start.28
  104.4 2.6 %collective-permute-done.29.refs_5_ = bf16[256,256]{1,0:T(8,128)(2,1)S(1)} collective-permute-done((bf16[256,256]{1,0:T(8,128)(2,1)S(1)}, bf16[256,256]{1,0:T(8,128)(2,1)S(1)}, u32[]{:S(2)}, u32[]{:S(2)}) %collective-permute-start.29) | collective-permute-done | bytes 131104 | tf_op jit(solution)/shard_map/ppermute | solution.py:61
  108.4 4.3 %collective-permute-done.31.refs_8_ = bf16[1024,256]{1,0:T(8,128)(2,1)S(1)} collective-permute-done((bf16[1024,256]{1,0:T(8,128)(2,1)S(1)}, bf16[1024,256]{1,0:T(8,128)(2,1)S(1)}, u32[]{:S(2)}, u32[]{:S(2)}) %collective-permute-start.31) | collective-permute-done | bytes 524320 | tf_op jit(solution)/shard_map/ppermute | solution.py:61
  112.7 2.7 %collective-permute-done.30.refs_7_ = bf16[1024,256]{1,0:T(8,128)(2,1)S(1)} collective-permute-done((bf16[1024,256]{1,0:T(8,128)(2,1)S(1)}, bf16[1024,256]{1,0:T(8,128)(2,1)S(1)}, u32[]{:S(2)}, u32[]{:S(2)}) %collective-permute-start.30) | collective-permute-done | bytes 524320 | tf_op jit(solution)/shard_map/ppermute | solution.py:61
  115.3 13.2 %attend.1 = (bf16[256,256]{1,0:T(8,128)(2,1)S(1)}, bf16[256,256]{1,0:T(8,128)(2,1)S(1)}, bf16[256,256]{1,0:T(8,128)(2,1)S(1)}, bf16[256,256]{1,0:T(8,128)(2,1)S(1)}) custom-call(s32[8]{0:T(128)S(1)} %stack.35.place, s32[4,128]{1,0:T(4,128)S(1)} %bitcast.41, s32[4,128]{1,0:T(4,128)S(1)} %collective-permute-done.9.low_span.refs_1_, s32[1,4096]{1,0:T(1,128)S(1)} %copy-done.2, ...), custom_call_target="tpu_custom_call" | custom-call | flops 4294967296 | bytes 6291456 | tf_op jit(solution)/shard_map/attend/pallas_call | solution.py:263
  129.2 1.1 collective-permute-start.33
  130.3 1.6 %collective-permute-start.34 = (bf16[256,256]{1,0:T(8,128)(2,1)S(1)}, bf16[256,256]{1,0:T(8,128)(2,1)S(1)}, u32[]{:S(2)}, u32[]{:S(2)}) collective-permute-start(bf16[256,256]{1,0:T(8,128)(2,1)S(1)} %get-tuple-element.91), channel_id=1, source_target_pairs={{0,18},{1,19},{2,16},{3,17},{4,22},{5,23},{6,20},{7,21},{8,26},{9,... | collective-permute-start | bytes 393224 | tf_op jit(solution)/shard_map/ppermute | solution.py:61
  131.9 2.1 %collective-permute-done.32.c1 = bf16[256,256]{1,0:T(8,128)(2,1)S(1)} collective-permute-done((bf16[256,256]{1,0:T(8,128)(2,1)S(1)}, bf16[256,256]{1,0:T(8,128)(2,1)S(1)}, u32[]{:S(2)}, u32[]{:S(2)}) %collective-permute-start.32) | collective-permute-done | bytes 131104 | tf_op jit(solution)/shard_map/ppermute | solution.py:61
  134.0 1.4 collective-permute-done.34.c3
  135.4 3.7 %outputs.2 = bf16[256,2048]{1,0:T(8,128)(2,1)S(1)} custom-call(s32[8]{0:T(128)S(1)} %stack.35.place, bf16[256,256]{1,0:T(8,128)(2,1)S(1)} %get-tuple-element.88.c0, bf16[256,256]{1,0:T(8,128)(2,1)S(1)} %collective-permute-done.32.c1, bf16[256,256]{1,0:T(8,128)(2,1)S(1)} %collective-permute-done.33.c2, bf16[256,256]{1,0:T(8,128)(2,1)S(1)} %collective-permute-done.34.c3, ...), custom_call_target="tpu_custom_call" | custom-call | flops 1073741824 | bytes 4194304 | tf_op jit(solution)/shard_map/outputs/pallas_call | solution.py:316
  139.2 4.6 %collective-permute-start.37 = (bf16[128,2048]{1,0:T(8,128)(2,1)S(1)}, bf16[128,2048]{1,0:T(8,128)(2,1)S(1)}, u32[]{:S(2)}, u32[]{:S(2)}) collective-permute-start(bf16[128,2048]{1,0:T(8,128)(2,1)S(1)} %slice.41), channel_id=1, source_target_pairs={{0,1},{1,0},{2,3},{3,2},{4,5},{5,4},{6,7},{7,6},{8,9},{9,8},{10,11... | collective-permute-start | bytes 1572872 | tf_op jit(solution)/shard_map/ppermute | solution.py:61
  143.8 3.7 %outputs.3 = bf16[256,2048]{1,0:T(8,128)(2,1)S(1)} custom-call(s32[8]{0:T(128)S(1)} %stack.35.place, bf16[256,256]{1,0:T(8,128)(2,1)S(1)} %get-tuple-element.88.c0, bf16[256,256]{1,0:T(8,128)(2,1)S(1)} %collective-permute-done.32.c1, bf16[256,256]{1,0:T(8,128)(2,1)S(1)} %collective-permute-done.33.c2, bf16[256,256]{1,0:T(8,128)(2,1)S(1)} %collective-permute-done.34.c3, ...), custom_call_target="tpu_custom_call" | custom-call | flops 1073741824 | bytes 4194304 | tf_op jit(solution)/shard_map/outputs/pallas_call | solution.py:316
  147.9 1.8 %collective-permute-done.38 = bf16[128,2048]{1,0:T(8,128)(2,1)S(1)} collective-permute-done((bf16[128,2048]{1,0:T(8,128)(2,1)S(1)}, bf16[128,2048]{1,0:T(8,128)(2,1)S(1)}, u32[]{:S(2)}, u32[]{:S(2)}) %collective-permute-start.38) | collective-permute-done | bytes 524320 | tf_op jit(solution)/shard_map/ppermute | solution.py:61
  149.8 1.2 fusion.5
  (77 shorter events, 10.2 us)
Async XLA Ops:
  0.0 9.8 %copy-start.8 = (bf16[1,4096]{1,0:T(2,128)(2,1)S(1)}, bf16[1,4096]{1,0:T(2,128)(2,1)}, u32[]{:S(2)}) copy-start(bf16[1,4096]{1,0:T(2,128)(2,1)} %param.11) | copy-start | bytes 24580
  0.0 9.8 %copy-start.4 = (bf16[1,128,4096]{2,1,0:T(8,128)(2,1)S(1)}, bf16[1,128,4096]{2,1,0:T(8,128)(2,1)}, u32[]{:S(2)}) copy-start(bf16[1,128,4096]{2,1,0:T(8,128)(2,1)} %param.9) | copy-start | bytes 3145732
  1.2 20.8 %collective-permute-start.3 = (bf16[64,4096]{1,0:T(8,128)(2,1)S(1)}, bf16[64,4096]{1,0:T(8,128)(2,1)S(1)}, u32[]{:S(2)}, u32[]{:S(2)}) collective-permute-start(bf16[64,4096]{1,0:T(8,128)(2,1)S(1)} %dynamic-slice_bitcast_fusion), channel_id=1, source_target_pairs={{0,18},{1,19},{2,16},{3,17},{4,22},{5,23},{6,20},{7,21},{8,26},{9,... | collective-permute-start | bytes 1572872 | tf_op jit(solution)/shard_map/ppermute | solution.py:61
  6.8 8.1 %collective-permute-start = (bf16[1,512,256]{2,1,0:T(8,128)(2,1)S(1)}, bf16[1,512,256]{2,1,0:T(8,128)(2,1)S(1)}, u32[]{:S(2)}, u32[]{:S(2)}) collective-permute-start(bf16[1,512,256]{2,1,0:T(8,128)(2,1)S(1)} %get-tuple-element.103), channel_id=1, source_target_pairs={{0,32},{1,33},{2,34},{3,35},{4,36},{5,37},{6,38},{7,39},{8,40},{9,... | collective-permute-start | bytes 786440 | tf_op jit(solution)/shard_map/ppermute | solution.py:61
  8.0 6.9 %collective-permute-start.1 = (bf16[1,512,256]{2,1,0:T(8,128)(2,1)S(1)}, bf16[1,512,256]{2,1,0:T(8,128)(2,1)S(1)}, u32[]{:S(2)}, u32[]{:S(2)}) collective-permute-start(bf16[1,512,256]{2,1,0:T(8,128)(2,1)S(1)} %get-tuple-element.102), channel_id=1, source_target_pairs={{0,96},{1,97},{2,98},{3,99},{4,100},{5,101},{6,102},{7,103},{8,104... | collective-permute-start | bytes 786440 | tf_op jit(solution)/shard_map/ppermute | solution.py:61
  9.5 8.0 %collective-permute-start.2 = (bf16[1,512,256]{2,1,0:T(8,128)(2,1)S(1)}, bf16[1,512,256]{2,1,0:T(8,128)(2,1)}, u32[]{:S(2)}, u32[]{:S(2)}) collective-permute-start(bf16[1,512,256]{2,1,0:T(8,128)(2,1)S(1)} %get-tuple-element.104.refs_0_), channel_id=1, source_target_pairs={{0,2},{1,3},{2,0},{3,1},{4,6},{5,7},{6,4},{7,5},{8,10},{9,11},{10,... | collective-permute-start | bytes 786440 | tf_op jit(solution)/shard_map/ppermute | solution.py:61
  21.9 21.9 %copy-start.3 = (s32[1,512]{1,0:T(1,128)S(1)}, s32[1,512]{1,0:T(1,128)}, u32[]{:S(2)}) copy-start(s32[1,512]{1,0:T(1,128)} %param.16) | copy-start | bytes 6148
  21.9 29.1 %collective-permute-start.10 = (bf16[128,4096]{1,0:T(8,128)(2,1)S(1)}, bf16[128,4096]{1,0:T(8,128)(2,1)}, u32[]{:S(2)}, u32[]{:S(2)}) collective-permute-start(bf16[128,4096]{1,0:T(8,128)(2,1)S(1)} %fusion.4.h0), channel_id=1, source_target_pairs={{0,1},{1,0},{2,3},{3,2},{4,5},{5,4},{6,7},{7,6},{8,9},{9,8},{10,11... | collective-permute-start | bytes 3145736 | tf_op jit(solution)/shard_map/ppermute | solution.py:61
  23.4 17.6 %copy-start = (bf16[2,512,256]{2,1,0:T(8,128)(2,1)}, bf16[2,512,256]{2,1,0:T(8,128)(2,1)S(1)}, u32[]{:S(2)}) copy-start(bf16[2,512,256]{2,1,0:T(8,128)(2,1)S(1)} %constant_dynamic-update-slice_fusion.refs_4_) | copy-start | bytes 1572868
  23.4 15.2 %collective-permute-start.5 = (bf16[2,512,256]{2,1,0:T(8,128)(2,1)S(1)}, bf16[2,512,256]{2,1,0:T(8,128)(2,1)}, u32[]{:S(2)}, u32[]{:S(2)}) collective-permute-start(bf16[2,512,256]{2,1,0:T(8,128)(2,1)S(1)} %constant_dynamic-update-slice_fusion.refs_4_), channel_id=1, source_target_pairs={{0,2},{1,3},{2,0},{3,1},{4,6},{5,7},{6,4},{7,5},{8,10},{9,11},{10,... | collective-permute-start | bytes 1572872 | tf_op jit(solution)/shard_map/ppermute | solution.py:61
  25.1 15.8 %collective-permute-start.6 = (bf16[64,4096]{1,0:T(8,128)(2,1)S(1)}, bf16[64,4096]{1,0:T(8,128)(2,1)S(1)}, u32[]{:S(2)}, u32[]{:S(2)}) collective-permute-start(bf16[64,4096]{1,0:T(8,128)(2,1)S(1)} %collective-permute-done.3.refs_0_), channel_id=1, source_target_pairs={{0,4},{1,5},{2,6},{3,7},{4,8},{5,9},{6,10},{7,11},{8,12},{9,13},{1... | collective-permute-start | bytes 1572872 | tf_op jit(solution)/shard_map/ppermute | solution.py:61
  26.7 14.2 %collective-permute-start.7 = (bf16[64,4096]{1,0:T(8,128)(2,1)S(1)}, bf16[64,4096]{1,0:T(8,128)(2,1)S(1)}, u32[]{:S(2)}, u32[]{:S(2)}) collective-permute-start(bf16[64,4096]{1,0:T(8,128)(2,1)S(1)} %collective-permute-done.3.refs_0_), channel_id=1, source_target_pairs={{0,12},{1,13},{2,14},{3,15},{4,0},{5,1},{6,2},{7,3},{8,4},{9,5},{1... | collective-permute-start | bytes 1572872 | tf_op jit(solution)/shard_map/ppermute | solution.py:61
  28.9 9.1 %collective-permute-start.4 = (bf16[1,512,256]{2,1,0:T(8,128)(2,1)}, bf16[1,512,256]{2,1,0:T(8,128)(2,1)}, u32[]{:S(2)}, u32[]{:S(2)}) collective-permute-start(bf16[1,512,256]{2,1,0:T(8,128)(2,1)} %get-tuple-element.52), channel_id=1, source_target_pairs={{0,64},{1,65},{2,66},{3,67},{4,68},{5,69},{6,70},{7,71},{8,72},{9,... | collective-permute-start | bytes 786440 | tf_op jit(solution)/shard_map/ppermute | solution.py:61
  41.0 8.3 %collective-permute-start.11 = (bf16[32,4096]{1,0:T(8,128)(2,1)S(1)}, bf16[32,4096]{1,0:T(8,128)(2,1)S(1)}, u32[]{:S(2)}, u32[]{:S(2)}) collective-permute-start(bf16[32,4096]{1,0:T(8,128)(2,1)S(1)} %slice.30), channel_id=1, source_target_pairs={{0,4},{1,5},{2,6},{3,7},{4,8},{5,9},{6,10},{7,11},{8,12},{9,13},{1... | collective-permute-start | bytes 786440 | tf_op jit(solution)/shard_map/ppermute | solution.py:61
  41.4 9.6 %collective-permute-start.12 = (bf16[32,4096]{1,0:T(8,128)(2,1)S(1)}, bf16[32,4096]{1,0:T(8,128)(2,1)S(1)}, u32[]{:S(2)}, u32[]{:S(2)}) collective-permute-start(bf16[32,4096]{1,0:T(8,128)(2,1)S(1)} %slice.31), channel_id=1, source_target_pairs={{0,12},{1,13},{2,14},{3,15},{4,0},{5,1},{6,2},{7,3},{8,4},{9,5},{1... | collective-permute-start | bytes 786440 | tf_op jit(solution)/shard_map/ppermute | solution.py:61
  43.8 2.9 %collective-permute-start.9 = (s32[4,128]{1,0:T(4,128)S(1)}, s32[4,128]{1,0:T(4,128)S(1)}, u32[]{:S(2)}, u32[]{:S(2)}) collective-permute-start(s32[4,128]{1,0:T(4,128)S(1)} %bitcast.40), channel_id=1, source_target_pairs={{0,16},{1,17},{2,18},{3,19},{4,20},{5,21},{6,22},{7,23},{8,24},{9,... | collective-permute-start | bytes 6152 | tf_op jit(solution)/shard_map/ppermute | solution.py:61
  45.4 10.2 %collective-permute-start.8 = (bf16[1,512,256]{2,1,0:T(8,128)(2,1)}, bf16[1,512,256]{2,1,0:T(8,128)(2,1)}, u32[]{:S(2)}, u32[]{:S(2)}) collective-permute-start(bf16[1,512,256]{2,1,0:T(8,128)(2,1)} %collective-permute-done.4.refs_8_), channel_id=1, source_target_pairs={{0,2},{1,3},{2,0},{3,1},{4,6},{5,7},{6,4},{7,5},{8,10},{9,11},{10,... | collective-permute-start | bytes 786440 | tf_op jit(solution)/shard_map/ppermute | solution.py:61
  46.7 9.3 %collective-permute-start.13 = (bf16[1,512,256]{2,1,0:T(8,128)(2,1)S(1)}, bf16[1,512,256]{2,1,0:T(8,128)(2,1)}, u32[]{:S(2)}, u32[]{:S(2)}) collective-permute-start(bf16[1,512,256]{2,1,0:T(8,128)(2,1)S(1)} %get-tuple-element.104.refs_0_), channel_id=1, source_target_pairs={{0,1},{1,0},{2,3},{3,2},{4,5},{5,4},{6,7},{7,6},{8,9},{9,8},{10,11... | collective-permute-start | bytes 786440 | tf_op jit(solution)/shard_map/ppermute | solution.py:61
  49.3 8.4 %collective-permute-start.15 = (bf16[2,512,256]{2,1,0:T(8,128)(2,1)}, bf16[2,512,256]{2,1,0:T(8,128)(2,1)}, u32[]{:S(2)}, u32[]{:S(2)}) collective-permute-start(bf16[2,512,256]{2,1,0:T(8,128)(2,1)} %copy-done), channel_id=1, source_target_pairs={{0,1},{1,0},{2,3},{3,2},{4,5},{5,4},{6,7},{7,6},{8,9},{9,8},{10,11... | collective-permute-start | bytes 1572872 | tf_op jit(solution)/shard_map/ppermute | solution.py:61
  51.0 6.7 %collective-permute-start.16 = (bf16[2,512,256]{2,1,0:T(8,128)(2,1)}, bf16[2,512,256]{2,1,0:T(8,128)(2,1)}, u32[]{:S(2)}, u32[]{:S(2)}) collective-permute-start(bf16[2,512,256]{2,1,0:T(8,128)(2,1)} %collective-permute-done.5.refs_6_), channel_id=1, source_target_pairs={{0,1},{1,0},{2,3},{3,2},{4,5},{5,4},{6,7},{7,6},{8,9},{9,8},{10,11... | collective-permute-start | bytes 1572872 | tf_op jit(solution)/shard_map/ppermute | solution.py:61
  51.0 5.2 %collective-permute-start.14 = (bf16[1,512,256]{2,1,0:T(8,128)(2,1)}, bf16[1,512,256]{2,1,0:T(8,128)(2,1)}, u32[]{:S(2)}, u32[]{:S(2)}) collective-permute-start(bf16[1,512,256]{2,1,0:T(8,128)(2,1)} %collective-permute-done.2.refs_2_), channel_id=1, source_target_pairs={{0,1},{1,0},{2,3},{3,2},{4,5},{5,4},{6,7},{7,6},{8,9},{9,8},{10,11... | collective-permute-start | bytes 786440 | tf_op jit(solution)/shard_map/ppermute | solution.py:61
  51.6 6.2 %copy-start.1 = (bf16[2,512,256]{2,1,0:T(8,128)(2,1)S(1)}, bf16[2,512,256]{2,1,0:T(8,128)(2,1)}, u32[]{:S(2)}) copy-start(bf16[2,512,256]{2,1,0:T(8,128)(2,1)} %copy-done) | copy-start | bytes 1572868
  55.6 2.1 %collective-permute-start.17 = (bf16[1,512,256]{2,1,0:T(8,128)(2,1)}, bf16[1,512,256]{2,1,0:T(8,128)(2,1)S(1)}, u32[]{:S(2)}, u32[]{:S(2)}) collective-permute-start(bf16[1,512,256]{2,1,0:T(8,128)(2,1)} %collective-permute-done.4.refs_8_), channel_id=1, source_target_pairs={{0,1},{1,0},{2,3},{3,2},{4,5},{5,4},{6,7},{7,6},{8,9},{9,8},{10,11... | collective-permute-start | bytes 786440 | tf_op jit(solution)/shard_map/ppermute | solution.py:61
  56.0 1.8 %collective-permute-start.18 = (bf16[1,512,256]{2,1,0:T(8,128)(2,1)}, bf16[1,512,256]{2,1,0:T(8,128)(2,1)S(1)}, u32[]{:S(2)}, u32[]{:S(2)}) collective-permute-start(bf16[1,512,256]{2,1,0:T(8,128)(2,1)} %collective-permute-done.8.refs_10_), channel_id=1, source_target_pairs={{0,1},{1,0},{2,3},{3,2},{4,5},{5,4},{6,7},{7,6},{8,9},{9,8},{10,11... | collective-permute-start | bytes 786440 | tf_op jit(solution)/shard_map/ppermute | solution.py:61
  56.2 26.8 %collective-permute-start.22 = (bf16[128,4096]{1,0:T(8,128)(2,1)S(1)}, bf16[128,4096]{1,0:T(8,128)(2,1)S(1)}, u32[]{:S(2)}, u32[]{:S(2)}) collective-permute-start(bf16[128,4096]{1,0:T(8,128)(2,1)S(1)} %fusion.4.h0), channel_id=1, source_target_pairs={{0,18},{1,19},{2,16},{3,17},{4,22},{5,23},{6,20},{7,21},{8,26},{9,... | collective-permute-start | bytes 3145736 | tf_op jit(solution)/shard_map/ppermute | solution.py:61
  57.8 29.4 %copy-start.7 = (bf16[64,4096]{1,0:T(8,128)(2,1)S(1)}, bf16[64,4096]{1,0:T(8,128)(2,1)}, u32[]{:S(2)}) copy-start(bf16[64,4096]{1,0:T(8,128)(2,1)} %get-tuple-element.78) | copy-start | bytes 1572868
  67.0 13.6 %collective-permute-start.19 = (bf16[2,512,256]{2,1,0:T(8,128)(2,1)S(1)}, bf16[2,512,256]{2,1,0:T(8,128)(2,1)S(1)}, u32[]{:S(2)}, u32[]{:S(2)}) collective-permute-start(bf16[2,512,256]{2,1,0:T(8,128)(2,1)S(1)} %get-tuple-element.68), channel_id=1, source_target_pairs={{0,16},{1,17},{2,18},{3,19},{4,20},{5,21},{6,22},{7,23},{8,24},{9,... | collective-permute-start | bytes 1572872 | tf_op jit(solution)/shard_map/ppermute | solution.py:61
  68.7 14.3 %collective-permute-start.20 = (bf16[2,512,256]{2,1,0:T(8,128)(2,1)S(1)}, bf16[2,512,256]{2,1,0:T(8,128)(2,1)S(1)}, u32[]{:S(2)}, u32[]{:S(2)}) collective-permute-start(bf16[2,512,256]{2,1,0:T(8,128)(2,1)S(1)} %get-tuple-element.69.refs_9_), channel_id=1, source_target_pairs={{0,4},{1,5},{2,6},{3,7},{4,8},{5,9},{6,10},{7,11},{8,12},{9,13},{1... | collective-permute-start | bytes 1572872 | tf_op jit(solution)/shard_map/ppermute | solution.py:61
  68.9 14.0 %collective-permute-start.21 = (bf16[2,512,256]{2,1,0:T(8,128)(2,1)S(1)}, bf16[2,512,256]{2,1,0:T(8,128)(2,1)S(1)}, u32[]{:S(2)}, u32[]{:S(2)}) collective-permute-start(bf16[2,512,256]{2,1,0:T(8,128)(2,1)S(1)} %get-tuple-element.69.refs_9_), channel_id=1, source_target_pairs={{0,12},{1,13},{2,14},{3,15},{4,0},{5,1},{6,2},{7,3},{8,4},{9,5},{1... | collective-permute-start | bytes 1572872 | tf_op jit(solution)/shard_map/ppermute | solution.py:61
  83.0 5.3 %collective-permute-start.25 = (bf16[128,4096]{1,0:T(8,128)(2,1)S(1)}, bf16[128,4096]{1,0:T(8,128)(2,1)S(1)}, u32[]{:S(2)}, u32[]{:S(2)}) collective-permute-start(bf16[128,4096]{1,0:T(8,128)(2,1)S(1)} %collective-permute-done.22.h0), channel_id=1, source_target_pairs={{0,1},{1,0},{2,3},{3,2},{4,5},{5,4},{6,7},{7,6},{8,9},{9,8},{10,11... | collective-permute-start | bytes 3145736 | tf_op jit(solution)/shard_map/ppermute | solution.py:61
  84.2 14.7 %collective-permute-start.23 = (bf16[2,512,256]{2,1,0:T(8,128)(2,1)S(1)}, bf16[2,512,256]{2,1,0:T(8,128)(2,1)S(1)}, u32[]{:S(2)}, u32[]{:S(2)}) collective-permute-start(bf16[2,512,256]{2,1,0:T(8,128)(2,1)S(1)} %collective-permute-done.19.refs_12_), channel_id=1, source_target_pairs={{0,4},{1,5},{2,6},{3,7},{4,8},{5,9},{6,10},{7,11},{8,12},{9,13},{1... | collective-permute-start | bytes 1572872 | tf_op jit(solution)/shard_map/ppermute | solution.py:61
  84.8 14.1 %collective-permute-start.24 = (bf16[2,512,256]{2,1,0:T(8,128)(2,1)S(1)}, bf16[2,512,256]{2,1,0:T(8,128)(2,1)S(1)}, u32[]{:S(2)}, u32[]{:S(2)}) collective-permute-start(bf16[2,512,256]{2,1,0:T(8,128)(2,1)S(1)} %collective-permute-done.19.refs_12_), channel_id=1, source_target_pairs={{0,12},{1,13},{2,14},{3,15},{4,0},{5,1},{6,2},{7,3},{8,4},{9,5},{1... | collective-permute-start | bytes 1572872 | tf_op jit(solution)/shard_map/ppermute | solution.py:61
  86.9 12.8 %collective-permute-start.26 = (bf16[64,4096]{1,0:T(8,128)(2,1)S(1)}, bf16[64,4096]{1,0:T(8,128)(2,1)S(1)}, u32[]{:S(2)}, u32[]{:S(2)}) collective-permute-start(bf16[64,4096]{1,0:T(8,128)(2,1)S(1)} %collective-permute-done.3.refs_0_), channel_id=1, source_target_pairs={{0,16},{1,17},{2,18},{3,19},{4,20},{5,21},{6,22},{7,23},{8,24},{9,... | collective-permute-start | bytes 1572872 | tf_op jit(solution)/shard_map/ppermute | solution.py:61
  87.2 13.7 %collective-permute-start.27 = (bf16[64,4096]{1,0:T(8,128)(2,1)S(1)}, bf16[64,4096]{1,0:T(8,128)(2,1)S(1)}, u32[]{:S(2)}, u32[]{:S(2)}) collective-permute-start(bf16[64,4096]{1,0:T(8,128)(2,1)S(1)} %copy-done.7), channel_id=1, source_target_pairs={{0,18},{1,19},{2,16},{3,17},{4,22},{5,23},{6,20},{7,21},{8,26},{9,... | collective-permute-start | bytes 1572872 | tf_op jit(solution)/shard_map/ppermute | solution.py:61
  91.5 15.4 %copy-start.6 = (bf16[64,4096]{1,0:T(8,128)(2,1)S(1)}, bf16[64,4096]{1,0:T(8,128)(2,1)}, u32[]{:S(2)}) copy-start(bf16[64,4096]{1,0:T(8,128)(2,1)} %get-tuple-element.98) | copy-start | bytes 1572868
  91.5 23.8 %copy-start.2 = (s32[1,4096]{1,0:T(1,128)S(1)}, s32[1,4096]{1,0:T(1,128)}, u32[]{:S(2)}) copy-start(s32[1,4096]{1,0:T(1,128)} %refs_2_.1) | copy-start | bytes 49156
  101.0 11.7 %collective-permute-start.31 = (bf16[1024,256]{1,0:T(8,128)(2,1)S(1)}, bf16[1024,256]{1,0:T(8,128)(2,1)S(1)}, u32[]{:S(2)}, u32[]{:S(2)}) collective-permute-start(bf16[1024,256]{1,0:T(8,128)(2,1)S(1)} %pad_maximum_fusion.1), channel_id=1, source_target_pairs={{0,12},{1,13},{2,14},{3,15},{4,0},{5,1},{6,2},{7,3},{8,4},{9,5},{1... | collective-permute-start | bytes 1572872 | tf_op jit(solution)/shard_map/ppermute | solution.py:61
  102.7 12.7 %collective-permute-start.30 = (bf16[1024,256]{1,0:T(8,128)(2,1)S(1)}, bf16[1024,256]{1,0:T(8,128)(2,1)S(1)}, u32[]{:S(2)}, u32[]{:S(2)}) collective-permute-start(bf16[1024,256]{1,0:T(8,128)(2,1)S(1)} %pad_maximum_fusion), channel_id=1, source_target_pairs={{0,4},{1,5},{2,6},{3,7},{4,8},{5,9},{6,10},{7,11},{8,12},{9,13},{1... | collective-permute-start | bytes 1572872 | tf_op jit(solution)/shard_map/ppermute | solution.py:61
  102.7 4.2 %collective-permute-start.29 = (bf16[256,256]{1,0:T(8,128)(2,1)S(1)}, bf16[256,256]{1,0:T(8,128)(2,1)S(1)}, u32[]{:S(2)}, u32[]{:S(2)}) collective-permute-start(bf16[256,256]{1,0:T(8,128)(2,1)S(1)} %get-tuple-element.82), channel_id=1, source_target_pairs={{0,16},{1,17},{2,18},{3,19},{4,20},{5,21},{6,22},{7,23},{8,24},{9,... | collective-permute-start | bytes 393224 | tf_op jit(solution)/shard_map/ppermute | solution.py:61
  102.8 5.6 %collective-permute-start.28 = (bf16[256,256]{1,0:T(8,128)(2,1)S(1)}, bf16[256,256]{1,0:T(8,128)(2,1)S(1)}, u32[]{:S(2)}, u32[]{:S(2)}) collective-permute-start(bf16[256,256]{1,0:T(8,128)(2,1)S(1)} %get-tuple-element.81), channel_id=1, source_target_pairs={{0,16},{1,17},{2,18},{3,19},{4,20},{5,21},{6,22},{7,23},{8,24},{9,... | collective-permute-start | bytes 393224 | tf_op jit(solution)/shard_map/ppermute | solution.py:61
  104.3 27.6 %collective-permute-start.35 = (bf16[64,4096]{1,0:T(8,128)(2,1)S(1)}, bf16[64,4096]{1,0:T(8,128)(2,1)S(1)}, u32[]{:S(2)}, u32[]{:S(2)}) collective-permute-start(bf16[64,4096]{1,0:T(8,128)(2,1)S(1)} %collective-permute-done.6.refs_1_), channel_id=1, source_target_pairs={{0,16},{1,17},{2,18},{3,19},{4,20},{5,21},{6,22},{7,23},{8,24},{9,... | collective-permute-start | bytes 1572872 | tf_op jit(solution)/shard_map/ppermute | solution.py:61
  106.9 25.0 %collective-permute-start.36 = (bf16[64,4096]{1,0:T(8,128)(2,1)S(1)}, bf16[64,4096]{1,0:T(8,128)(2,1)S(1)}, u32[]{:S(2)}, u32[]{:S(2)}) collective-permute-start(bf16[64,4096]{1,0:T(8,128)(2,1)S(1)} %copy-done.6), channel_id=1, source_target_pairs={{0,18},{1,19},{2,16},{3,17},{4,22},{5,23},{6,20},{7,21},{8,26},{9,... | collective-permute-start | bytes 1572872 | tf_op jit(solution)/shard_map/ppermute | solution.py:61
  128.6 5.4 %collective-permute-start.32 = (bf16[256,256]{1,0:T(8,128)(2,1)S(1)}, bf16[256,256]{1,0:T(8,128)(2,1)S(1)}, u32[]{:S(2)}, u32[]{:S(2)}) collective-permute-start(bf16[256,256]{1,0:T(8,128)(2,1)S(1)} %get-tuple-element.89), channel_id=1, source_target_pairs={{0,2},{1,3},{2,0},{3,1},{4,6},{5,7},{6,4},{7,5},{8,10},{9,11},{10,... | collective-permute-start | bytes 393224 | tf_op jit(solution)/shard_map/ppermute | solution.py:61
  129.2 4.9 %collective-permute-start.33 = (bf16[256,256]{1,0:T(8,128)(2,1)S(1)}, bf16[256,256]{1,0:T(8,128)(2,1)S(1)}, u32[]{:S(2)}, u32[]{:S(2)}) collective-permute-start(bf16[256,256]{1,0:T(8,128)(2,1)S(1)} %get-tuple-element.90), channel_id=1, source_target_pairs={{0,16},{1,17},{2,18},{3,19},{4,20},{5,21},{6,22},{7,23},{8,24},{9,... | collective-permute-start | bytes 393224 | tf_op jit(solution)/shard_map/ppermute | solution.py:61
  130.3 5.1 %collective-permute-start.34 = (bf16[256,256]{1,0:T(8,128)(2,1)S(1)}, bf16[256,256]{1,0:T(8,128)(2,1)S(1)}, u32[]{:S(2)}, u32[]{:S(2)}) collective-permute-start(bf16[256,256]{1,0:T(8,128)(2,1)S(1)} %get-tuple-element.91), channel_id=1, source_target_pairs={{0,18},{1,19},{2,16},{3,17},{4,22},{5,23},{6,20},{7,21},{8,26},{9,... | collective-permute-start | bytes 393224 | tf_op jit(solution)/shard_map/ppermute | solution.py:61
  139.2 8.6 %collective-permute-start.37 = (bf16[128,2048]{1,0:T(8,128)(2,1)S(1)}, bf16[128,2048]{1,0:T(8,128)(2,1)S(1)}, u32[]{:S(2)}, u32[]{:S(2)}) collective-permute-start(bf16[128,2048]{1,0:T(8,128)(2,1)S(1)} %slice.41), channel_id=1, source_target_pairs={{0,1},{1,0},{2,3},{3,2},{4,5},{5,4},{6,7},{7,6},{8,9},{9,8},{10,11... | collective-permute-start | bytes 1572872 | tf_op jit(solution)/shard_map/ppermute | solution.py:61
  147.6 2.1 %copy-start.5 = (bf16[1,128,4096]{2,1,0:T(8,128)(2,1)S(1)}, bf16[1,128,4096]{2,1,0:T(8,128)(2,1)}, u32[]{:S(2)}) copy-start(bf16[1,128,4096]{2,1,0:T(8,128)(2,1)} %param.9) | copy-start | bytes 3145732
  147.7 2.0 %collective-permute-start.38 = (bf16[128,2048]{1,0:T(8,128)(2,1)S(1)}, bf16[128,2048]{1,0:T(8,128)(2,1)S(1)}, u32[]{:S(2)}, u32[]{:S(2)}) collective-permute-start(bf16[128,2048]{1,0:T(8,128)(2,1)S(1)} %slice.43), channel_id=1, source_target_pairs={{0,1},{1,0},{2,3},{3,2},{4,5},{5,4},{6,7},{7,6},{8,9},{9,8},{10,11... | collective-permute-start | bytes 1572872 | tf_op jit(solution)/shard_map/ppermute | solution.py:61

commit v4 on v3

--- a/solution.py
+++ b/solution.py
@@ -97,69 +97,102 @@
     return (pl.ds(at * 1024, 1024),)
 
 
-def key_value_kernel(place, *refs):
-    blocks, (w_key, w_value, mine, other, panel, keys, values, sums, arrived) = refs[:12], refs[12:]
-    wait_key = fetch(w_key, keys, arrived.at[0], 4, row_piece)
-    wait_value = fetch(w_value, values, arrived.at[1], 4, row_piece)
-    for at, block in enumerate(blocks):
-        group, flip = divmod(at, 4)
-        for lead, step in enumerate(X_GROUPS[group]):
-            column = place[3 + step] * 1024 + jnp.bitwise_xor(place[2], flip) * 256
-            panel[:, pl.ds(pl.multiple_of(column, 256), 256)] = block[lead]
-    for step in range(4):
-        block = panel[:, step * 1024 : (step + 1) * 1024]
-        for at, (wait, held) in enumerate(((wait_key, keys), (wait_value, values))):
-            wait(step)
-            product = dot(block, held[step * 1024 : (step + 1) * 1024])
-            if step == 0:
-                sums[at] = product
-            else:
-                sums[at] += product
-    for out, side in ((mine, place[1]), (other, 1 - place[1])):
-        for at in range(2):
-            out[at] = sums[at, :, pl.ds(pl.multiple_of(side * HD, HD), HD)].astype(BF16)
+def key_value_kernel(steps, place, *refs):
+    count = 4 * len(set(group for group, _, _ in steps))
+    blocks, refs = refs[:count], refs[count:]
+    w_key, w_value, refs = refs[0], refs[1], refs[2:]
+    sums, refs = (None, refs) if steps[0][2] == 0 else (refs[0], refs[1:])
+    keys, values, arrived = refs[-3:]
+    copies = []
+    for at, (_, _, step) in enumerate(steps):
+        for flip in range(4):
+            row = place[3 + step] * 1024 + jnp.bitwise_xor(place[2], flip) * 256
+            source = pl.ds(pl.multiple_of(row, 256), 256)
+            target = pl.ds(at * 1024 + flip * 256, 256)
+            for which, (weight, held) in enumerate(((w_key, keys), (w_value, values))):
+                copies.append(
+                    pltpu.make_async_copy(
+                        weight.at[source], held.at[target], arrived.at[which, at * 4 + flip]
+                    )
+                )
+    for copy in copies:
+        copy.start()
+    if sums is None:
+        total = refs[0]
+    else:
+        mine, other, total = refs[:3]
+        total[...] = sums[...]
+    first = min(group for group, _, _ in steps)
+    for at, (group, lead, step) in enumerate(steps):
+        panel = jnp.concatenate(
+            [blocks[(group - first) * 4 + flip][lead] for flip in range(4)], axis=1
+        )
+        for copy in copies[at * 8 : at * 8 + 8]:
+            copy.wait()
+        for which, held in enumerate((keys, values)):
+            for side in range(2):
+                columns = slice(side * HD, (side + 1) * HD)
+                product = dot(panel, held[at * 1024 : (at + 1) * 1024, columns])
+                if step == 0:
+                    total[which, :, columns] = product
+                else:
+                    total[which, :, columns] += product
+    if sums is not None:
+        for side in range(2):
+
+            @pl.when(place[1] == side)
+            def _():
+                mine[...] = total[:, :, side * HD : (side + 1) * HD].astype(BF16)
+                other[...] = total[:, :, (1 - side) * HD : (2 - side) * HD].astype(BF16)
 
 
 def hbm(count):
     return [pl.BlockSpec(memory_space=pltpu.HBM)] * count
 
 
-def key_values(place, blocks, w_key, w_value):
+def key_values(place, blocks, w_key, w_value, steps, sums=()):
     rows = blocks[0].shape[1]
+    total = (2, rows, 512)
     out = jax.ShapeDtypeStruct((2, rows, HD), BF16)
+    depth = 1024 * len(steps)
     return pl.pallas_call(
-        key_value_kernel,
-        out_shape=(out, out),
-        in_specs=smem(1) + vmem(12) + hbm(2),
-        out_specs=tuple(vmem(2)),
-        scratch_shapes=[
-            pltpu.VMEM((rows, 4096), BF16),
-            pltpu.VMEM((4096, 512), BF16),
-            pltpu.VMEM((4096, 512), BF16),
-            pltpu.VMEM((2, rows, 512), F32),
-            pltpu.SemaphoreType.DMA((2, 4)),
+        functools.partial(key_value_kernel, steps),
+        out_shape=(out, out) if sums else jax.ShapeDtypeStruct(total, F32),
+        in_specs=smem(1) + vmem(len(blocks)) + hbm(2) + vmem(len(sums)),
+        out_specs=tuple(vmem(2)) if sums else vmem(1)[0],
+        scratch_shapes=([pltpu.VMEM(total, F32)] if sums else [])
+        + [
+            pltpu.VMEM((depth, 512), BF16),
+            pltpu.VMEM((depth, 512), BF16),
+            pltpu.SemaphoreType.DMA((2, 4 * len(steps))),
         ],
         compiler_params=params(48),
         cost_estimate=pl.CostEstimate(
-            flops=2 * rows * 4096 * 1024, bytes_accessed=8 * MIB + rows * 8192, transcendentals=0
+            flops=2 * rows * depth * 1024, bytes_accessed=depth * 3072, transcendentals=0
         ),
         name="key_values",
-    )(place, *blocks, w_key, w_value)
+    )(place, *blocks, w_key, w_value, *sums)
 
 
 def query_kernel(place, h0, h1, w_query, mine, other, weight, sums, arrived):
     wait = fetch(w_query, weight, arrived, 4, row_piece)
-    rows = h0.shape[0]
     for step in range(4):
         span = slice(step * 1024, (step + 1) * 1024)
+        rows = jnp.concatenate([h0[:, span], h1[:, span]])
         wait(step)
-        product = dot(jnp.concatenate([h0[:, span], h1[:, span]]), weight[span])
-        if step == 0:
-            sums[...] = product
-        else:
-            sums[...] += product
-    for out, side in ((mine, place[1]), (other, 1 - place[1])):
-        out[...] = sums[:, pl.ds(pl.multiple_of(side * HD, HD), HD)].astype(BF16)
+        for side in range(2):
+            columns = slice(side * HD, (side + 1) * HD)
+            product = dot(rows, weight[span, columns])
+            if step == 0:
+                sums[:, columns] = product
+            else:
+                sums[:, columns] += product
+    for side in range(2):
+
+        @pl.when(place[1] == side)
+        def _():
+            mine[...] = sums[:, side * HD : (side + 1) * HD].astype(BF16)
+            other[...] = sums[:, (1 - side) * HD : (2 - side) * HD].astype(BF16)
 
 
 def queries(place, blocks, w_query):
@@ -361,40 +394,48 @@
     def rows_for_cut(head, turn):
         return lax.dynamic_slice(w_own, (head * HD + (z + turn) % 4 * 64, 0), (64, 4096))
 
-    piece = send(rows_for_cut(1 - low, 0), Y_CUT)
+    first, encoder_panel = lax.optimization_barrier((rows_for_cut(1 - low, 0), encoder_panel))
+    piece = send(first, Y_CUT)
     own = panel_of(0, 0, 512)
     up, down = send(panel_of(1, 0, 512), X_UP), send(panel_of(3, 0, 512), X_DOWN)
+    two = send(panel_of(2, 0, 512), X_TWO)
     local_rows = decoder_rows[0]
     hidden = normed_rows(local_rows, norm_gain[0])
-    up, down, own_far, two, hidden, piece, w_own = lax.optimization_barrier(
-        (up, down, send(own, Y_FAR), panel_of(2, 0, 512), hidden, piece, w_own)
-    )
-    pair = jnp.concatenate([up, down])
-    two, pair_far, piece_below, piece_above, cut_1, cut_2 = lax.optimization_barrier(
-        (
-            send(two, X_TWO),
-            send(pair, Y_FAR),
-            send(piece, Z_UP),
-            send(piece, Z_DOWN),
-            rows_for_cut(low, 1),
-            rows_for_cut(low, 2),
-        )
-    )
+    up, down, two, own_far, hidden, piece, w_own = lax.optimization_barrier(
+        (up, down, two, send(own, Y_FAR), hidden, piece, w_own)
+    )
+    rest = jnp.concatenate([up, down, two])
+    piece_below, piece_above = send(piece, Z_UP), send(piece, Z_DOWN)
+
     near_mine, near_other = queries(place, (hidden, send(hidden, CORE)), w_query[0])
+    blocks = [own, send(own, CORE), own_far, send(own_far, CORE)]
+    sums = key_values(place, blocks, w_key[0], w_value[0], ((0, 0, 0),))
+    piece_below, piece_above, near_mine, near_other = lax.optimization_barrier(
+        (piece_below, piece_above, near_mine, near_other)
+    )
     far_rows = [piece, piece_below, piece_above]
     far_rows += [send(piece_below[:32], Z_UP), send(piece_above[32:], Z_DOWN)]
-    two_far, ids_low, near_mine, near_other, *far_rows = lax.optimization_barrier(
-        (send(two, Y_FAR), send(ids_own, Y_LOW), near_mine, near_other, *far_rows)
-    )
-    panels, fars = [own, pair, two], [own_far, pair_far, two_far]
-
-
-    blocks = []
-    for near, far in zip(panels, fars):
-        blocks += [near, send(near, CORE), far, send(far, CORE)]
-    mine, other = key_values(place, blocks, w_key[0], w_value[0])
-
-    hidden, _ = lax.optimization_barrier((hidden, two_far))
+    cut_1, cut_2 = rows_for_cut(low, 1), rows_for_cut(low, 2)
+    rest_far, ids_low, sums, near_mine, near_other, cut_1, cut_2, *far_rows = (
+        lax.optimization_barrier(
+            (
+                send(rest, Y_FAR),
+                send(ids_own, Y_LOW),
+                sums,
+                near_mine,
+                near_other,
+                cut_1,
+                cut_2,
+                *far_rows,
+            )
+        )
+    )
+
+    blocks = [rest, send(rest, CORE), rest_far, send(rest_far, CORE)]
+    steps = ((1, 0, 1), (1, 1, 2), (1, 2, 3))
+    mine, other = key_values(place, blocks, w_key[0], w_value[0], steps, (sums,))
+
+    hidden, _ = lax.optimization_barrier((hidden, rest_far))
     hidden_cut = send(hidden, Y_CUT)
     below_0, above_0 = send(mine, Z_UP), send(mine, Z_DOWN)
     theirs, below_0, above_0, hidden_cut, piece, cut_1 = lax.optimization_barrier(

time: 149 us -> 143 us (0.960); the launches traced: 151 us -> 143 us
  starting transfers between devices: 50.1 us -> 45.4 us
  waiting for transfers between devices: 55.6 us -> 53.2 us
  Pallas kernels: 37.1 us -> 35.5 us
    ppermute x39 -> x36, starting transfers between devices: 50.1 us -> 45.4 us  [send(): return lax.ppermute(array, AXES, pairs)]
    pallas_call x1, Pallas kernels: 13.2 us -> 9.38 us  [attend(): pl.pallas_call(functools.partial(attend_kernel, pieces, keys), out_shape=...]
    ppermute x39 -> x36, waiting for transfers between devices: 55.6 us -> 53.2 us  [send(): return lax.ppermute(array, AXES, pairs)]
    pallas_call x1 -> x2, Pallas kernels: 9.18 us -> 11.2 us  [key_values(): pl.pallas_call(functools.partial(key_value_kernel, steps), out_shape=(out...]
  transfers between devices with their start and end apart: 39 -> 36, of which waited for: 21 -> 17; matrix products, arithmetic and copies ran while one was open for 4% -> 3% of each run, Pallas kernels for 22% -> 22%
where the time goes in v4:
time: 143 us
  waiting for transfers between devices  53.2 us (37%)
  starting transfers between devices  45.4 us (32%)
  Pallas kernels  35.5 us (25%)
  local copies, waits for them, and re-layouts  6.08 us (4%)
  other arithmetic  2.13 us (1%)
    ppermute x36, waiting for transfers between devices, send(): return lax.ppermute(array, AXES, pairs)  53.2 us
    ppermute x36, starting transfers between devices, send(): return lax.ppermute(array, AXES, pairs)  45.4 us
    pallas_call x2, Pallas kernels, key_values(): pl.pallas_call(functools.partial(key_value_kernel, steps), out_shape=(out...  11.2 us
    pallas_call x1, Pallas kernels, attend(): pl.pallas_call(functools.partial(attend_kernel, pieces, keys), out_shape=...  9.38 us
    pallas_call x2, Pallas kernels, outputs(): pl.pallas_call(functools.partial(output_kernel, part * width), out_shape=...  7.5 us
    pallas_call x2, Pallas kernels, queries(): pl.pallas_call(query_kernel, out_shape=(out, out), in_specs=smem(1) + vme...  7.35 us
  transfers between devices with their start and end apart: 36, of which 17 were waited for; matrix products, arithmetic and copies ran while one was open for 3% of the time, Pallas kernels for 22%

profile of v4, /device:TPU:1, one launch (start us, length us, event | category | flops | bytes accessed | tf_op | source)
XLA Modules:
  0.0 142.7 jit_solution(16327460141347694140)
XLA Ops:
  0.0 1.2 dynamic-slice_bitcast_fusion
  1.2 3.6 %collective-permute-start.4 = (bf16[64,4096]{1,0:T(8,128)(2,1)S(1)}, bf16[64,4096]{1,0:T(8,128)(2,1)S(1)}, u32[]{:S(2)}, u32[]{:S(2)}) collective-permute-start(bf16[64,4096]{1,0:T(8,128)(2,1)S(1)} %dynamic-slice_bitcast_fusion), channel_id=1, source_target_pairs={{0,18},{1,19},{2,16},{3,17},{4,22},{5,23},{6,20},{7,21},{8,26},{9,... | collective-permute-start | bytes 1572872 | tf_op jit(solution)/shard_map/ppermute | solution.py:61
  4.8 2.0 %constant_dynamic-slice_fusion.2 = (bf16[1,512,256]{2,1,0:T(8,128)(2,1)}, bf16[1,512,256]{2,1,0:T(8,128)(2,1)S(1)}, bf16[1,512,256]{2,1,0:T(8,128)(2,1)S(1)}, bf16[1,512,256]{2,1,0:T(8,128)(2,1)S(1)}) fusion(bf16[4,512,256]{2,1,0:T(8,128)(2,1)} %param.10, s32[]{:T(128)S(6)} %select_n.82, s32[]{:T(128)S(6)} %select_n.81, s32[]{:T(128)S(6)} %select_n.80, ...), kind=kLoop, calls=%fused_computation.22 | loop fusion | bytes 2097168 | tf_op jit(solution)/shard_map/dynamic_slice | solution.py:388
  6.8 2.7 %collective-permute-start.2 = (bf16[1,512,256]{2,1,0:T(8,128)(2,1)S(1)}, bf16[1,512,256]{2,1,0:T(8,128)(2,1)S(1)}, u32[]{:S(2)}, u32[]{:S(2)}) collective-permute-start(bf16[1,512,256]{2,1,0:T(8,128)(2,1)S(1)} %get-tuple-element.108), channel_id=1, source_target_pairs={{0,64},{1,65},{2,66},{3,67},{4,68},{5,69},{6,70},{7,71},{8,72},{9,... | collective-permute-start | bytes 786440 | tf_op jit(solution)/shard_map/ppermute | solution.py:61
  9.5 0.9 collective-permute-start.1
  12.0 3.1 %collective-permute-done.2 = bf16[1,512,256]{2,1,0:T(8,128)(2,1)S(1)} collective-permute-done((bf16[1,512,256]{2,1,0:T(8,128)(2,1)S(1)}, bf16[1,512,256]{2,1,0:T(8,128)(2,1)S(1)}, u32[]{:S(2)}, u32[]{:S(2)}) %collective-permute-start.2) | collective-permute-done | bytes 262176 | tf_op jit(solution)/shard_map/ppermute | solution.py:61
  15.1 6.1 %collective-permute-done.1 = bf16[1,512,256]{2,1,0:T(8,128)(2,1)S(1)} collective-permute-done((bf16[1,512,256]{2,1,0:T(8,128)(2,1)S(1)}, bf16[1,512,256]{2,1,0:T(8,128)(2,1)S(1)}, u32[]{:S(2)}, u32[]{:S(2)}) %collective-permute-start.1) | collective-permute-done | bytes 262176 | tf_op jit(solution)/shard_map/ppermute | solution.py:61
  21.9 1.4 collective-permute-start.11
  23.3 3.8 %collective-permute-start.10 = (bf16[64,4096]{1,0:T(8,128)(2,1)S(1)}, bf16[64,4096]{1,0:T(8,128)(2,1)S(1)}, u32[]{:S(2)}, u32[]{:S(2)}) collective-permute-start(bf16[64,4096]{1,0:T(8,128)(2,1)S(1)} %collective-permute-done.4.refs_0_), channel_id=1, source_target_pairs={{0,12},{1,13},{2,14},{3,15},{4,0},{5,1},{6,2},{7,3},{8,4},{9,5},{1... | collective-permute-start | bytes 1572872 | tf_op jit(solution)/shard_map/ppermute | solution.py:61
  27.2 1.7 %collective-permute-start.5 = (bf16[3,512,256]{2,1,0:T(8,128)(2,1)S(1)}, bf16[3,512,256]{2,1,0:T(8,128)(2,1)}, u32[]{:S(2)}, u32[]{:S(2)}) collective-permute-start(bf16[3,512,256]{2,1,0:T(8,128)(2,1)S(1)} %constant_dynamic-update-slice_fusion.refs_0_), channel_id=1, source_target_pairs={{0,2},{1,3},{2,0},{3,1},{4,6},{5,7},{6,4},{7,5},{8,10},{9,11},{10,... | collective-permute-start | bytes 2359304 | tf_op jit(solution)/shard_map/ppermute | solution.py:61
  29.6 4.0 %queries.2 = (bf16[256,256]{1,0:T(8,128)(2,1)S(1)}, bf16[256,256]{1,0:T(8,128)(2,1)S(1)}) custom-call(s32[8]{0:T(128)S(1)} %stack.35.place, bf16[128,4096]{1,0:T(8,128)(2,1)S(1)} %fusion.4.h0, bf16[128,4096]{1,0:T(8,128)(2,1)} %collective-permute-done.11.h1, bf16[4096,512]{1,0:T(8,128)(2,1)} %bitcast.46), custom_call_target="tpu_custom_call" | custom-call | flops 1073741824 | bytes 8388608 | tf_op jit(solution)/shard_map/queries/pallas_call | solution.py:201
  33.7 4.7 %collective-permute-done.10.refs_2_ = bf16[64,4096]{1,0:T(8,128)(2,1)S(1)} collective-permute-done((bf16[64,4096]{1,0:T(8,128)(2,1)S(1)}, bf16[64,4096]{1,0:T(8,128)(2,1)S(1)}, u32[]{:S(2)}, u32[]{:S(2)}) %collective-permute-start.10) | collective-permute-done | bytes 524320 | tf_op jit(solution)/shard_map/ppermute | solution.py:61
  38.4 3.2 %collective-permute-done.9.refs_1_ = bf16[64,4096]{1,0:T(8,128)(2,1)S(1)} collective-permute-done((bf16[64,4096]{1,0:T(8,128)(2,1)S(1)}, bf16[64,4096]{1,0:T(8,128)(2,1)S(1)}, u32[]{:S(2)}, u32[]{:S(2)}) %collective-permute-start.9) | collective-permute-done | bytes 524320 | tf_op jit(solution)/shard_map/ppermute | solution.py:61
  42.1 1.1 collective-permute-start.12
  43.2 1.3 constant_dynamic-slice_fusion
  44.6 1.8 %collective-permute-start.14 = (bf16[3,512,256]{2,1,0:T(8,128)(2,1)S(1)}, bf16[3,512,256]{2,1,0:T(8,128)(2,1)S(1)}, u32[]{:S(2)}, u32[]{:S(2)}) collective-permute-start(bf16[3,512,256]{2,1,0:T(8,128)(2,1)S(1)} %constant_dynamic-update-slice_fusion.refs_0_), channel_id=1, source_target_pairs={{0,1},{1,0},{2,3},{3,2},{4,5},{5,4},{6,7},{7,6},{8,9},{9,8},{10,11... | collective-permute-start | bytes 2359304 | tf_op jit(solution)/shard_map/ppermute | solution.py:61
  46.4 3.9 %key_values.2.refs_6_ = f32[2,512,512]{2,1,0:T(8,128)S(1)} custom-call(s32[8]{0:T(128)S(1)} %stack.35.place, bf16[1,512,256]{2,1,0:T(8,128)(2,1)} %get-tuple-element.107.refs_0_, bf16[1,512,256]{2,1,0:T(8,128)(2,1)} %collective-permute-done.7.refs_1_, bf16[1,512,256]{2,1,0:T(8,128)(2,1)S(1)} %copy-done.2, ...), custom_call_target="tpu_custom_call" | custom-call | flops 1073741824 | bytes 3145728 | tf_op jit(solution)/shard_map/key_values/pallas_call | solution.py:158
  50.3 1.3 copy-done
  52.0 2.7 %collective-permute-start.19 = (bf16[128,4096]{1,0:T(8,128)(2,1)S(1)}, bf16[128,4096]{1,0:T(8,128)(2,1)S(1)}, u32[]{:S(2)}, u32[]{:S(2)}) collective-permute-start(bf16[128,4096]{1,0:T(8,128)(2,1)S(1)} %fusion.4.h0), channel_id=1, source_target_pairs={{0,18},{1,19},{2,16},{3,17},{4,22},{5,23},{6,20},{7,21},{8,26},{9,... | collective-permute-start | bytes 3145736 | tf_op jit(solution)/shard_map/ppermute | solution.py:61
  54.7 7.4 %key_values.3 = (bf16[2,512,256]{2,1,0:T(8,128)(2,1)S(1)}, bf16[2,512,256]{2,1,0:T(8,128)(2,1)S(1)}) custom-call(s32[8]{0:T(128)S(1)} %stack.35.place, bf16[3,512,256]{2,1,0:T(8,128)(2,1)S(1)} %constant_dynamic-update-slice_fusion.refs_0_, bf16[3,512,256]{2,1,0:T(8,128)(2,1)S(1)} %collective-permute-done.14.refs_1_, ...), custom_call_target="tpu_custom_call" | custom-call | flops 3221225472 | bytes 9437184 | tf_op jit(solution)/shard_map/key_values/pallas_call | solution.py:158
  62.1 1.1 collective-permute-start.16
  63.2 1.2 collective-permute-start.18
  64.6 13.0 %collective-permute-done.19.h0 = bf16[128,4096]{1,0:T(8,128)(2,1)S(1)} collective-permute-done((bf16[128,4096]{1,0:T(8,128)(2,1)S(1)}, bf16[128,4096]{1,0:T(8,128)(2,1)S(1)}, u32[]{:S(2)}, u32[]{:S(2)}) %collective-permute-start.19) | collective-permute-done | bytes 1048608 | tf_op jit(solution)/shard_map/ppermute | solution.py:61
  78.1 1.8 %collective-permute-start.22 = (bf16[128,4096]{1,0:T(8,128)(2,1)S(1)}, bf16[128,4096]{1,0:T(8,128)(2,1)S(1)}, u32[]{:S(2)}, u32[]{:S(2)}) collective-permute-start(bf16[128,4096]{1,0:T(8,128)(2,1)S(1)} %collective-permute-done.19.h0), channel_id=1, source_target_pairs={{0,1},{1,0},{2,3},{3,2},{4,5},{5,4},{6,7},{7,6},{8,9},{9,8},{10,11... | collective-permute-start | bytes 3145736 | tf_op jit(solution)/shard_map/ppermute | solution.py:61
  80.0 1.5 %collective-permute-start.20 = (bf16[2,512,256]{2,1,0:T(8,128)(2,1)S(1)}, bf16[2,512,256]{2,1,0:T(8,128)(2,1)S(1)}, u32[]{:S(2)}, u32[]{:S(2)}) collective-permute-start(bf16[2,512,256]{2,1,0:T(8,128)(2,1)S(1)} %collective-permute-done.16.refs_12_), channel_id=1, source_target_pairs={{0,4},{1,5},{2,6},{3,7},{4,8},{5,9},{6,10},{7,11},{8,12},{9,13},{1... | collective-permute-start | bytes 1572872 | tf_op jit(solution)/shard_map/ppermute | solution.py:61
  81.5 2.7 %collective-permute-start.24 = (bf16[64,4096]{1,0:T(8,128)(2,1)S(1)}, bf16[64,4096]{1,0:T(8,128)(2,1)S(1)}, u32[]{:S(2)}, u32[]{:S(2)}) collective-permute-start(bf16[64,4096]{1,0:T(8,128)(2,1)S(1)} %get-tuple-element.84), channel_id=1, source_target_pairs={{0,18},{1,19},{2,16},{3,17},{4,22},{5,23},{6,20},{7,21},{8,26},{9,... | collective-permute-start | bytes 1572872 | tf_op jit(solution)/shard_map/ppermute | solution.py:61
  84.2 3.3 %queries.3 = (bf16[256,256]{1,0:T(8,128)(2,1)S(1)}, bf16[256,256]{1,0:T(8,128)(2,1)S(1)}) custom-call(s32[8]{0:T(128)S(1)} %stack.35.place, bf16[128,4096]{1,0:T(8,128)(2,1)S(1)} %collective-permute-done.19.h0, bf16[128,4096]{1,0:T(8,128)(2,1)S(1)} %collective-permute-done.22.h1, bf16[4096,512]{1,0:T(8,128)(2,1)} %bitcast.47), custom_call_target="tpu_custom_call" | custom-call | flops 1073741824 | bytes 8388608 | tf_op jit(solution)/shard_map/queries/pallas_call | solution.py:201
  87.6 6.8 %collective-permute-done.23.refs_5_ = bf16[64,4096]{1,0:T(8,128)(2,1)S(1)} collective-permute-done((bf16[64,4096]{1,0:T(8,128)(2,1)S(1)}, bf16[64,4096]{1,0:T(8,128)(2,1)S(1)}, u32[]{:S(2)}, u32[]{:S(2)}) %collective-permute-start.23) | collective-permute-done | bytes 524320 | tf_op jit(solution)/shard_map/ppermute | solution.py:61
  94.3 1.0 collective-permute-done.24.refs_7_
  95.4 1.8 %collective-permute-start.28 = (bf16[1024,256]{1,0:T(8,128)(2,1)S(1)}, bf16[1024,256]{1,0:T(8,128)(2,1)S(1)}, u32[]{:S(2)}, u32[]{:S(2)}) collective-permute-start(bf16[1024,256]{1,0:T(8,128)(2,1)S(1)} %pad_maximum_fusion.1), channel_id=1, source_target_pairs={{0,12},{1,13},{2,14},{3,15},{4,0},{5,1},{6,2},{7,3},{8,4},{9,5},{1... | collective-permute-start | bytes 1572872 | tf_op jit(solution)/shard_map/ppermute | solution.py:61
  97.3 0.8 collective-permute-start.26
  98.1 0.7 collective-permute-start.25
  98.8 0.8 collective-permute-start.32
  99.6 1.9 %collective-permute-done.26.refs_5_ = bf16[256,256]{1,0:T(8,128)(2,1)S(1)} collective-permute-done((bf16[256,256]{1,0:T(8,128)(2,1)S(1)}, bf16[256,256]{1,0:T(8,128)(2,1)S(1)}, u32[]{:S(2)}, u32[]{:S(2)}) %collective-permute-start.26) | collective-permute-done | bytes 131104 | tf_op jit(solution)/shard_map/ppermute | solution.py:61
  101.5 2.3 %collective-permute-start.33 = (bf16[64,4096]{1,0:T(8,128)(2,1)S(1)}, bf16[64,4096]{1,0:T(8,128)(2,1)S(1)}, u32[]{:S(2)}, u32[]{:S(2)}) collective-permute-start(bf16[64,4096]{1,0:T(8,128)(2,1)S(1)} %get-tuple-element.104), channel_id=1, source_target_pairs={{0,18},{1,19},{2,16},{3,17},{4,22},{5,23},{6,20},{7,21},{8,26},{9,... | collective-permute-start | bytes 1572872 | tf_op jit(solution)/shard_map/ppermute | solution.py:61
  103.8 3.3 %collective-permute-done.28.refs_8_ = bf16[1024,256]{1,0:T(8,128)(2,1)S(1)} collective-permute-done((bf16[1024,256]{1,0:T(8,128)(2,1)S(1)}, bf16[1024,256]{1,0:T(8,128)(2,1)S(1)}, u32[]{:S(2)}, u32[]{:S(2)}) %collective-permute-start.28) | collective-permute-done | bytes 524320 | tf_op jit(solution)/shard_map/ppermute | solution.py:61
  107.2 2.4 %collective-permute-done.27.refs_7_ = bf16[1024,256]{1,0:T(8,128)(2,1)S(1)} collective-permute-done((bf16[1024,256]{1,0:T(8,128)(2,1)S(1)}, bf16[1024,256]{1,0:T(8,128)(2,1)S(1)}, u32[]{:S(2)}, u32[]{:S(2)}) %collective-permute-start.27) | collective-permute-done | bytes 524320 | tf_op jit(solution)/shard_map/ppermute | solution.py:61
  109.6 9.4 %attend.1 = (bf16[256,256]{1,0:T(8,128)(2,1)S(1)}, bf16[256,256]{1,0:T(8,128)(2,1)S(1)}, bf16[256,256]{1,0:T(8,128)(2,1)S(1)}, bf16[256,256]{1,0:T(8,128)(2,1)S(1)}) custom-call(s32[8]{0:T(128)S(1)} %stack.35.place, s32[4,128]{1,0:T(4,128)S(1)} %bitcast.41, s32[4,128]{1,0:T(4,128)S(1)} %collective-permute-done.6.low_span.refs_1_, s32[1,4096]{1,0:T(1,128)S(1)} %copy-done.3, ...), custom_call_target="tpu_custom_call" | custom-call | flops 4294967296 | bytes 6291456 | tf_op jit(solution)/shard_map/attend/pallas_call | solution.py:296
  119.0 2.1 %collective-permute-start.29 = (bf16[256,256]{1,0:T(8,128)(2,1)S(1)}, bf16[256,256]{1,0:T(8,128)(2,1)S(1)}, u32[]{:S(2)}, u32[]{:S(2)}) collective-permute-start(bf16[256,256]{1,0:T(8,128)(2,1)S(1)} %get-tuple-element.95), channel_id=1, source_target_pairs={{0,2},{1,3},{2,0},{3,1},{4,6},{5,7},{6,4},{7,5},{8,10},{9,11},{10,... | collective-permute-start | bytes 393224 | tf_op jit(solution)/shard_map/ppermute | solution.py:61
  121.1 0.6 collective-permute-start.30
  122.3 2.1 %collective-permute-done.29.c1 = bf16[256,256]{1,0:T(8,128)(2,1)S(1)} collective-permute-done((bf16[256,256]{1,0:T(8,128)(2,1)S(1)}, bf16[256,256]{1,0:T(8,128)(2,1)S(1)}, u32[]{:S(2)}, u32[]{:S(2)}) %collective-permute-start.29) | collective-permute-done | bytes 131104 | tf_op jit(solution)/shard_map/ppermute | solution.py:61
  124.4 1.1 collective-permute-done.30.c2
  125.5 1.6 %collective-permute-done.31.c3 = bf16[256,256]{1,0:T(8,128)(2,1)S(1)} collective-permute-done((bf16[256,256]{1,0:T(8,128)(2,1)S(1)}, bf16[256,256]{1,0:T(8,128)(2,1)S(1)}, u32[]{:S(2)}, u32[]{:S(2)}) %collective-permute-start.31) | collective-permute-done | bytes 131104 | tf_op jit(solution)/shard_map/ppermute | solution.py:61
  127.0 3.7 %outputs.3 = bf16[256,2048]{1,0:T(8,128)(2,1)S(1)} custom-call(s32[8]{0:T(128)S(1)} %stack.35.place, bf16[256,256]{1,0:T(8,128)(2,1)S(1)} %get-tuple-element.94.c0, bf16[256,256]{1,0:T(8,128)(2,1)S(1)} %collective-permute-done.29.c1, bf16[256,256]{1,0:T(8,128)(2,1)S(1)} %collective-permute-done.30.c2, bf16[256,256]{1,0:T(8,128)(2,1)S(1)} %collective-permute-done.31.c3, ...), custom_call_target="tpu_custom_call" | custom-call | flops 1073741824 | bytes 4194304 | tf_op jit(solution)/shard_map/outputs/pallas_call | solution.py:349
  130.8 4.7 %collective-permute-start.35 = (bf16[128,2048]{1,0:T(8,128)(2,1)S(1)}, bf16[128,2048]{1,0:T(8,128)(2,1)S(1)}, u32[]{:S(2)}, u32[]{:S(2)}) collective-permute-start(bf16[128,2048]{1,0:T(8,128)(2,1)S(1)} %slice.43), channel_id=1, source_target_pairs={{0,1},{1,0},{2,3},{3,2},{4,5},{5,4},{6,7},{7,6},{8,9},{9,8},{10,11... | collective-permute-start | bytes 1572872 | tf_op jit(solution)/shard_map/ppermute | solution.py:61
  135.5 3.7 %outputs.2 = bf16[256,2048]{1,0:T(8,128)(2,1)S(1)} custom-call(s32[8]{0:T(128)S(1)} %stack.35.place, bf16[256,256]{1,0:T(8,128)(2,1)S(1)} %get-tuple-element.94.c0, bf16[256,256]{1,0:T(8,128)(2,1)S(1)} %collective-permute-done.29.c1, bf16[256,256]{1,0:T(8,128)(2,1)S(1)} %collective-permute-done.30.c2, bf16[256,256]{1,0:T(8,128)(2,1)S(1)} %collective-permute-done.31.c3, ...), custom_call_target="tpu_custom_call" | custom-call | flops 1073741824 | bytes 4194304 | tf_op jit(solution)/shard_map/outputs/pallas_call | solution.py:349
  139.6 1.8 %collective-permute-done.34 = bf16[128,2048]{1,0:T(8,128)(2,1)S(1)} collective-permute-done((bf16[128,2048]{1,0:T(8,128)(2,1)S(1)}, bf16[128,2048]{1,0:T(8,128)(2,1)S(1)}, u32[]{:S(2)}, u32[]{:S(2)}) %collective-permute-start.34) | collective-permute-done | bytes 524320 | tf_op jit(solution)/shard_map/ppermute | solution.py:61
  141.5 1.2 fusion.5
  (71 shorter events, 6.0 us)
Async XLA Ops:
  0.0 11.3 %copy-start.5 = (bf16[1,128,4096]{2,1,0:T(8,128)(2,1)S(1)}, bf16[1,128,4096]{2,1,0:T(8,128)(2,1)}, u32[]{:S(2)}) copy-start(bf16[1,128,4096]{2,1,0:T(8,128)(2,1)} %param.9) | copy-start | bytes 3145732
  0.0 11.6 %copy-start.7 = (bf16[1,4096]{1,0:T(2,128)(2,1)S(1)}, bf16[1,4096]{1,0:T(2,128)(2,1)}, u32[]{:S(2)}) copy-start(bf16[1,4096]{1,0:T(2,128)(2,1)} %param.11) | copy-start | bytes 24580
  1.2 20.8 %collective-permute-start.4 = (bf16[64,4096]{1,0:T(8,128)(2,1)S(1)}, bf16[64,4096]{1,0:T(8,128)(2,1)S(1)}, u32[]{:S(2)}, u32[]{:S(2)}) collective-permute-start(bf16[64,4096]{1,0:T(8,128)(2,1)S(1)} %dynamic-slice_bitcast_fusion), channel_id=1, source_target_pairs={{0,18},{1,19},{2,16},{3,17},{4,22},{5,23},{6,20},{7,21},{8,26},{9,... | collective-permute-start | bytes 1572872 | tf_op jit(solution)/shard_map/ppermute | solution.py:61
  6.8 8.4 %collective-permute-start.2 = (bf16[1,512,256]{2,1,0:T(8,128)(2,1)S(1)}, bf16[1,512,256]{2,1,0:T(8,128)(2,1)S(1)}, u32[]{:S(2)}, u32[]{:S(2)}) collective-permute-start(bf16[1,512,256]{2,1,0:T(8,128)(2,1)S(1)} %get-tuple-element.108), channel_id=1, source_target_pairs={{0,64},{1,65},{2,66},{3,67},{4,68},{5,69},{6,70},{7,71},{8,72},{9,... | collective-permute-start | bytes 786440 | tf_op jit(solution)/shard_map/ppermute | solution.py:61
  9.5 11.7 %collective-permute-start.1 = (bf16[1,512,256]{2,1,0:T(8,128)(2,1)S(1)}, bf16[1,512,256]{2,1,0:T(8,128)(2,1)S(1)}, u32[]{:S(2)}, u32[]{:S(2)}) collective-permute-start(bf16[1,512,256]{2,1,0:T(8,128)(2,1)S(1)} %get-tuple-element.109), channel_id=1, source_target_pairs={{0,96},{1,97},{2,98},{3,99},{4,100},{5,101},{6,102},{7,103},{8,104... | collective-permute-start | bytes 786440 | tf_op jit(solution)/shard_map/ppermute | solution.py:61
  10.4 11.2 %collective-permute-start = (bf16[1,512,256]{2,1,0:T(8,128)(2,1)S(1)}, bf16[1,512,256]{2,1,0:T(8,128)(2,1)S(1)}, u32[]{:S(2)}, u32[]{:S(2)}) collective-permute-start(bf16[1,512,256]{2,1,0:T(8,128)(2,1)S(1)} %get-tuple-element.110), channel_id=1, source_target_pairs={{0,32},{1,33},{2,34},{3,35},{4,36},{5,37},{6,38},{7,39},{8,40},{9,... | collective-permute-start | bytes 786440 | tf_op jit(solution)/shard_map/ppermute | solution.py:61
  11.0 10.6 %collective-permute-start.3 = (bf16[1,512,256]{2,1,0:T(8,128)(2,1)}, bf16[1,512,256]{2,1,0:T(8,128)(2,1)S(1)}, u32[]{:S(2)}, u32[]{:S(2)}) collective-permute-start(bf16[1,512,256]{2,1,0:T(8,128)(2,1)} %get-tuple-element.107.refs_0_), channel_id=1, source_target_pairs={{0,2},{1,3},{2,0},{3,1},{4,6},{5,7},{6,4},{7,5},{8,10},{9,11},{10,... | collective-permute-start | bytes 786440 | tf_op jit(solution)/shard_map/ppermute | solution.py:61
  21.6 5.6 %copy-start.1 = (bf16[1,512,256]{2,1,0:T(8,128)(2,1)}, bf16[1,512,256]{2,1,0:T(8,128)(2,1)S(1)}, u32[]{:S(2)}) copy-start(bf16[1,512,256]{2,1,0:T(8,128)(2,1)S(1)} %collective-permute-done.3.refs_2_) | copy-start | bytes 786436
  21.9 7.6 %collective-permute-start.11 = (bf16[128,4096]{1,0:T(8,128)(2,1)S(1)}, bf16[128,4096]{1,0:T(8,128)(2,1)}, u32[]{:S(2)}, u32[]{:S(2)}) collective-permute-start(bf16[128,4096]{1,0:T(8,128)(2,1)S(1)} %fusion.4.h0), channel_id=1, source_target_pairs={{0,1},{1,0},{2,3},{3,2},{4,5},{5,4},{6,7},{7,6},{8,9},{9,8},{10,11... | collective-permute-start | bytes 3145736 | tf_op jit(solution)/shard_map/ppermute | solution.py:61
  23.3 15.1 %collective-permute-start.10 = (bf16[64,4096]{1,0:T(8,128)(2,1)S(1)}, bf16[64,4096]{1,0:T(8,128)(2,1)S(1)}, u32[]{:S(2)}, u32[]{:S(2)}) collective-permute-start(bf16[64,4096]{1,0:T(8,128)(2,1)S(1)} %collective-permute-done.4.refs_0_), channel_id=1, source_target_pairs={{0,12},{1,13},{2,14},{3,15},{4,0},{5,1},{6,2},{7,3},{8,4},{9,5},{1... | collective-permute-start | bytes 1572872 | tf_op jit(solution)/shard_map/ppermute | solution.py:61
  27.1 14.6 %collective-permute-start.9 = (bf16[64,4096]{1,0:T(8,128)(2,1)S(1)}, bf16[64,4096]{1,0:T(8,128)(2,1)S(1)}, u32[]{:S(2)}, u32[]{:S(2)}) collective-permute-start(bf16[64,4096]{1,0:T(8,128)(2,1)S(1)} %collective-permute-done.4.refs_0_), channel_id=1, source_target_pairs={{0,4},{1,5},{2,6},{3,7},{4,8},{5,9},{6,10},{7,11},{8,12},{9,13},{1... | collective-permute-start | bytes 1572872 | tf_op jit(solution)/shard_map/ppermute | solution.py:61
  27.2 24.5 %collective-permute-start.5 = (bf16[3,512,256]{2,1,0:T(8,128)(2,1)S(1)}, bf16[3,512,256]{2,1,0:T(8,128)(2,1)}, u32[]{:S(2)}, u32[]{:S(2)}) collective-permute-start(bf16[3,512,256]{2,1,0:T(8,128)(2,1)S(1)} %constant_dynamic-update-slice_fusion.refs_0_), channel_id=1, source_target_pairs={{0,2},{1,3},{2,0},{3,1},{4,6},{5,7},{6,4},{7,5},{8,10},{9,11},{10,... | collective-permute-start | bytes 2359304 | tf_op jit(solution)/shard_map/ppermute | solution.py:61
  28.9 15.6 %collective-permute-start.7 = (bf16[1,512,256]{2,1,0:T(8,128)(2,1)}, bf16[1,512,256]{2,1,0:T(8,128)(2,1)}, u32[]{:S(2)}, u32[]{:S(2)}) collective-permute-start(bf16[1,512,256]{2,1,0:T(8,128)(2,1)} %get-tuple-element.107.refs_0_), channel_id=1, source_target_pairs={{0,1},{1,0},{2,3},{3,2},{4,5},{5,4},{6,7},{7,6},{8,9},{9,8},{10,11... | collective-permute-start | bytes 786440 | tf_op jit(solution)/shard_map/ppermute | solution.py:61
  29.5 15.1 %collective-permute-start.8 = (bf16[1,512,256]{2,1,0:T(8,128)(2,1)}, bf16[1,512,256]{2,1,0:T(8,128)(2,1)S(1)}, u32[]{:S(2)}, u32[]{:S(2)}) collective-permute-start(bf16[1,512,256]{2,1,0:T(8,128)(2,1)} %copy-done.1), channel_id=1, source_target_pairs={{0,1},{1,0},{2,3},{3,2},{4,5},{5,4},{6,7},{7,6},{8,9},{9,8},{10,11... | collective-permute-start | bytes 786440 | tf_op jit(solution)/shard_map/ppermute | solution.py:61
  33.7 10.8 %copy-start.4 = (s32[1,512]{1,0:T(1,128)S(1)}, s32[1,512]{1,0:T(1,128)}, u32[]{:S(2)}) copy-start(s32[1,512]{1,0:T(1,128)} %param.16) | copy-start | bytes 6148
  33.7 12.8 %copy-start.2 = (bf16[1,512,256]{2,1,0:T(8,128)(2,1)S(1)}, bf16[1,512,256]{2,1,0:T(8,128)(2,1)}, u32[]{:S(2)}) copy-start(bf16[1,512,256]{2,1,0:T(8,128)(2,1)} %copy-done.1) | copy-start | bytes 786436
  41.7 10.0 %collective-permute-start.13 = (bf16[32,4096]{1,0:T(8,128)(2,1)S(1)}, bf16[32,4096]{1,0:T(8,128)(2,1)S(1)}, u32[]{:S(2)}, u32[]{:S(2)}) collective-permute-start(bf16[32,4096]{1,0:T(8,128)(2,1)S(1)} %slice.31), channel_id=1, source_target_pairs={{0,12},{1,13},{2,14},{3,15},{4,0},{5,1},{6,2},{7,3},{8,4},{9,5},{1... | collective-permute-start | bytes 786440 | tf_op jit(solution)/shard_map/ppermute | solution.py:61
  42.1 9.6 %collective-permute-start.12 = (bf16[32,4096]{1,0:T(8,128)(2,1)S(1)}, bf16[32,4096]{1,0:T(8,128)(2,1)S(1)}, u32[]{:S(2)}, u32[]{:S(2)}) collective-permute-start(bf16[32,4096]{1,0:T(8,128)(2,1)S(1)} %slice.30), channel_id=1, source_target_pairs={{0,4},{1,5},{2,6},{3,7},{4,8},{5,9},{6,10},{7,11},{8,12},{9,13},{1... | collective-permute-start | bytes 786440 | tf_op jit(solution)/shard_map/ppermute | solution.py:61
  44.5 7.2 %collective-permute-start.6 = (s32[4,128]{1,0:T(4,128)S(1)}, s32[4,128]{1,0:T(4,128)S(1)}, u32[]{:S(2)}, u32[]{:S(2)}) collective-permute-start(s32[4,128]{1,0:T(4,128)S(1)} %bitcast.40), channel_id=1, source_target_pairs={{0,16},{1,17},{2,18},{3,19},{4,20},{5,21},{6,22},{7,23},{8,24},{9,... | collective-permute-start | bytes 6152 | tf_op jit(solution)/shard_map/ppermute | solution.py:61
  44.6 10.1 %collective-permute-start.14 = (bf16[3,512,256]{2,1,0:T(8,128)(2,1)S(1)}, bf16[3,512,256]{2,1,0:T(8,128)(2,1)S(1)}, u32[]{:S(2)}, u32[]{:S(2)}) collective-permute-start(bf16[3,512,256]{2,1,0:T(8,128)(2,1)S(1)} %constant_dynamic-update-slice_fusion.refs_0_), channel_id=1, source_target_pairs={{0,1},{1,0},{2,3},{3,2},{4,5},{5,4},{6,7},{7,6},{8,9},{9,8},{10,11... | collective-permute-start | bytes 2359304 | tf_op jit(solution)/shard_map/ppermute | solution.py:61
  50.3 1.3 copy-start
  51.7 3.0 %collective-permute-start.15 = (bf16[3,512,256]{2,1,0:T(8,128)(2,1)}, bf16[3,512,256]{2,1,0:T(8,128)(2,1)S(1)}, u32[]{:S(2)}, u32[]{:S(2)}) collective-permute-start(bf16[3,512,256]{2,1,0:T(8,128)(2,1)} %collective-permute-done.5.refs_2_), channel_id=1, source_target_pairs={{0,1},{1,0},{2,3},{3,2},{4,5},{5,4},{6,7},{7,6},{8,9},{9,8},{10,11... | collective-permute-start | bytes 2359304 | tf_op jit(solution)/shard_map/ppermute | solution.py:61
  52.0 25.7 %collective-permute-start.19 = (bf16[128,4096]{1,0:T(8,128)(2,1)S(1)}, bf16[128,4096]{1,0:T(8,128)(2,1)S(1)}, u32[]{:S(2)}, u32[]{:S(2)}) collective-permute-start(bf16[128,4096]{1,0:T(8,128)(2,1)S(1)} %fusion.4.h0), channel_id=1, source_target_pairs={{0,18},{1,19},{2,16},{3,17},{4,22},{5,23},{6,20},{7,21},{8,26},{9,... | collective-permute-start | bytes 3145736 | tf_op jit(solution)/shard_map/ppermute | solution.py:61
  62.1 15.6 %collective-permute-start.16 = (bf16[2,512,256]{2,1,0:T(8,128)(2,1)S(1)}, bf16[2,512,256]{2,1,0:T(8,128)(2,1)S(1)}, u32[]{:S(2)}, u32[]{:S(2)}) collective-permute-start(bf16[2,512,256]{2,1,0:T(8,128)(2,1)S(1)} %get-tuple-element.74), channel_id=1, source_target_pairs={{0,16},{1,17},{2,18},{3,19},{4,20},{5,21},{6,22},{7,23},{8,24},{9,... | collective-permute-start | bytes 1572872 | tf_op jit(solution)/shard_map/ppermute | solution.py:61
  63.2 14.5 %collective-permute-start.18 = (bf16[2,512,256]{2,1,0:T(8,128)(2,1)S(1)}, bf16[2,512,256]{2,1,0:T(8,128)(2,1)S(1)}, u32[]{:S(2)}, u32[]{:S(2)}) collective-permute-start(bf16[2,512,256]{2,1,0:T(8,128)(2,1)S(1)} %get-tuple-element.75.refs_9_), channel_id=1, source_target_pairs={{0,12},{1,13},{2,14},{3,15},{4,0},{5,1},{6,2},{7,3},{8,4},{9,5},{1... | collective-permute-start | bytes 1572872 | tf_op jit(solution)/shard_map/ppermute | solution.py:61
  64.4 13.7 %collective-permute-start.17 = (bf16[2,512,256]{2,1,0:T(8,128)(2,1)S(1)}, bf16[2,512,256]{2,1,0:T(8,128)(2,1)S(1)}, u32[]{:S(2)}, u32[]{:S(2)}) collective-permute-start(bf16[2,512,256]{2,1,0:T(8,128)(2,1)S(1)} %get-tuple-element.75.refs_9_), channel_id=1, source_target_pairs={{0,4},{1,5},{2,6},{3,7},{4,8},{5,9},{6,10},{7,11},{8,12},{9,13},{1... | collective-permute-start | bytes 1572872 | tf_op jit(solution)/shard_map/ppermute | solution.py:61
  78.1 6.1 %collective-permute-start.22 = (bf16[128,4096]{1,0:T(8,128)(2,1)S(1)}, bf16[128,4096]{1,0:T(8,128)(2,1)S(1)}, u32[]{:S(2)}, u32[]{:S(2)}) collective-permute-start(bf16[128,4096]{1,0:T(8,128)(2,1)S(1)} %collective-permute-done.19.h0), channel_id=1, source_target_pairs={{0,1},{1,0},{2,3},{3,2},{4,5},{5,4},{6,7},{7,6},{8,9},{9,8},{10,11... | collective-permute-start | bytes 3145736 | tf_op jit(solution)/shard_map/ppermute | solution.py:61
  79.9 15.4 %collective-permute-start.21 = (bf16[2,512,256]{2,1,0:T(8,128)(2,1)S(1)}, bf16[2,512,256]{2,1,0:T(8,128)(2,1)S(1)}, u32[]{:S(2)}, u32[]{:S(2)}) collective-permute-start(bf16[2,512,256]{2,1,0:T(8,128)(2,1)S(1)} %collective-permute-done.16.refs_12_), channel_id=1, source_target_pairs={{0,12},{1,13},{2,14},{3,15},{4,0},{5,1},{6,2},{7,3},{8,4},{9,5},{1... | collective-permute-start | bytes 1572872 | tf_op jit(solution)/shard_map/ppermute | solution.py:61
  80.0 15.4 %collective-permute-start.20 = (bf16[2,512,256]{2,1,0:T(8,128)(2,1)S(1)}, bf16[2,512,256]{2,1,0:T(8,128)(2,1)S(1)}, u32[]{:S(2)}, u32[]{:S(2)}) collective-permute-start(bf16[2,512,256]{2,1,0:T(8,128)(2,1)S(1)} %collective-permute-done.16.refs_12_), channel_id=1, source_target_pairs={{0,4},{1,5},{2,6},{3,7},{4,8},{5,9},{6,10},{7,11},{8,12},{9,13},{1... | collective-permute-start | bytes 1572872 | tf_op jit(solution)/shard_map/ppermute | solution.py:61
  81.4 12.9 %collective-permute-start.23 = (bf16[64,4096]{1,0:T(8,128)(2,1)S(1)}, bf16[64,4096]{1,0:T(8,128)(2,1)S(1)}, u32[]{:S(2)}, u32[]{:S(2)}) collective-permute-start(bf16[64,4096]{1,0:T(8,128)(2,1)S(1)} %collective-permute-done.4.refs_0_), channel_id=1, source_target_pairs={{0,16},{1,17},{2,18},{3,19},{4,20},{5,21},{6,22},{7,23},{8,24},{9,... | collective-permute-start | bytes 1572872 | tf_op jit(solution)/shard_map/ppermute | solution.py:61
  81.5 13.8 %collective-permute-start.24 = (bf16[64,4096]{1,0:T(8,128)(2,1)S(1)}, bf16[64,4096]{1,0:T(8,128)(2,1)S(1)}, u32[]{:S(2)}, u32[]{:S(2)}) collective-permute-start(bf16[64,4096]{1,0:T(8,128)(2,1)S(1)} %get-tuple-element.84), channel_id=1, source_target_pairs={{0,18},{1,19},{2,16},{3,17},{4,22},{5,23},{6,20},{7,21},{8,26},{9,... | collective-permute-start | bytes 1572872 | tf_op jit(solution)/shard_map/ppermute | solution.py:61
  87.5 22.1 %copy-start.3 = (s32[1,4096]{1,0:T(1,128)S(1)}, s32[1,4096]{1,0:T(1,128)}, u32[]{:S(2)}) copy-start(s32[1,4096]{1,0:T(1,128)} %refs_2_.1) | copy-start | bytes 49156
  95.4 11.7 %collective-permute-start.28 = (bf16[1024,256]{1,0:T(8,128)(2,1)S(1)}, bf16[1024,256]{1,0:T(8,128)(2,1)S(1)}, u32[]{:S(2)}, u32[]{:S(2)}) collective-permute-start(bf16[1024,256]{1,0:T(8,128)(2,1)S(1)} %pad_maximum_fusion.1), channel_id=1, source_target_pairs={{0,12},{1,13},{2,14},{3,15},{4,0},{5,1},{6,2},{7,3},{8,4},{9,5},{1... | collective-permute-start | bytes 1572872 | tf_op jit(solution)/shard_map/ppermute | solution.py:61
  97.2 12.4 %collective-permute-start.27 = (bf16[1024,256]{1,0:T(8,128)(2,1)S(1)}, bf16[1024,256]{1,0:T(8,128)(2,1)S(1)}, u32[]{:S(2)}, u32[]{:S(2)}) collective-permute-start(bf16[1024,256]{1,0:T(8,128)(2,1)S(1)} %pad_maximum_fusion), channel_id=1, source_target_pairs={{0,4},{1,5},{2,6},{3,7},{4,8},{5,9},{6,10},{7,11},{8,12},{9,13},{1... | collective-permute-start | bytes 1572872 | tf_op jit(solution)/shard_map/ppermute | solution.py:61
  97.3 4.2 %collective-permute-start.26 = (bf16[256,256]{1,0:T(8,128)(2,1)S(1)}, bf16[256,256]{1,0:T(8,128)(2,1)S(1)}, u32[]{:S(2)}, u32[]{:S(2)}) collective-permute-start(bf16[256,256]{1,0:T(8,128)(2,1)S(1)} %get-tuple-element.88), channel_id=1, source_target_pairs={{0,16},{1,17},{2,18},{3,19},{4,20},{5,21},{6,22},{7,23},{8,24},{9,... | collective-permute-start | bytes 393224 | tf_op jit(solution)/shard_map/ppermute | solution.py:61
  98.1 5.7 %collective-permute-start.25 = (bf16[256,256]{1,0:T(8,128)(2,1)S(1)}, bf16[256,256]{1,0:T(8,128)(2,1)S(1)}, u32[]{:S(2)}, u32[]{:S(2)}) collective-permute-start(bf16[256,256]{1,0:T(8,128)(2,1)S(1)} %get-tuple-element.87), channel_id=1, source_target_pairs={{0,16},{1,17},{2,18},{3,19},{4,20},{5,21},{6,22},{7,23},{8,24},{9,... | collective-permute-start | bytes 393224 | tf_op jit(solution)/shard_map/ppermute | solution.py:61
  98.8 23.5 %collective-permute-start.32 = (bf16[64,4096]{1,0:T(8,128)(2,1)S(1)}, bf16[64,4096]{1,0:T(8,128)(2,1)S(1)}, u32[]{:S(2)}, u32[]{:S(2)}) collective-permute-start(bf16[64,4096]{1,0:T(8,128)(2,1)S(1)} %collective-permute-done.9.refs_1_), channel_id=1, source_target_pairs={{0,16},{1,17},{2,18},{3,19},{4,20},{5,21},{6,22},{7,23},{8,24},{9,... | collective-permute-start | bytes 1572872 | tf_op jit(solution)/shard_map/ppermute | solution.py:61
  101.5 20.8 %collective-permute-start.33 = (bf16[64,4096]{1,0:T(8,128)(2,1)S(1)}, bf16[64,4096]{1,0:T(8,128)(2,1)S(1)}, u32[]{:S(2)}, u32[]{:S(2)}) collective-permute-start(bf16[64,4096]{1,0:T(8,128)(2,1)S(1)} %get-tuple-element.104), channel_id=1, source_target_pairs={{0,18},{1,19},{2,16},{3,17},{4,22},{5,23},{6,20},{7,21},{8,26},{9,... | collective-permute-start | bytes 1572872 | tf_op jit(solution)/shard_map/ppermute | solution.py:61
  119.0 5.4 %collective-permute-start.29 = (bf16[256,256]{1,0:T(8,128)(2,1)S(1)}, bf16[256,256]{1,0:T(8,128)(2,1)S(1)}, u32[]{:S(2)}, u32[]{:S(2)}) collective-permute-start(bf16[256,256]{1,0:T(8,128)(2,1)S(1)} %get-tuple-element.95), channel_id=1, source_target_pairs={{0,2},{1,3},{2,0},{3,1},{4,6},{5,7},{6,4},{7,5},{8,10},{9,11},{10,... | collective-permute-start | bytes 393224 | tf_op jit(solution)/shard_map/ppermute | solution.py:61
  121.1 4.4 %collective-permute-start.30 = (bf16[256,256]{1,0:T(8,128)(2,1)S(1)}, bf16[256,256]{1,0:T(8,128)(2,1)S(1)}, u32[]{:S(2)}, u32[]{:S(2)}) collective-permute-start(bf16[256,256]{1,0:T(8,128)(2,1)S(1)} %get-tuple-element.96), channel_id=1, source_target_pairs={{0,16},{1,17},{2,18},{3,19},{4,20},{5,21},{6,22},{7,23},{8,24},{9,... | collective-permute-start | bytes 393224 | tf_op jit(solution)/shard_map/ppermute | solution.py:61
  121.7 5.3 %collective-permute-start.31 = (bf16[256,256]{1,0:T(8,128)(2,1)S(1)}, bf16[256,256]{1,0:T(8,128)(2,1)S(1)}, u32[]{:S(2)}, u32[]{:S(2)}) collective-permute-start(bf16[256,256]{1,0:T(8,128)(2,1)S(1)} %get-tuple-element.97), channel_id=1, source_target_pairs={{0,18},{1,19},{2,16},{3,17},{4,22},{5,23},{6,20},{7,21},{8,26},{9,... | collective-permute-start | bytes 393224 | tf_op jit(solution)/shard_map/ppermute | solution.py:61
  130.8 8.6 %collective-permute-start.35 = (bf16[128,2048]{1,0:T(8,128)(2,1)S(1)}, bf16[128,2048]{1,0:T(8,128)(2,1)S(1)}, u32[]{:S(2)}, u32[]{:S(2)}) collective-permute-start(bf16[128,2048]{1,0:T(8,128)(2,1)S(1)} %slice.43), channel_id=1, source_target_pairs={{0,1},{1,0},{2,3},{3,2},{4,5},{5,4},{6,7},{7,6},{8,9},{9,8},{10,11... | collective-permute-start | bytes 1572872 | tf_op jit(solution)/shard_map/ppermute | solution.py:61
  139.3 2.1 %copy-start.6 = (bf16[1,128,4096]{2,1,0:T(8,128)(2,1)S(1)}, bf16[1,128,4096]{2,1,0:T(8,128)(2,1)}, u32[]{:S(2)}) copy-start(bf16[1,128,4096]{2,1,0:T(8,128)(2,1)} %param.9) | copy-start | bytes 3145732
  139.4 2.0 %collective-permute-start.34 = (bf16[128,2048]{1,0:T(8,128)(2,1)S(1)}, bf16[128,2048]{1,0:T(8,128)(2,1)S(1)}, u32[]{:S(2)}, u32[]{:S(2)}) collective-permute-start(bf16[128,2048]{1,0:T(8,128)(2,1)S(1)} %slice.41), channel_id=1, source_target_pairs={{0,1},{1,0},{2,3},{3,2},{4,5},{5,4},{6,7},{7,6},{8,9},{9,8},{10,11... | collective-permute-start | bytes 1572872 | tf_op jit(solution)/shard_map/ppermute | solution.py:61

commit v5 on v4

--- a/solution.py
+++ b/solution.py
@@ -216,9 +216,11 @@
     )(place, *blocks, w_query)
 
 
-def attend_kernel(pieces, keys, place, own_span, low_span, key_span, *refs):
+def attend_kernel(pieces, keys, last, place, own_span, low_span, key_span, *refs):
     ids_own, ids_low, key_ids, near, far_low, near_low, far = refs[:7]
-    arrays, outs, (query, ids, scores, peak, total, context) = refs[7:-10], refs[-10:-6], refs[-6:]
+    query, ids, scores, peak, total, context = refs[-6:]
+    outs, refs = (refs[-10:-6], refs[7:-10]) if last else (refs[-9:-6], refs[7:-9])
+    arrays, before = (refs[:-3], refs[-3:]) if last else (refs, None)
     block = ATTEND_ROWS
     scale = HD ** (-0.5) * math.log2(math.e)
     low, mp, z = place[1], place[2], place[7]
@@ -235,9 +237,13 @@
         rows = pl.ds(pl.multiple_of(at * block, block), block)
         lowest = jnp.where(at == 0, own_span[0, 0], low_span[0, 0])
         highest_id = jnp.where(at == 0, own_span[3, 127], low_span[3, 127])
-        peak[...] = jnp.full_like(peak, -1e30)
-        total[...] = jnp.zeros_like(total)
-        context[...] = jnp.zeros_like(context)
+        if last:
+            peak[...] = before[0][rows]
+            earlier = jnp.max(peak[...], axis=-1, keepdims=True)
+        else:
+            peak[...] = jnp.full_like(peak, -1e30)
+            total[...] = jnp.zeros_like(total)
+            context[...] = jnp.zeros_like(context)
 
         def rows_of(held):
             array, lead, row = held
@@ -266,6 +272,10 @@
 
         for_each_part(score)
         highest = jnp.max(peak[...], axis=-1, keepdims=True)
+        if last:
+            shrink = jnp.exp2(earlier - highest)
+            total[...] = before[1][rows] * shrink
+            context[...] = before[2][rows] * shrink
 
         def weigh(part, part_keys, part_values, first):
             weights = jnp.exp2(scores[part] - highest)
@@ -276,6 +286,11 @@
             context[...] += dot(weights.astype(BF16), part_values[...])
 
         for_each_part(weigh)
+        if not last:
+            for out, value in zip(outs, (peak, total, context)):
+                out[rows] = value[...]
+            return 0
+
         whole = jnp.sum(total[...], axis=-1, keepdims=True)
         context[...] = context[...] / whole
 
@@ -291,16 +306,19 @@
     lax.fori_loop(0, 2, one_block, 0)
 
 
-def attend(keys, pieces, arrays, place, ids_own, ids_low, key_ids, blocks):
-    out = jax.ShapeDtypeStruct((256, HD), BF16)
+def attend(keys, pieces, arrays, place, ids_own, ids_low, key_ids, blocks, before=()):
+    rows = 2 * ATTEND_ROWS
+    context = jax.ShapeDtypeStruct((256, HD), BF16)
+    state = [jax.ShapeDtypeStruct((rows, width), F32) for width in (128, 128, HD)]
+    outs = (context,) * 4 if before else tuple(state)
     return pl.pallas_call(
-        functools.partial(attend_kernel, pieces, keys),
-        out_shape=(out,) * 4,
-        in_specs=smem(4) + vmem(7 + len(arrays)),
-        out_specs=tuple(vmem(4)),
+        functools.partial(attend_kernel, pieces, keys, bool(before)),
+        out_shape=outs,
+        in_specs=smem(4) + vmem(7 + len(arrays) + len(before)),
+        out_specs=tuple(vmem(len(outs))),
         scratch_shapes=[
-            pltpu.VMEM((2 * ATTEND_ROWS, HD), BF16),
-            pltpu.VMEM((2 * ATTEND_ROWS, 128), jnp.int32),
+            pltpu.VMEM((rows, HD), BF16),
+            pltpu.VMEM((rows, 128), jnp.int32),
             pltpu.VMEM((len(pieces), ATTEND_ROWS, keys), F32),
             pltpu.VMEM((ATTEND_ROWS, 128), F32),
             pltpu.VMEM((ATTEND_ROWS, 128), F32),
@@ -308,10 +326,12 @@
         ],
         compiler_params=params(28),
         cost_estimate=pl.CostEstimate(
-            flops=4 * 1024 * 4096 * 256, bytes_accessed=6 * MIB, transcendentals=1024 * 1024
+            flops=256 * 1024 * 256 * len(pieces),
+            bytes_accessed=6 * MIB,
+            transcendentals=1024 * 64 * len(pieces),
         ),
         name="attend",
-    )(place, ids_own, ids_low, key_ids, ids_own, ids_low, key_ids, *blocks, *arrays)
+    )(place, ids_own, ids_low, key_ids, ids_own, ids_low, key_ids, *blocks, *arrays, *before)
 
 
 def output_kernel(first, place, c0, c1, c2, c3, w_own, *refs):
@@ -345,7 +365,7 @@
 
 
 def outputs(place, contexts, w_own, pieces, part, parts):
-    width, step = 4096 // parts, 512
+    width, step = 4096 // parts, 1024
     return pl.pallas_call(
         functools.partial(output_kernel, part * width),
         out_shape=jax.ShapeDtypeStruct((256, width), BF16),
@@ -438,25 +458,34 @@
     hidden, _ = lax.optimization_barrier((hidden, rest_far))
     hidden_cut = send(hidden, Y_CUT)
     below_0, above_0 = send(mine, Z_UP), send(mine, Z_DOWN)
-    theirs, below_0, above_0, hidden_cut, piece, cut_1 = lax.optimization_barrier(
-        (send(other, Y_LOW), below_0, above_0, hidden_cut, far_rows[0], cut_1)
+    theirs, below_0, above_0, hidden_cut, piece, cut_1, near_low = lax.optimization_barrier(
+        (
+            send(other, Y_LOW),
+            below_0,
+            above_0,
+            hidden_cut,
+            far_rows[0],
+            cut_1,
+            send(near_other, Y_LOW),
+        )
     )
     below_1, above_1 = send(theirs, Z_UP), send(theirs, Z_DOWN)
 
     far_mine, far_other = queries(place, (hidden_cut, send(hidden_cut, CORE)), w_query[0])
     other_0, other_1 = send(piece, Y_LOW), send(cut_1, Y_CUT)
-    below_1, above_1, far_mine, far_other, other_0, other_1, piece, cut_2 = (
+    far_low = send(far_other, Y_LOW)
+    below_1, above_1, far_mine, far_low, other_0, other_1, piece, cut_2 = (
         lax.optimization_barrier(
-            (below_1, above_1, far_mine, far_other, other_0, other_1, far_rows[1], cut_2)
+            (below_1, above_1, far_mine, far_low, other_0, other_1, far_rows[1], cut_2)
         )
     )
     across_keys = send(jnp.concatenate([below_0[0], below_1[0]]), Z_UP)
     across_values = send(jnp.concatenate([above_0[1], above_1[1]]), Z_DOWN)
     far_rows += [other_0, send(piece, Y_LOW), other_1, send(cut_2, Y_CUT)]
 
-    blocks = (near_mine, send(far_other, Y_LOW), send(near_other, Y_LOW), far_mine)
-
-    arrays, pieces = [across_keys, across_values], []
+    blocks = (near_mine, far_low, near_low, far_mine)
+
+    arrays, pieces, last_pieces = [], [], []
     for flip_low, (held, below, above) in enumerate(
         ((mine, below_0, above_0), (theirs, below_1, above_1))
     ):
@@ -467,10 +496,12 @@
                 pieces.append((flip_low, turn, row, (at, (0,), row), (at, (1,), row)))
         for row in range(0, 512, KEYS):
             held_row = flip_low * 512 + row
-            pieces.append((flip_low, 2, row, (0, (), held_row), (1, (), held_row)))
-
+            last_pieces.append((flip_low, 2, row, (0, (), held_row), (1, (), held_row)))
+
+    state = attend(KEYS, pieces, arrays, place, ids_own, ids_low, encoder_segments, blocks)
+    arrays = [across_keys, across_values]
     contexts = attend(
-        KEYS, pieces, arrays, place, ids_own, ids_low, encoder_segments, blocks
+        KEYS, last_pieces, arrays, place, ids_own, ids_low, encoder_segments, blocks, state
     )
 
     contexts = (contexts[0],) + tuple(

time: 143 us -> 139 us (0.972)
  waiting for transfers between devices: 53.2 us -> 50.2 us
    ppermute x36, waiting for transfers between devices: 53.2 us -> 50.2 us  [send(): return lax.ppermute(array, AXES, pairs)]
    pallas_call x1 -> x2, Pallas kernels: 9.38 us -> 9.06 us  [attend(): pl.pallas_call(functools.partial(attend_kernel, pieces, keys, bool(before...]
  transfers between devices with their start and end apart: 36 -> 36, of which waited for: 17 -> 16; matrix products, arithmetic and copies ran while one was open for 3% -> 3% of each run, Pallas kernels for 22% -> 22%
where the time goes in v5:
time: 139 us; the launch traced here: 138 us
  waiting for transfers between devices  50.2 us (36%)
  starting transfers between devices  45.1 us (32%)
  Pallas kernels  34.4 us (25%)
  local copies, waits for them, and re-layouts  6.07 us (4%)
  other arithmetic  2.13 us (2%)
    ppermute x36, waiting for transfers between devices, send(): return lax.ppermute(array, AXES, pairs)  50.2 us
    ppermute x36, starting transfers between devices, send(): return lax.ppermute(array, AXES, pairs)  45.1 us
    pallas_call x2, Pallas kernels, key_values(): pl.pallas_call(functools.partial(key_value_kernel, steps), out_shape=(out...  11.2 us
    pallas_call x2, Pallas kernels, attend(): pl.pallas_call(functools.partial(attend_kernel, pieces, keys, bool(before...  9.06 us
    pallas_call x2, Pallas kernels, queries(): pl.pallas_call(query_kernel, out_shape=(out, out), in_specs=smem(1) + vme...  7.35 us
    pallas_call x2, Pallas kernels, outputs(): pl.pallas_call(functools.partial(output_kernel, part * width), out_shape=...  6.79 us
  transfers between devices with their start and end apart: 36, of which 16 were waited for; matrix products, arithmetic and copies ran while one was open for 3% of the time, Pallas kernels for 22%

profile of v5, /device:TPU:1, one launch (start us, length us, event | category | flops | bytes accessed | tf_op | source)
XLA Modules:
  0.0 138.3 jit_solution(8925345220678421317)
XLA Ops:
  0.0 1.2 dynamic-slice_bitcast_fusion
  1.2 3.6 %collective-permute-start.4 = (bf16[64,4096]{1,0:T(8,128)(2,1)S(1)}, bf16[64,4096]{1,0:T(8,128)(2,1)S(1)}, u32[]{:S(2)}, u32[]{:S(2)}) collective-permute-start(bf16[64,4096]{1,0:T(8,128)(2,1)S(1)} %dynamic-slice_bitcast_fusion), channel_id=1, source_target_pairs={{0,18},{1,19},{2,16},{3,17},{4,22},{5,23},{6,20},{7,21},{8,26},{9,... | collective-permute-start | bytes 1572872 | tf_op jit(solution)/shard_map/ppermute | solution.py:61
  4.8 2.0 %constant_dynamic-slice_fusion.2 = (bf16[1,512,256]{2,1,0:T(8,128)(2,1)}, bf16[1,512,256]{2,1,0:T(8,128)(2,1)S(1)}, bf16[1,512,256]{2,1,0:T(8,128)(2,1)S(1)}, bf16[1,512,256]{2,1,0:T(8,128)(2,1)S(1)}) fusion(bf16[4,512,256]{2,1,0:T(8,128)(2,1)} %param.10, s32[]{:T(128)S(6)} %select_n.82, s32[]{:T(128)S(6)} %select_n.81, s32[]{:T(128)S(6)} %select_n.80, ...), kind=kLoop, calls=%fused_computation.22 | loop fusion | bytes 2097168 | tf_op jit(solution)/shard_map/dynamic_slice | solution.py:408
  6.8 2.7 %collective-permute-start.2 = (bf16[1,512,256]{2,1,0:T(8,128)(2,1)S(1)}, bf16[1,512,256]{2,1,0:T(8,128)(2,1)S(1)}, u32[]{:S(2)}, u32[]{:S(2)}) collective-permute-start(bf16[1,512,256]{2,1,0:T(8,128)(2,1)S(1)} %get-tuple-element.116), channel_id=1, source_target_pairs={{0,64},{1,65},{2,66},{3,67},{4,68},{5,69},{6,70},{7,71},{8,72},{9,... | collective-permute-start | bytes 786440 | tf_op jit(solution)/shard_map/ppermute | solution.py:61
  9.5 0.9 collective-permute-start.1
  10.4 0.6 collective-permute-start
  12.0 3.1 %collective-permute-done.2 = bf16[1,512,256]{2,1,0:T(8,128)(2,1)S(1)} collective-permute-done((bf16[1,512,256]{2,1,0:T(8,128)(2,1)S(1)}, bf16[1,512,256]{2,1,0:T(8,128)(2,1)S(1)}, u32[]{:S(2)}, u32[]{:S(2)}) %collective-permute-start.2) | collective-permute-done | bytes 262176 | tf_op jit(solution)/shard_map/ppermute | solution.py:61
  15.1 6.1 %collective-permute-done.1 = bf16[1,512,256]{2,1,0:T(8,128)(2,1)S(1)} collective-permute-done((bf16[1,512,256]{2,1,0:T(8,128)(2,1)S(1)}, bf16[1,512,256]{2,1,0:T(8,128)(2,1)S(1)}, u32[]{:S(2)}, u32[]{:S(2)}) %collective-permute-start.1) | collective-permute-done | bytes 262176 | tf_op jit(solution)/shard_map/ppermute | solution.py:61
  21.9 1.4 collective-permute-start.11
  23.3 3.8 %collective-permute-start.10 = (bf16[64,4096]{1,0:T(8,128)(2,1)S(1)}, bf16[64,4096]{1,0:T(8,128)(2,1)S(1)}, u32[]{:S(2)}, u32[]{:S(2)}) collective-permute-start(bf16[64,4096]{1,0:T(8,128)(2,1)S(1)} %collective-permute-done.4.refs_0_), channel_id=1, source_target_pairs={{0,12},{1,13},{2,14},{3,15},{4,0},{5,1},{6,2},{7,3},{8,4},{9,5},{1... | collective-permute-start | bytes 1572872 | tf_op jit(solution)/shard_map/ppermute | solution.py:61
  27.2 1.7 %collective-permute-start.5 = (bf16[3,512,256]{2,1,0:T(8,128)(2,1)S(1)}, bf16[3,512,256]{2,1,0:T(8,128)(2,1)}, u32[]{:S(2)}, u32[]{:S(2)}) collective-permute-start(bf16[3,512,256]{2,1,0:T(8,128)(2,1)S(1)} %constant_dynamic-update-slice_fusion.refs_0_), channel_id=1, source_target_pairs={{0,2},{1,3},{2,0},{3,1},{4,6},{5,7},{6,4},{7,5},{8,10},{9,11},{10,... | collective-permute-start | bytes 2359304 | tf_op jit(solution)/shard_map/ppermute | solution.py:61
  28.9 0.6 collective-permute-start.7
  29.6 4.0 %queries.2 = (bf16[256,256]{1,0:T(8,128)(2,1)S(1)}, bf16[256,256]{1,0:T(8,128)(2,1)S(1)}) custom-call(s32[8]{0:T(128)S(1)} %stack.35.place, bf16[128,4096]{1,0:T(8,128)(2,1)S(1)} %fusion.4.h0, bf16[128,4096]{1,0:T(8,128)(2,1)} %collective-permute-done.11.h1, bf16[4096,512]{1,0:T(8,128)(2,1)} %bitcast.48), custom_call_target="tpu_custom_call" | custom-call | flops 1073741824 | bytes 8388608 | tf_op jit(solution)/shard_map/queries/pallas_call | solution.py:201
  33.7 4.7 %collective-permute-done.10.refs_2_ = bf16[64,4096]{1,0:T(8,128)(2,1)S(1)} collective-permute-done((bf16[64,4096]{1,0:T(8,128)(2,1)S(1)}, bf16[64,4096]{1,0:T(8,128)(2,1)S(1)}, u32[]{:S(2)}, u32[]{:S(2)}) %collective-permute-start.10) | collective-permute-done | bytes 524320 | tf_op jit(solution)/shard_map/ppermute | solution.py:61
  38.4 3.2 %collective-permute-done.9.refs_1_ = bf16[64,4096]{1,0:T(8,128)(2,1)S(1)} collective-permute-done((bf16[64,4096]{1,0:T(8,128)(2,1)S(1)}, bf16[64,4096]{1,0:T(8,128)(2,1)S(1)}, u32[]{:S(2)}, u32[]{:S(2)}) %collective-permute-start.9) | collective-permute-done | bytes 524320 | tf_op jit(solution)/shard_map/ppermute | solution.py:61
  42.1 1.1 collective-permute-start.12
  43.2 1.3 constant_dynamic-slice_fusion
  44.6 1.8 %collective-permute-start.14 = (bf16[3,512,256]{2,1,0:T(8,128)(2,1)S(1)}, bf16[3,512,256]{2,1,0:T(8,128)(2,1)S(1)}, u32[]{:S(2)}, u32[]{:S(2)}) collective-permute-start(bf16[3,512,256]{2,1,0:T(8,128)(2,1)S(1)} %constant_dynamic-update-slice_fusion.refs_0_), channel_id=1, source_target_pairs={{0,1},{1,0},{2,3},{3,2},{4,5},{5,4},{6,7},{7,6},{8,9},{9,8},{10,11... | collective-permute-start | bytes 2359304 | tf_op jit(solution)/shard_map/ppermute | solution.py:61
  46.4 3.9 %key_values.2.refs_6_ = f32[2,512,512]{2,1,0:T(8,128)S(1)} custom-call(s32[8]{0:T(128)S(1)} %stack.35.place, bf16[1,512,256]{2,1,0:T(8,128)(2,1)} %get-tuple-element.115.refs_0_, bf16[1,512,256]{2,1,0:T(8,128)(2,1)} %collective-permute-done.7.refs_1_, bf16[1,512,256]{2,1,0:T(8,128)(2,1)S(1)} %copy-done.3, ...), custom_call_target="tpu_custom_call" | custom-call | flops 1073741824 | bytes 3145728 | tf_op jit(solution)/shard_map/key_values/pallas_call | solution.py:158
  50.3 1.3 copy-done
  52.0 2.7 %collective-permute-start.19 = (bf16[128,4096]{1,0:T(8,128)(2,1)S(1)}, bf16[128,4096]{1,0:T(8,128)(2,1)S(1)}, u32[]{:S(2)}, u32[]{:S(2)}) collective-permute-start(bf16[128,4096]{1,0:T(8,128)(2,1)S(1)} %fusion.4.h0), channel_id=1, source_target_pairs={{0,18},{1,19},{2,16},{3,17},{4,22},{5,23},{6,20},{7,21},{8,26},{9,... | collective-permute-start | bytes 3145736 | tf_op jit(solution)/shard_map/ppermute | solution.py:61
  54.7 7.4 %key_values.3 = (bf16[2,512,256]{2,1,0:T(8,128)(2,1)S(1)}, bf16[2,512,256]{2,1,0:T(8,128)(2,1)S(1)}) custom-call(s32[8]{0:T(128)S(1)} %stack.35.place, bf16[3,512,256]{2,1,0:T(8,128)(2,1)S(1)} %constant_dynamic-update-slice_fusion.refs_0_, bf16[3,512,256]{2,1,0:T(8,128)(2,1)S(1)} %collective-permute-done.14.refs_1_, ...), custom_call_target="tpu_custom_call" | custom-call | flops 3221225472 | bytes 9437184 | tf_op jit(solution)/shard_map/key_values/pallas_call | solution.py:158
  62.1 1.1 collective-permute-start.16
  63.2 1.2 collective-permute-start.18
  65.1 13.0 %collective-permute-done.20.refs_5_ = bf16[256,256]{1,0:T(8,128)(2,1)S(1)} collective-permute-done((bf16[256,256]{1,0:T(8,128)(2,1)S(1)}, bf16[256,256]{1,0:T(8,128)(2,1)S(1)}, u32[]{:S(2)}, u32[]{:S(2)}) %collective-permute-start.20) | collective-permute-done | bytes 131104 | tf_op jit(solution)/shard_map/ppermute | solution.py:61
  78.1 1.8 %collective-permute-start.23 = (bf16[128,4096]{1,0:T(8,128)(2,1)S(1)}, bf16[128,4096]{1,0:T(8,128)(2,1)S(1)}, u32[]{:S(2)}, u32[]{:S(2)}) collective-permute-start(bf16[128,4096]{1,0:T(8,128)(2,1)S(1)} %collective-permute-done.19.h0), channel_id=1, source_target_pairs={{0,1},{1,0},{2,3},{3,2},{4,5},{5,4},{6,7},{7,6},{8,9},{9,8},{10,11... | collective-permute-start | bytes 3145736 | tf_op jit(solution)/shard_map/ppermute | solution.py:61
  80.4 0.9 collective-permute-start.21
  81.4 0.7 collective-permute-start.25
  82.1 2.7 %collective-permute-start.26 = (bf16[64,4096]{1,0:T(8,128)(2,1)S(1)}, bf16[64,4096]{1,0:T(8,128)(2,1)S(1)}, u32[]{:S(2)}, u32[]{:S(2)}) collective-permute-start(bf16[64,4096]{1,0:T(8,128)(2,1)S(1)} %get-tuple-element.89), channel_id=1, source_target_pairs={{0,18},{1,19},{2,16},{3,17},{4,22},{5,23},{6,20},{7,21},{8,26},{9,... | collective-permute-start | bytes 1572872 | tf_op jit(solution)/shard_map/ppermute | solution.py:61
  84.8 3.3 %queries.3 = (bf16[256,256]{1,0:T(8,128)(2,1)S(1)}, bf16[256,256]{1,0:T(8,128)(2,1)S(1)}) custom-call(s32[8]{0:T(128)S(1)} %stack.35.place, bf16[128,4096]{1,0:T(8,128)(2,1)S(1)} %collective-permute-done.19.h0, bf16[128,4096]{1,0:T(8,128)(2,1)S(1)} %collective-permute-done.23.h1, bf16[4096,512]{1,0:T(8,128)(2,1)} %bitcast.49), custom_call_target="tpu_custom_call" | custom-call | flops 1073741824 | bytes 8388608 | tf_op jit(solution)/shard_map/queries/pallas_call | solution.py:201
  88.4 5.9 %collective-permute-done.25.refs_5_ = bf16[64,4096]{1,0:T(8,128)(2,1)S(1)} collective-permute-done((bf16[64,4096]{1,0:T(8,128)(2,1)S(1)}, bf16[64,4096]{1,0:T(8,128)(2,1)S(1)}, u32[]{:S(2)}, u32[]{:S(2)}) %collective-permute-start.25) | collective-permute-done | bytes 524320 | tf_op jit(solution)/shard_map/ppermute | solution.py:61
  94.3 1.5 %collective-permute-done.26.refs_7_ = bf16[64,4096]{1,0:T(8,128)(2,1)S(1)} collective-permute-done((bf16[64,4096]{1,0:T(8,128)(2,1)S(1)}, bf16[64,4096]{1,0:T(8,128)(2,1)S(1)}, u32[]{:S(2)}, u32[]{:S(2)}) %collective-permute-start.26) | collective-permute-done | bytes 524320 | tf_op jit(solution)/shard_map/ppermute | solution.py:61
  95.8 1.3 collective-permute-done.24.refs_4_
  97.2 1.7 %collective-permute-start.28 = (bf16[1024,256]{1,0:T(8,128)(2,1)S(1)}, bf16[1024,256]{1,0:T(8,128)(2,1)S(1)}, u32[]{:S(2)}, u32[]{:S(2)}) collective-permute-start(bf16[1024,256]{1,0:T(8,128)(2,1)S(1)} %pad_maximum_fusion.1), channel_id=1, source_target_pairs={{0,12},{1,13},{2,14},{3,15},{4,0},{5,1},{6,2},{7,3},{8,4},{9,5},{1... | collective-permute-start | bytes 1572872 | tf_op jit(solution)/shard_map/ppermute | solution.py:61
  99.1 1.5 %collective-permute-start.32 = (bf16[64,4096]{1,0:T(8,128)(2,1)S(1)}, bf16[64,4096]{1,0:T(8,128)(2,1)S(1)}, u32[]{:S(2)}, u32[]{:S(2)}) collective-permute-start(bf16[64,4096]{1,0:T(8,128)(2,1)S(1)} %collective-permute-done.9.refs_1_), channel_id=1, source_target_pairs={{0,16},{1,17},{2,18},{3,19},{4,20},{5,21},{6,22},{7,23},{8,24},{9,... | collective-permute-start | bytes 1572872 | tf_op jit(solution)/shard_map/ppermute | solution.py:61
  100.5 2.7 %collective-permute-start.33 = (bf16[64,4096]{1,0:T(8,128)(2,1)S(1)}, bf16[64,4096]{1,0:T(8,128)(2,1)S(1)}, u32[]{:S(2)}, u32[]{:S(2)}) collective-permute-start(bf16[64,4096]{1,0:T(8,128)(2,1)S(1)} %get-tuple-element.112), channel_id=1, source_target_pairs={{0,18},{1,19},{2,16},{3,17},{4,22},{5,23},{6,20},{7,21},{8,26},{9,... | collective-permute-start | bytes 1572872 | tf_op jit(solution)/shard_map/ppermute | solution.py:61
  103.2 6.0 %attend.2 = (f32[1024,128]{1,0:T(8,128)S(1)}, f32[1024,128]{1,0:T(8,128)S(1)}, f32[1024,256]{1,0:T(8,128)S(1)}) custom-call(s32[8]{0:T(128)S(1)} %stack.35.place, s32[4,128]{1,0:T(4,128)S(1)} %bitcast.41, s32[4,128]{1,0:T(4,128)S(1)} %collective-permute-done.6.low_span.refs_1_, s32[1,4096]{1,0:T(1,128)S(1)} %copy-done.1, s32[4,128]{1,0:T(4,128)S(1)} %bitcast.42, ...), custom_call_target="tpu_custom_call" | custom-call | flops 805306368 | bytes 6291456 | tf_op jit(solution)/shard_map/attend/pallas_call | solution.py:314
  109.3 2.6 %collective-permute-done.27.refs_7_ = bf16[1024,256]{1,0:T(8,128)(2,1)S(1)} collective-permute-done((bf16[1024,256]{1,0:T(8,128)(2,1)S(1)}, bf16[1024,256]{1,0:T(8,128)(2,1)S(1)}, u32[]{:S(2)}, u32[]{:S(2)}) %collective-permute-start.27) | collective-permute-done | bytes 524320 | tf_op jit(solution)/shard_map/ppermute | solution.py:61
  111.9 3.1 %attend.3 = (bf16[256,256]{1,0:T(8,128)(2,1)S(1)}, bf16[256,256]{1,0:T(8,128)(2,1)S(1)}, bf16[256,256]{1,0:T(8,128)(2,1)S(1)}, bf16[256,256]{1,0:T(8,128)(2,1)S(1)}) custom-call(s32[8]{0:T(128)S(1)} %stack.35.place, s32[4,128]{1,0:T(4,128)S(1)} %bitcast.43, s32[4,128]{1,0:T(4,128)S(1)} %collective-permute-done.6.low_span.refs_1_, s32[1,4096]{1,0:T(1,128)S(1)} %copy-done.1, ...), custom_call_target="tpu_custom_call" | custom-call | flops 268435456 | bytes 6291456 | tf_op jit(solution)/shard_map/attend/pallas_call | solution.py:314
  115.0 3.8 %collective-permute-start.29 = (bf16[256,256]{1,0:T(8,128)(2,1)S(1)}, bf16[256,256]{1,0:T(8,128)(2,1)S(1)}, u32[]{:S(2)}, u32[]{:S(2)}) collective-permute-start(bf16[256,256]{1,0:T(8,128)(2,1)S(1)} %get-tuple-element.103), channel_id=1, source_target_pairs={{0,2},{1,3},{2,0},{3,1},{4,6},{5,7},{6,4},{7,5},{8,10},{9,11},{10,... | collective-permute-start | bytes 393224 | tf_op jit(solution)/shard_map/ppermute | solution.py:61
  119.2 2.0 %collective-permute-done.29.c1 = bf16[256,256]{1,0:T(8,128)(2,1)S(1)} collective-permute-done((bf16[256,256]{1,0:T(8,128)(2,1)S(1)}, bf16[256,256]{1,0:T(8,128)(2,1)S(1)}, u32[]{:S(2)}, u32[]{:S(2)}) %collective-permute-start.29) | collective-permute-done | bytes 131104 | tf_op jit(solution)/shard_map/ppermute | solution.py:61
  121.2 2.0 %collective-permute-done.30.c2 = bf16[256,256]{1,0:T(8,128)(2,1)S(1)} collective-permute-done((bf16[256,256]{1,0:T(8,128)(2,1)S(1)}, bf16[256,256]{1,0:T(8,128)(2,1)S(1)}, u32[]{:S(2)}, u32[]{:S(2)}) %collective-permute-start.30) | collective-permute-done | bytes 131104 | tf_op jit(solution)/shard_map/ppermute | solution.py:61
  123.2 2.0 %collective-permute-done.31.c3 = bf16[256,256]{1,0:T(8,128)(2,1)S(1)} collective-permute-done((bf16[256,256]{1,0:T(8,128)(2,1)S(1)}, bf16[256,256]{1,0:T(8,128)(2,1)S(1)}, u32[]{:S(2)}, u32[]{:S(2)}) %collective-permute-start.31) | collective-permute-done | bytes 131104 | tf_op jit(solution)/shard_map/ppermute | solution.py:61
  125.3 3.4 %outputs.3 = bf16[256,2048]{1,0:T(8,128)(2,1)S(1)} custom-call(s32[8]{0:T(128)S(1)} %stack.35.place, bf16[256,256]{1,0:T(8,128)(2,1)S(1)} %get-tuple-element.102.c0, bf16[256,256]{1,0:T(8,128)(2,1)S(1)} %collective-permute-done.29.c1, bf16[256,256]{1,0:T(8,128)(2,1)S(1)} %collective-permute-done.30.c2, bf16[256,256]{1,0:T(8,128)(2,1)S(1)} %collective-permute-done.31.c3, ...), custom_call_target="tpu_custom_call" | custom-call | flops 1073741824 | bytes 4194304 | tf_op jit(solution)/shard_map/outputs/pallas_call | solution.py:369
  128.7 2.8 %collective-permute-start.35 = (bf16[128,2048]{1,0:T(8,128)(2,1)S(1)}, bf16[128,2048]{1,0:T(8,128)(2,1)S(1)}, u32[]{:S(2)}, u32[]{:S(2)}) collective-permute-start(bf16[128,2048]{1,0:T(8,128)(2,1)S(1)} %slice.43), channel_id=1, source_target_pairs={{0,1},{1,0},{2,3},{3,2},{4,5},{5,4},{6,7},{7,6},{8,9},{9,8},{10,11... | collective-permute-start | bytes 1572872 | tf_op jit(solution)/shard_map/ppermute | solution.py:61
  131.5 3.4 %outputs.2 = bf16[256,2048]{1,0:T(8,128)(2,1)S(1)} custom-call(s32[8]{0:T(128)S(1)} %stack.35.place, bf16[256,256]{1,0:T(8,128)(2,1)S(1)} %get-tuple-element.102.c0, bf16[256,256]{1,0:T(8,128)(2,1)S(1)} %collective-permute-done.29.c1, bf16[256,256]{1,0:T(8,128)(2,1)S(1)} %collective-permute-done.30.c2, bf16[256,256]{1,0:T(8,128)(2,1)S(1)} %collective-permute-done.31.c3, ...), custom_call_target="tpu_custom_call" | custom-call | flops 1073741824 | bytes 4194304 | tf_op jit(solution)/shard_map/outputs/pallas_call | solution.py:369
  135.2 1.8 %collective-permute-done.34 = bf16[128,2048]{1,0:T(8,128)(2,1)S(1)} collective-permute-done((bf16[128,2048]{1,0:T(8,128)(2,1)S(1)}, bf16[128,2048]{1,0:T(8,128)(2,1)S(1)}, u32[]{:S(2)}, u32[]{:S(2)}) %collective-permute-start.34) | collective-permute-done | bytes 524320 | tf_op jit(solution)/shard_map/ppermute | solution.py:61
  137.1 1.2 fusion.5
  (72 shorter events, 5.5 us)
Async XLA Ops:
  0.0 11.3 %copy-start.5 = (bf16[1,128,4096]{2,1,0:T(8,128)(2,1)S(1)}, bf16[1,128,4096]{2,1,0:T(8,128)(2,1)}, u32[]{:S(2)}) copy-start(bf16[1,128,4096]{2,1,0:T(8,128)(2,1)} %param.9) | copy-start | bytes 3145732
  0.0 11.6 %copy-start.7 = (bf16[1,4096]{1,0:T(2,128)(2,1)S(1)}, bf16[1,4096]{1,0:T(2,128)(2,1)}, u32[]{:S(2)}) copy-start(bf16[1,4096]{1,0:T(2,128)(2,1)} %param.11) | copy-start | bytes 24580
  1.2 20.8 %collective-permute-start.4 = (bf16[64,4096]{1,0:T(8,128)(2,1)S(1)}, bf16[64,4096]{1,0:T(8,128)(2,1)S(1)}, u32[]{:S(2)}, u32[]{:S(2)}) collective-permute-start(bf16[64,4096]{1,0:T(8,128)(2,1)S(1)} %dynamic-slice_bitcast_fusion), channel_id=1, source_target_pairs={{0,18},{1,19},{2,16},{3,17},{4,22},{5,23},{6,20},{7,21},{8,26},{9,... | collective-permute-start | bytes 1572872 | tf_op jit(solution)/shard_map/ppermute | solution.py:61
  6.8 8.4 %collective-permute-start.2 = (bf16[1,512,256]{2,1,0:T(8,128)(2,1)S(1)}, bf16[1,512,256]{2,1,0:T(8,128)(2,1)S(1)}, u32[]{:S(2)}, u32[]{:S(2)}) collective-permute-start(bf16[1,512,256]{2,1,0:T(8,128)(2,1)S(1)} %get-tuple-element.116), channel_id=1, source_target_pairs={{0,64},{1,65},{2,66},{3,67},{4,68},{5,69},{6,70},{7,71},{8,72},{9,... | collective-permute-start | bytes 786440 | tf_op jit(solution)/shard_map/ppermute | solution.py:61
  9.5 11.7 %collective-permute-start.1 = (bf16[1,512,256]{2,1,0:T(8,128)(2,1)S(1)}, bf16[1,512,256]{2,1,0:T(8,128)(2,1)S(1)}, u32[]{:S(2)}, u32[]{:S(2)}) collective-permute-start(bf16[1,512,256]{2,1,0:T(8,128)(2,1)S(1)} %get-tuple-element.117), channel_id=1, source_target_pairs={{0,96},{1,97},{2,98},{3,99},{4,100},{5,101},{6,102},{7,103},{8,104... | collective-permute-start | bytes 786440 | tf_op jit(solution)/shard_map/ppermute | solution.py:61
  10.4 11.2 %collective-permute-start = (bf16[1,512,256]{2,1,0:T(8,128)(2,1)S(1)}, bf16[1,512,256]{2,1,0:T(8,128)(2,1)S(1)}, u32[]{:S(2)}, u32[]{:S(2)}) collective-permute-start(bf16[1,512,256]{2,1,0:T(8,128)(2,1)S(1)} %get-tuple-element.118), channel_id=1, source_target_pairs={{0,32},{1,33},{2,34},{3,35},{4,36},{5,37},{6,38},{7,39},{8,40},{9,... | collective-permute-start | bytes 786440 | tf_op jit(solution)/shard_map/ppermute | solution.py:61
  11.0 10.6 %collective-permute-start.3 = (bf16[1,512,256]{2,1,0:T(8,128)(2,1)}, bf16[1,512,256]{2,1,0:T(8,128)(2,1)S(1)}, u32[]{:S(2)}, u32[]{:S(2)}) collective-permute-start(bf16[1,512,256]{2,1,0:T(8,128)(2,1)} %get-tuple-element.115.refs_0_), channel_id=1, source_target_pairs={{0,2},{1,3},{2,0},{3,1},{4,6},{5,7},{6,4},{7,5},{8,10},{9,11},{10,... | collective-permute-start | bytes 786440 | tf_op jit(solution)/shard_map/ppermute | solution.py:61
  21.6 5.6 %copy-start.2 = (bf16[1,512,256]{2,1,0:T(8,128)(2,1)}, bf16[1,512,256]{2,1,0:T(8,128)(2,1)S(1)}, u32[]{:S(2)}) copy-start(bf16[1,512,256]{2,1,0:T(8,128)(2,1)S(1)} %collective-permute-done.3.refs_2_) | copy-start | bytes 786436
  21.9 7.6 %collective-permute-start.11 = (bf16[128,4096]{1,0:T(8,128)(2,1)S(1)}, bf16[128,4096]{1,0:T(8,128)(2,1)}, u32[]{:S(2)}, u32[]{:S(2)}) collective-permute-start(bf16[128,4096]{1,0:T(8,128)(2,1)S(1)} %fusion.4.h0), channel_id=1, source_target_pairs={{0,1},{1,0},{2,3},{3,2},{4,5},{5,4},{6,7},{7,6},{8,9},{9,8},{10,11... | collective-permute-start | bytes 3145736 | tf_op jit(solution)/shard_map/ppermute | solution.py:61
  23.3 15.1 %collective-permute-start.10 = (bf16[64,4096]{1,0:T(8,128)(2,1)S(1)}, bf16[64,4096]{1,0:T(8,128)(2,1)S(1)}, u32[]{:S(2)}, u32[]{:S(2)}) collective-permute-start(bf16[64,4096]{1,0:T(8,128)(2,1)S(1)} %collective-permute-done.4.refs_0_), channel_id=1, source_target_pairs={{0,12},{1,13},{2,14},{3,15},{4,0},{5,1},{6,2},{7,3},{8,4},{9,5},{1... | collective-permute-start | bytes 1572872 | tf_op jit(solution)/shard_map/ppermute | solution.py:61
  27.1 14.6 %collective-permute-start.9 = (bf16[64,4096]{1,0:T(8,128)(2,1)S(1)}, bf16[64,4096]{1,0:T(8,128)(2,1)S(1)}, u32[]{:S(2)}, u32[]{:S(2)}) collective-permute-start(bf16[64,4096]{1,0:T(8,128)(2,1)S(1)} %collective-permute-done.4.refs_0_), channel_id=1, source_target_pairs={{0,4},{1,5},{2,6},{3,7},{4,8},{5,9},{6,10},{7,11},{8,12},{9,13},{1... | collective-permute-start | bytes 1572872 | tf_op jit(solution)/shard_map/ppermute | solution.py:61
  27.2 24.5 %collective-permute-start.5 = (bf16[3,512,256]{2,1,0:T(8,128)(2,1)S(1)}, bf16[3,512,256]{2,1,0:T(8,128)(2,1)}, u32[]{:S(2)}, u32[]{:S(2)}) collective-permute-start(bf16[3,512,256]{2,1,0:T(8,128)(2,1)S(1)} %constant_dynamic-update-slice_fusion.refs_0_), channel_id=1, source_target_pairs={{0,2},{1,3},{2,0},{3,1},{4,6},{5,7},{6,4},{7,5},{8,10},{9,11},{10,... | collective-permute-start | bytes 2359304 | tf_op jit(solution)/shard_map/ppermute | solution.py:61
  28.9 15.6 %collective-permute-start.7 = (bf16[1,512,256]{2,1,0:T(8,128)(2,1)}, bf16[1,512,256]{2,1,0:T(8,128)(2,1)}, u32[]{:S(2)}, u32[]{:S(2)}) collective-permute-start(bf16[1,512,256]{2,1,0:T(8,128)(2,1)} %get-tuple-element.115.refs_0_), channel_id=1, source_target_pairs={{0,1},{1,0},{2,3},{3,2},{4,5},{5,4},{6,7},{7,6},{8,9},{9,8},{10,11... | collective-permute-start | bytes 786440 | tf_op jit(solution)/shard_map/ppermute | solution.py:61
  29.5 15.1 %collective-permute-start.8 = (bf16[1,512,256]{2,1,0:T(8,128)(2,1)}, bf16[1,512,256]{2,1,0:T(8,128)(2,1)S(1)}, u32[]{:S(2)}, u32[]{:S(2)}) collective-permute-start(bf16[1,512,256]{2,1,0:T(8,128)(2,1)} %copy-done.2), channel_id=1, source_target_pairs={{0,1},{1,0},{2,3},{3,2},{4,5},{5,4},{6,7},{7,6},{8,9},{9,8},{10,11... | collective-permute-start | bytes 786440 | tf_op jit(solution)/shard_map/ppermute | solution.py:61
  33.7 10.8 %copy-start.4 = (s32[1,512]{1,0:T(1,128)S(1)}, s32[1,512]{1,0:T(1,128)}, u32[]{:S(2)}) copy-start(s32[1,512]{1,0:T(1,128)} %param.16) | copy-start | bytes 6148
  33.7 12.8 %copy-start.3 = (bf16[1,512,256]{2,1,0:T(8,128)(2,1)S(1)}, bf16[1,512,256]{2,1,0:T(8,128)(2,1)}, u32[]{:S(2)}) copy-start(bf16[1,512,256]{2,1,0:T(8,128)(2,1)} %copy-done.2) | copy-start | bytes 786436
  41.7 10.0 %collective-permute-start.13 = (bf16[32,4096]{1,0:T(8,128)(2,1)S(1)}, bf16[32,4096]{1,0:T(8,128)(2,1)S(1)}, u32[]{:S(2)}, u32[]{:S(2)}) collective-permute-start(bf16[32,4096]{1,0:T(8,128)(2,1)S(1)} %slice.31), channel_id=1, source_target_pairs={{0,12},{1,13},{2,14},{3,15},{4,0},{5,1},{6,2},{7,3},{8,4},{9,5},{1... | collective-permute-start | bytes 786440 | tf_op jit(solution)/shard_map/ppermute | solution.py:61
  42.1 9.6 %collective-permute-start.12 = (bf16[32,4096]{1,0:T(8,128)(2,1)S(1)}, bf16[32,4096]{1,0:T(8,128)(2,1)S(1)}, u32[]{:S(2)}, u32[]{:S(2)}) collective-permute-start(bf16[32,4096]{1,0:T(8,128)(2,1)S(1)} %slice.30), channel_id=1, source_target_pairs={{0,4},{1,5},{2,6},{3,7},{4,8},{5,9},{6,10},{7,11},{8,12},{9,13},{1... | collective-permute-start | bytes 786440 | tf_op jit(solution)/shard_map/ppermute | solution.py:61
  44.5 7.2 %collective-permute-start.6 = (s32[4,128]{1,0:T(4,128)S(1)}, s32[4,128]{1,0:T(4,128)S(1)}, u32[]{:S(2)}, u32[]{:S(2)}) collective-permute-start(s32[4,128]{1,0:T(4,128)S(1)} %bitcast.40), channel_id=1, source_target_pairs={{0,16},{1,17},{2,18},{3,19},{4,20},{5,21},{6,22},{7,23},{8,24},{9,... | collective-permute-start | bytes 6152 | tf_op jit(solution)/shard_map/ppermute | solution.py:61
  44.6 10.1 %collective-permute-start.14 = (bf16[3,512,256]{2,1,0:T(8,128)(2,1)S(1)}, bf16[3,512,256]{2,1,0:T(8,128)(2,1)S(1)}, u32[]{:S(2)}, u32[]{:S(2)}) collective-permute-start(bf16[3,512,256]{2,1,0:T(8,128)(2,1)S(1)} %constant_dynamic-update-slice_fusion.refs_0_), channel_id=1, source_target_pairs={{0,1},{1,0},{2,3},{3,2},{4,5},{5,4},{6,7},{7,6},{8,9},{9,8},{10,11... | collective-permute-start | bytes 2359304 | tf_op jit(solution)/shard_map/ppermute | solution.py:61
  50.3 1.3 copy-start
  51.7 3.0 %collective-permute-start.15 = (bf16[3,512,256]{2,1,0:T(8,128)(2,1)}, bf16[3,512,256]{2,1,0:T(8,128)(2,1)S(1)}, u32[]{:S(2)}, u32[]{:S(2)}) collective-permute-start(bf16[3,512,256]{2,1,0:T(8,128)(2,1)} %collective-permute-done.5.refs_2_), channel_id=1, source_target_pairs={{0,1},{1,0},{2,3},{3,2},{4,5},{5,4},{6,7},{7,6},{8,9},{9,8},{10,11... | collective-permute-start | bytes 2359304 | tf_op jit(solution)/shard_map/ppermute | solution.py:61
  52.0 26.1 %collective-permute-start.19 = (bf16[128,4096]{1,0:T(8,128)(2,1)S(1)}, bf16[128,4096]{1,0:T(8,128)(2,1)S(1)}, u32[]{:S(2)}, u32[]{:S(2)}) collective-permute-start(bf16[128,4096]{1,0:T(8,128)(2,1)S(1)} %fusion.4.h0), channel_id=1, source_target_pairs={{0,18},{1,19},{2,16},{3,17},{4,22},{5,23},{6,20},{7,21},{8,26},{9,... | collective-permute-start | bytes 3145736 | tf_op jit(solution)/shard_map/ppermute | solution.py:61
  62.1 16.0 %collective-permute-start.16 = (bf16[2,512,256]{2,1,0:T(8,128)(2,1)S(1)}, bf16[2,512,256]{2,1,0:T(8,128)(2,1)S(1)}, u32[]{:S(2)}, u32[]{:S(2)}) collective-permute-start(bf16[2,512,256]{2,1,0:T(8,128)(2,1)S(1)} %get-tuple-element.78), channel_id=1, source_target_pairs={{0,16},{1,17},{2,18},{3,19},{4,20},{5,21},{6,22},{7,23},{8,24},{9,... | collective-permute-start | bytes 1572872 | tf_op jit(solution)/shard_map/ppermute | solution.py:61
  63.2 14.9 %collective-permute-start.18 = (bf16[2,512,256]{2,1,0:T(8,128)(2,1)S(1)}, bf16[2,512,256]{2,1,0:T(8,128)(2,1)S(1)}, u32[]{:S(2)}, u32[]{:S(2)}) collective-permute-start(bf16[2,512,256]{2,1,0:T(8,128)(2,1)S(1)} %get-tuple-element.79.refs_7_), channel_id=1, source_target_pairs={{0,12},{1,13},{2,14},{3,15},{4,0},{5,1},{6,2},{7,3},{8,4},{9,5},{1... | collective-permute-start | bytes 1572872 | tf_op jit(solution)/shard_map/ppermute | solution.py:61
  64.4 13.7 %collective-permute-start.17 = (bf16[2,512,256]{2,1,0:T(8,128)(2,1)S(1)}, bf16[2,512,256]{2,1,0:T(8,128)(2,1)S(1)}, u32[]{:S(2)}, u32[]{:S(2)}) collective-permute-start(bf16[2,512,256]{2,1,0:T(8,128)(2,1)S(1)} %get-tuple-element.79.refs_7_), channel_id=1, source_target_pairs={{0,4},{1,5},{2,6},{3,7},{4,8},{5,9},{6,10},{7,11},{8,12},{9,13},{1... | collective-permute-start | bytes 1572872 | tf_op jit(solution)/shard_map/ppermute | solution.py:61
  64.6 13.5 %collective-permute-start.20 = (bf16[256,256]{1,0:T(8,128)(2,1)S(1)}, bf16[256,256]{1,0:T(8,128)(2,1)S(1)}, u32[]{:S(2)}, u32[]{:S(2)}) collective-permute-start(bf16[256,256]{1,0:T(8,128)(2,1)S(1)} %get-tuple-element.83), channel_id=1, source_target_pairs={{0,16},{1,17},{2,18},{3,19},{4,20},{5,21},{6,22},{7,23},{8,24},{9,... | collective-permute-start | bytes 393224 | tf_op jit(solution)/shard_map/ppermute | solution.py:61
  78.1 6.6 %collective-permute-start.23 = (bf16[128,4096]{1,0:T(8,128)(2,1)S(1)}, bf16[128,4096]{1,0:T(8,128)(2,1)S(1)}, u32[]{:S(2)}, u32[]{:S(2)}) collective-permute-start(bf16[128,4096]{1,0:T(8,128)(2,1)S(1)} %collective-permute-done.19.h0), channel_id=1, source_target_pairs={{0,1},{1,0},{2,3},{3,2},{4,5},{5,4},{6,7},{7,6},{8,9},{9,8},{10,11... | collective-permute-start | bytes 3145736 | tf_op jit(solution)/shard_map/ppermute | solution.py:61
  79.9 15.9 %collective-permute-start.22 = (bf16[2,512,256]{2,1,0:T(8,128)(2,1)S(1)}, bf16[2,512,256]{2,1,0:T(8,128)(2,1)S(1)}, u32[]{:S(2)}, u32[]{:S(2)}) collective-permute-start(bf16[2,512,256]{2,1,0:T(8,128)(2,1)S(1)} %collective-permute-done.16.refs_10_), channel_id=1, source_target_pairs={{0,12},{1,13},{2,14},{3,15},{4,0},{5,1},{6,2},{7,3},{8,4},{9,5},{1... | collective-permute-start | bytes 1572872 | tf_op jit(solution)/shard_map/ppermute | solution.py:61
  80.4 15.4 %collective-permute-start.21 = (bf16[2,512,256]{2,1,0:T(8,128)(2,1)S(1)}, bf16[2,512,256]{2,1,0:T(8,128)(2,1)S(1)}, u32[]{:S(2)}, u32[]{:S(2)}) collective-permute-start(bf16[2,512,256]{2,1,0:T(8,128)(2,1)S(1)} %collective-permute-done.16.refs_10_), channel_id=1, source_target_pairs={{0,4},{1,5},{2,6},{3,7},{4,8},{5,9},{6,10},{7,11},{8,12},{9,13},{1... | collective-permute-start | bytes 1572872 | tf_op jit(solution)/shard_map/ppermute | solution.py:61
  81.4 12.9 %collective-permute-start.25 = (bf16[64,4096]{1,0:T(8,128)(2,1)S(1)}, bf16[64,4096]{1,0:T(8,128)(2,1)S(1)}, u32[]{:S(2)}, u32[]{:S(2)}) collective-permute-start(bf16[64,4096]{1,0:T(8,128)(2,1)S(1)} %collective-permute-done.4.refs_0_), channel_id=1, source_target_pairs={{0,16},{1,17},{2,18},{3,19},{4,20},{5,21},{6,22},{7,23},{8,24},{9,... | collective-permute-start | bytes 1572872 | tf_op jit(solution)/shard_map/ppermute | solution.py:61
  82.1 13.7 %collective-permute-start.26 = (bf16[64,4096]{1,0:T(8,128)(2,1)S(1)}, bf16[64,4096]{1,0:T(8,128)(2,1)S(1)}, u32[]{:S(2)}, u32[]{:S(2)}) collective-permute-start(bf16[64,4096]{1,0:T(8,128)(2,1)S(1)} %get-tuple-element.89), channel_id=1, source_target_pairs={{0,18},{1,19},{2,16},{3,17},{4,22},{5,23},{6,20},{7,21},{8,26},{9,... | collective-permute-start | bytes 1572872 | tf_op jit(solution)/shard_map/ppermute | solution.py:61
  88.1 15.1 %copy-start.1 = (s32[1,4096]{1,0:T(1,128)S(1)}, s32[1,4096]{1,0:T(1,128)}, u32[]{:S(2)}) copy-start(s32[1,4096]{1,0:T(1,128)} %refs_2_.3) | copy-start | bytes 49156
  88.1 9.0 %collective-permute-start.24 = (bf16[256,256]{1,0:T(8,128)(2,1)S(1)}, bf16[256,256]{1,0:T(8,128)(2,1)S(1)}, u32[]{:S(2)}, u32[]{:S(2)}) collective-permute-start(bf16[256,256]{1,0:T(8,128)(2,1)S(1)} %get-tuple-element.87), channel_id=1, source_target_pairs={{0,16},{1,17},{2,18},{3,19},{4,20},{5,21},{6,22},{7,23},{8,24},{9,... | collective-permute-start | bytes 393224 | tf_op jit(solution)/shard_map/ppermute | solution.py:61
  97.2 12.1 %collective-permute-start.28 = (bf16[1024,256]{1,0:T(8,128)(2,1)S(1)}, bf16[1024,256]{1,0:T(8,128)(2,1)S(1)}, u32[]{:S(2)}, u32[]{:S(2)}) collective-permute-start(bf16[1024,256]{1,0:T(8,128)(2,1)S(1)} %pad_maximum_fusion.1), channel_id=1, source_target_pairs={{0,12},{1,13},{2,14},{3,15},{4,0},{5,1},{6,2},{7,3},{8,4},{9,5},{1... | collective-permute-start | bytes 1572872 | tf_op jit(solution)/shard_map/ppermute | solution.py:61
  99.0 12.9 %collective-permute-start.27 = (bf16[1024,256]{1,0:T(8,128)(2,1)S(1)}, bf16[1024,256]{1,0:T(8,128)(2,1)S(1)}, u32[]{:S(2)}, u32[]{:S(2)}) collective-permute-start(bf16[1024,256]{1,0:T(8,128)(2,1)S(1)} %pad_maximum_fusion), channel_id=1, source_target_pairs={{0,4},{1,5},{2,6},{3,7},{4,8},{5,9},{6,10},{7,11},{8,12},{9,13},{1... | collective-permute-start | bytes 1572872 | tf_op jit(solution)/shard_map/ppermute | solution.py:61
  99.1 20.2 %collective-permute-start.32 = (bf16[64,4096]{1,0:T(8,128)(2,1)S(1)}, bf16[64,4096]{1,0:T(8,128)(2,1)S(1)}, u32[]{:S(2)}, u32[]{:S(2)}) collective-permute-start(bf16[64,4096]{1,0:T(8,128)(2,1)S(1)} %collective-permute-done.9.refs_1_), channel_id=1, source_target_pairs={{0,16},{1,17},{2,18},{3,19},{4,20},{5,21},{6,22},{7,23},{8,24},{9,... | collective-permute-start | bytes 1572872 | tf_op jit(solution)/shard_map/ppermute | solution.py:61
  100.5 18.7 %collective-permute-start.33 = (bf16[64,4096]{1,0:T(8,128)(2,1)S(1)}, bf16[64,4096]{1,0:T(8,128)(2,1)S(1)}, u32[]{:S(2)}, u32[]{:S(2)}) collective-permute-start(bf16[64,4096]{1,0:T(8,128)(2,1)S(1)} %get-tuple-element.112), channel_id=1, source_target_pairs={{0,18},{1,19},{2,16},{3,17},{4,22},{5,23},{6,20},{7,21},{8,26},{9,... | collective-permute-start | bytes 1572872 | tf_op jit(solution)/shard_map/ppermute | solution.py:61
  115.0 6.2 %collective-permute-start.29 = (bf16[256,256]{1,0:T(8,128)(2,1)S(1)}, bf16[256,256]{1,0:T(8,128)(2,1)S(1)}, u32[]{:S(2)}, u32[]{:S(2)}) collective-permute-start(bf16[256,256]{1,0:T(8,128)(2,1)S(1)} %get-tuple-element.103), channel_id=1, source_target_pairs={{0,2},{1,3},{2,0},{3,1},{4,6},{5,7},{6,4},{7,5},{8,10},{9,11},{10,... | collective-permute-start | bytes 393224 | tf_op jit(solution)/shard_map/ppermute | solution.py:61
  118.8 4.4 %collective-permute-start.30 = (bf16[256,256]{1,0:T(8,128)(2,1)S(1)}, bf16[256,256]{1,0:T(8,128)(2,1)S(1)}, u32[]{:S(2)}, u32[]{:S(2)}) collective-permute-start(bf16[256,256]{1,0:T(8,128)(2,1)S(1)} %get-tuple-element.104), channel_id=1, source_target_pairs={{0,16},{1,17},{2,18},{3,19},{4,20},{5,21},{6,22},{7,23},{8,24},{9,... | collective-permute-start | bytes 393224 | tf_op jit(solution)/shard_map/ppermute | solution.py:61
  118.8 6.4 %collective-permute-start.31 = (bf16[256,256]{1,0:T(8,128)(2,1)S(1)}, bf16[256,256]{1,0:T(8,128)(2,1)S(1)}, u32[]{:S(2)}, u32[]{:S(2)}) collective-permute-start(bf16[256,256]{1,0:T(8,128)(2,1)S(1)} %get-tuple-element.105), channel_id=1, source_target_pairs={{0,18},{1,19},{2,16},{3,17},{4,22},{5,23},{6,20},{7,21},{8,26},{9,... | collective-permute-start | bytes 393224 | tf_op jit(solution)/shard_map/ppermute | solution.py:61
  128.7 6.4 %collective-permute-start.35 = (bf16[128,2048]{1,0:T(8,128)(2,1)S(1)}, bf16[128,2048]{1,0:T(8,128)(2,1)S(1)}, u32[]{:S(2)}, u32[]{:S(2)}) collective-permute-start(bf16[128,2048]{1,0:T(8,128)(2,1)S(1)} %slice.43), channel_id=1, source_target_pairs={{0,1},{1,0},{2,3},{3,2},{4,5},{5,4},{6,7},{7,6},{8,9},{9,8},{10,11... | collective-permute-start | bytes 1572872 | tf_op jit(solution)/shard_map/ppermute | solution.py:61
  135.0 2.1 %copy-start.6 = (bf16[1,128,4096]{2,1,0:T(8,128)(2,1)S(1)}, bf16[1,128,4096]{2,1,0:T(8,128)(2,1)}, u32[]{:S(2)}) copy-start(bf16[1,128,4096]{2,1,0:T(8,128)(2,1)} %param.9) | copy-start | bytes 3145732
  135.0 2.0 %collective-permute-start.34 = (bf16[128,2048]{1,0:T(8,128)(2,1)S(1)}, bf16[128,2048]{1,0:T(8,128)(2,1)S(1)}, u32[]{:S(2)}, u32[]{:S(2)}) collective-permute-start(bf16[128,2048]{1,0:T(8,128)(2,1)S(1)} %slice.41), channel_id=1, source_target_pairs={{0,1},{1,0},{2,3},{3,2},{4,5},{5,4},{6,7},{7,6},{8,9},{9,8},{10,11... | collective-permute-start | bytes 1572872 | tf_op jit(solution)/shard_map/ppermute | solution.py:61

commit v6 on v5

--- a/solution.py
+++ b/solution.py
@@ -11,7 +11,7 @@
 HD = 256
 AXES = ("section", "seq", "mp")
 SHAPE = (4, 2, 4, 2, 2)
-KEYS = 256
+KEYS = 512
 ATTEND_ROWS = 512
 MIB = 1 << 20
 F32 = jnp.float32

time: 139 us -> 138 us (level)
  Pallas kernels: 34.4 us -> 30.5 us
  waiting for transfers between devices: 50.2 us -> 53.1 us
    pallas_call x2, Pallas kernels: 9.06 us -> 5.1 us  [attend(): pl.pallas_call(functools.partial(attend_kernel, pieces, keys, bool(before...]
    ppermute x36, waiting for transfers between devices: 50.2 us -> 53.1 us  [send(): return lax.ppermute(array, AXES, pairs)]
  transfers between devices with their start and end apart: 36 -> 36, of which waited for: 16 -> 16; matrix products, arithmetic and copies ran while one was open for 3% -> 3% of each run, Pallas kernels for 22% -> 20%
where the time goes in v6:
time: 138 us; the launch traced here: 137 us
  waiting for transfers between devices  53.1 us (38%)
  starting transfers between devices  45.1 us (33%)
  Pallas kernels  30.5 us (22%)
  local copies, waits for them, and re-layouts  6.07 us (4%)
  other arithmetic  2.13 us (2%)
    ppermute x36, waiting for transfers between devices, send(): return lax.ppermute(array, AXES, pairs)  53.1 us
    ppermute x36, starting transfers between devices, send(): return lax.ppermute(array, AXES, pairs)  45.1 us
    pallas_call x2, Pallas kernels, key_values(): pl.pallas_call(functools.partial(key_value_kernel, steps), out_shape=(out...  11.2 us
    pallas_call x2, Pallas kernels, queries(): pl.pallas_call(query_kernel, out_shape=(out, out), in_specs=smem(1) + vme...  7.35 us
    pallas_call x2, Pallas kernels, outputs(): pl.pallas_call(functools.partial(output_kernel, part * width), out_shape=...  6.79 us
    pallas_call x2, Pallas kernels, attend(): pl.pallas_call(functools.partial(attend_kernel, pieces, keys, bool(before...  5.1 us
  transfers between devices with their start and end apart: 36, of which 16 were waited for; matrix products, arithmetic and copies ran while one was open for 3% of the time, Pallas kernels for 20%

profile of v6, /device:TPU:1, one launch (start us, length us, event | category | flops | bytes accessed | tf_op | source)
XLA Modules:
  0.0 137.2 jit_solution(95168254072039109)
XLA Ops:
  0.0 1.2 dynamic-slice_bitcast_fusion
  1.2 3.6 %collective-permute-start.4 = (bf16[64,4096]{1,0:T(8,128)(2,1)S(1)}, bf16[64,4096]{1,0:T(8,128)(2,1)S(1)}, u32[]{:S(2)}, u32[]{:S(2)}) collective-permute-start(bf16[64,4096]{1,0:T(8,128)(2,1)S(1)} %dynamic-slice_bitcast_fusion), channel_id=1, source_target_pairs={{0,18},{1,19},{2,16},{3,17},{4,22},{5,23},{6,20},{7,21},{8,26},{9,... | collective-permute-start | bytes 1572872 | tf_op jit(solution)/shard_map/ppermute | solution.py:61
  4.8 2.0 %constant_dynamic-slice_fusion.2 = (bf16[1,512,256]{2,1,0:T(8,128)(2,1)}, bf16[1,512,256]{2,1,0:T(8,128)(2,1)S(1)}, bf16[1,512,256]{2,1,0:T(8,128)(2,1)S(1)}, bf16[1,512,256]{2,1,0:T(8,128)(2,1)S(1)}) fusion(bf16[4,512,256]{2,1,0:T(8,128)(2,1)} %param.10, s32[]{:T(128)S(6)} %select_n.82, s32[]{:T(128)S(6)} %select_n.81, s32[]{:T(128)S(6)} %select_n.80, ...), kind=kLoop, calls=%fused_computation.22 | loop fusion | bytes 2097168 | tf_op jit(solution)/shard_map/dynamic_slice | solution.py:408
  6.8 2.7 %collective-permute-start.2 = (bf16[1,512,256]{2,1,0:T(8,128)(2,1)S(1)}, bf16[1,512,256]{2,1,0:T(8,128)(2,1)S(1)}, u32[]{:S(2)}, u32[]{:S(2)}) collective-permute-start(bf16[1,512,256]{2,1,0:T(8,128)(2,1)S(1)} %get-tuple-element.116), channel_id=1, source_target_pairs={{0,64},{1,65},{2,66},{3,67},{4,68},{5,69},{6,70},{7,71},{8,72},{9,... | collective-permute-start | bytes 786440 | tf_op jit(solution)/shard_map/ppermute | solution.py:61
  9.5 0.9 collective-permute-start.1
  10.4 0.6 collective-permute-start
  12.0 3.1 %collective-permute-done.2 = bf16[1,512,256]{2,1,0:T(8,128)(2,1)S(1)} collective-permute-done((bf16[1,512,256]{2,1,0:T(8,128)(2,1)S(1)}, bf16[1,512,256]{2,1,0:T(8,128)(2,1)S(1)}, u32[]{:S(2)}, u32[]{:S(2)}) %collective-permute-start.2) | collective-permute-done | bytes 262176 | tf_op jit(solution)/shard_map/ppermute | solution.py:61
  15.1 6.1 %collective-permute-done.1 = bf16[1,512,256]{2,1,0:T(8,128)(2,1)S(1)} collective-permute-done((bf16[1,512,256]{2,1,0:T(8,128)(2,1)S(1)}, bf16[1,512,256]{2,1,0:T(8,128)(2,1)S(1)}, u32[]{:S(2)}, u32[]{:S(2)}) %collective-permute-start.1) | collective-permute-done | bytes 262176 | tf_op jit(solution)/shard_map/ppermute | solution.py:61
  21.9 1.4 %collective-permute-start.11 = (bf16[128,4096]{1,0:T(8,128)(2,1)S(1)}, bf16[128,4096]{1,0:T(8,128)(2,1)}, u32[]{:S(2)}, u32[]{:S(2)}) collective-permute-start(bf16[128,4096]{1,0:T(8,128)(2,1)S(1)} %fusion.4.h0), channel_id=1, source_target_pairs={{0,1},{1,0},{2,3},{3,2},{4,5},{5,4},{6,7},{7,6},{8,9},{9,8},{10,11... | collective-permute-start | bytes 3145736 | tf_op jit(solution)/shard_map/ppermute | solution.py:61
  23.3 3.8 %collective-permute-start.10 = (bf16[64,4096]{1,0:T(8,128)(2,1)S(1)}, bf16[64,4096]{1,0:T(8,128)(2,1)S(1)}, u32[]{:S(2)}, u32[]{:S(2)}) collective-permute-start(bf16[64,4096]{1,0:T(8,128)(2,1)S(1)} %collective-permute-done.4.refs_0_), channel_id=1, source_target_pairs={{0,12},{1,13},{2,14},{3,15},{4,0},{5,1},{6,2},{7,3},{8,4},{9,5},{1... | collective-permute-start | bytes 1572872 | tf_op jit(solution)/shard_map/ppermute | solution.py:61
  27.2 1.7 %collective-permute-start.5 = (bf16[3,512,256]{2,1,0:T(8,128)(2,1)S(1)}, bf16[3,512,256]{2,1,0:T(8,128)(2,1)}, u32[]{:S(2)}, u32[]{:S(2)}) collective-permute-start(bf16[3,512,256]{2,1,0:T(8,128)(2,1)S(1)} %constant_dynamic-update-slice_fusion.refs_0_), channel_id=1, source_target_pairs={{0,2},{1,3},{2,0},{3,1},{4,6},{5,7},{6,4},{7,5},{8,10},{9,11},{10,... | collective-permute-start | bytes 2359304 | tf_op jit(solution)/shard_map/ppermute | solution.py:61
  29.6 4.0 %queries.2 = (bf16[256,256]{1,0:T(8,128)(2,1)S(1)}, bf16[256,256]{1,0:T(8,128)(2,1)S(1)}) custom-call(s32[8]{0:T(128)S(1)} %stack.35.place, bf16[128,4096]{1,0:T(8,128)(2,1)S(1)} %fusion.4.h0, bf16[128,4096]{1,0:T(8,128)(2,1)} %collective-permute-done.11.h1, bf16[4096,512]{1,0:T(8,128)(2,1)} %bitcast.48), custom_call_target="tpu_custom_call" | custom-call | flops 1073741824 | bytes 8388608 | tf_op jit(solution)/shard_map/queries/pallas_call | solution.py:201
  33.7 4.7 %collective-permute-done.10.refs_2_ = bf16[64,4096]{1,0:T(8,128)(2,1)S(1)} collective-permute-done((bf16[64,4096]{1,0:T(8,128)(2,1)S(1)}, bf16[64,4096]{1,0:T(8,128)(2,1)S(1)}, u32[]{:S(2)}, u32[]{:S(2)}) %collective-permute-start.10) | collective-permute-done | bytes 524320 | tf_op jit(solution)/shard_map/ppermute | solution.py:61
  38.4 3.2 %collective-permute-done.9.refs_1_ = bf16[64,4096]{1,0:T(8,128)(2,1)S(1)} collective-permute-done((bf16[64,4096]{1,0:T(8,128)(2,1)S(1)}, bf16[64,4096]{1,0:T(8,128)(2,1)S(1)}, u32[]{:S(2)}, u32[]{:S(2)}) %collective-permute-start.9) | collective-permute-done | bytes 524320 | tf_op jit(solution)/shard_map/ppermute | solution.py:61
  42.1 1.1 collective-permute-start.12
  43.2 1.3 constant_dynamic-slice_fusion
  44.6 1.8 %collective-permute-start.14 = (bf16[3,512,256]{2,1,0:T(8,128)(2,1)S(1)}, bf16[3,512,256]{2,1,0:T(8,128)(2,1)S(1)}, u32[]{:S(2)}, u32[]{:S(2)}) collective-permute-start(bf16[3,512,256]{2,1,0:T(8,128)(2,1)S(1)} %constant_dynamic-update-slice_fusion.refs_0_), channel_id=1, source_target_pairs={{0,1},{1,0},{2,3},{3,2},{4,5},{5,4},{6,7},{7,6},{8,9},{9,8},{10,11... | collective-permute-start | bytes 2359304 | tf_op jit(solution)/shard_map/ppermute | solution.py:61
  46.4 3.9 %key_values.2.refs_6_ = f32[2,512,512]{2,1,0:T(8,128)S(1)} custom-call(s32[8]{0:T(128)S(1)} %stack.35.place, bf16[1,512,256]{2,1,0:T(8,128)(2,1)} %get-tuple-element.115.refs_0_, bf16[1,512,256]{2,1,0:T(8,128)(2,1)} %collective-permute-done.7.refs_1_, bf16[1,512,256]{2,1,0:T(8,128)(2,1)S(1)} %copy-done.3, ...), custom_call_target="tpu_custom_call" | custom-call | flops 1073741824 | bytes 3145728 | tf_op jit(solution)/shard_map/key_values/pallas_call | solution.py:158
  50.3 1.3 copy-done
  52.0 2.7 %collective-permute-start.19 = (bf16[128,4096]{1,0:T(8,128)(2,1)S(1)}, bf16[128,4096]{1,0:T(8,128)(2,1)S(1)}, u32[]{:S(2)}, u32[]{:S(2)}) collective-permute-start(bf16[128,4096]{1,0:T(8,128)(2,1)S(1)} %fusion.4.h0), channel_id=1, source_target_pairs={{0,18},{1,19},{2,16},{3,17},{4,22},{5,23},{6,20},{7,21},{8,26},{9,... | collective-permute-start | bytes 3145736 | tf_op jit(solution)/shard_map/ppermute | solution.py:61
  54.7 7.4 %key_values.3 = (bf16[2,512,256]{2,1,0:T(8,128)(2,1)S(1)}, bf16[2,512,256]{2,1,0:T(8,128)(2,1)S(1)}) custom-call(s32[8]{0:T(128)S(1)} %stack.35.place, bf16[3,512,256]{2,1,0:T(8,128)(2,1)S(1)} %constant_dynamic-update-slice_fusion.refs_0_, bf16[3,512,256]{2,1,0:T(8,128)(2,1)S(1)} %collective-permute-done.14.refs_1_, ...), custom_call_target="tpu_custom_call" | custom-call | flops 3221225472 | bytes 9437184 | tf_op jit(solution)/shard_map/key_values/pallas_call | solution.py:158
  62.1 1.1 collective-permute-start.16
  63.2 1.2 collective-permute-start.18
  65.1 13.0 %collective-permute-done.20.refs_5_ = bf16[256,256]{1,0:T(8,128)(2,1)S(1)} collective-permute-done((bf16[256,256]{1,0:T(8,128)(2,1)S(1)}, bf16[256,256]{1,0:T(8,128)(2,1)S(1)}, u32[]{:S(2)}, u32[]{:S(2)}) %collective-permute-start.20) | collective-permute-done | bytes 131104 | tf_op jit(solution)/shard_map/ppermute | solution.py:61
  78.1 1.8 %collective-permute-start.23 = (bf16[128,4096]{1,0:T(8,128)(2,1)S(1)}, bf16[128,4096]{1,0:T(8,128)(2,1)S(1)}, u32[]{:S(2)}, u32[]{:S(2)}) collective-permute-start(bf16[128,4096]{1,0:T(8,128)(2,1)S(1)} %collective-permute-done.19.h0), channel_id=1, source_target_pairs={{0,1},{1,0},{2,3},{3,2},{4,5},{5,4},{6,7},{7,6},{8,9},{9,8},{10,11... | collective-permute-start | bytes 3145736 | tf_op jit(solution)/shard_map/ppermute | solution.py:61
  80.4 0.9 collective-permute-start.21
  81.4 0.7 collective-permute-start.25
  82.1 2.7 %collective-permute-start.26 = (bf16[64,4096]{1,0:T(8,128)(2,1)S(1)}, bf16[64,4096]{1,0:T(8,128)(2,1)S(1)}, u32[]{:S(2)}, u32[]{:S(2)}) collective-permute-start(bf16[64,4096]{1,0:T(8,128)(2,1)S(1)} %get-tuple-element.89), channel_id=1, source_target_pairs={{0,18},{1,19},{2,16},{3,17},{4,22},{5,23},{6,20},{7,21},{8,26},{9,... | collective-permute-start | bytes 1572872 | tf_op jit(solution)/shard_map/ppermute | solution.py:61
  84.8 3.3 %queries.3 = (bf16[256,256]{1,0:T(8,128)(2,1)S(1)}, bf16[256,256]{1,0:T(8,128)(2,1)S(1)}) custom-call(s32[8]{0:T(128)S(1)} %stack.35.place, bf16[128,4096]{1,0:T(8,128)(2,1)S(1)} %collective-permute-done.19.h0, bf16[128,4096]{1,0:T(8,128)(2,1)S(1)} %collective-permute-done.23.h1, bf16[4096,512]{1,0:T(8,128)(2,1)} %bitcast.49), custom_call_target="tpu_custom_call" | custom-call | flops 1073741824 | bytes 8388608 | tf_op jit(solution)/shard_map/queries/pallas_call | solution.py:201
  88.4 5.9 %collective-permute-done.25.refs_5_ = bf16[64,4096]{1,0:T(8,128)(2,1)S(1)} collective-permute-done((bf16[64,4096]{1,0:T(8,128)(2,1)S(1)}, bf16[64,4096]{1,0:T(8,128)(2,1)S(1)}, u32[]{:S(2)}, u32[]{:S(2)}) %collective-permute-start.25) | collective-permute-done | bytes 524320 | tf_op jit(solution)/shard_map/ppermute | solution.py:61
  94.3 1.5 %collective-permute-done.26.refs_7_ = bf16[64,4096]{1,0:T(8,128)(2,1)S(1)} collective-permute-done((bf16[64,4096]{1,0:T(8,128)(2,1)S(1)}, bf16[64,4096]{1,0:T(8,128)(2,1)S(1)}, u32[]{:S(2)}, u32[]{:S(2)}) %collective-permute-start.26) | collective-permute-done | bytes 524320 | tf_op jit(solution)/shard_map/ppermute | solution.py:61
  95.8 1.3 collective-permute-done.24.refs_4_
  97.2 1.7 %collective-permute-start.28 = (bf16[1024,256]{1,0:T(8,128)(2,1)S(1)}, bf16[1024,256]{1,0:T(8,128)(2,1)S(1)}, u32[]{:S(2)}, u32[]{:S(2)}) collective-permute-start(bf16[1024,256]{1,0:T(8,128)(2,1)S(1)} %pad_maximum_fusion.1), channel_id=1, source_target_pairs={{0,12},{1,13},{2,14},{3,15},{4,0},{5,1},{6,2},{7,3},{8,4},{9,5},{1... | collective-permute-start | bytes 1572872 | tf_op jit(solution)/shard_map/ppermute | solution.py:61
  99.1 1.5 %collective-permute-start.32 = (bf16[64,4096]{1,0:T(8,128)(2,1)S(1)}, bf16[64,4096]{1,0:T(8,128)(2,1)S(1)}, u32[]{:S(2)}, u32[]{:S(2)}) collective-permute-start(bf16[64,4096]{1,0:T(8,128)(2,1)S(1)} %collective-permute-done.9.refs_1_), channel_id=1, source_target_pairs={{0,16},{1,17},{2,18},{3,19},{4,20},{5,21},{6,22},{7,23},{8,24},{9,... | collective-permute-start | bytes 1572872 | tf_op jit(solution)/shard_map/ppermute | solution.py:61
  100.5 2.7 %collective-permute-start.33 = (bf16[64,4096]{1,0:T(8,128)(2,1)S(1)}, bf16[64,4096]{1,0:T(8,128)(2,1)S(1)}, u32[]{:S(2)}, u32[]{:S(2)}) collective-permute-start(bf16[64,4096]{1,0:T(8,128)(2,1)S(1)} %get-tuple-element.112), channel_id=1, source_target_pairs={{0,18},{1,19},{2,16},{3,17},{4,22},{5,23},{6,20},{7,21},{8,26},{9,... | collective-permute-start | bytes 1572872 | tf_op jit(solution)/shard_map/ppermute | solution.py:61
  103.2 3.1 %attend.2 = (f32[1024,128]{1,0:T(8,128)S(1)}, f32[1024,128]{1,0:T(8,128)S(1)}, f32[1024,256]{1,0:T(8,128)S(1)}) custom-call(s32[8]{0:T(128)S(1)} %stack.35.place, s32[4,128]{1,0:T(4,128)S(1)} %bitcast.41, s32[4,128]{1,0:T(4,128)S(1)} %collective-permute-done.6.low_span.refs_1_, s32[1,4096]{1,0:T(1,128)S(1)} %copy-done.1, s32[4,128]{1,0:T(4,128)S(1)} %bitcast.42, ...), custom_call_target="tpu_custom_call" | custom-call | flops 402653184 | bytes 6291456 | tf_op jit(solution)/shard_map/attend/pallas_call | solution.py:314
  106.3 3.0 %collective-permute-done.28.refs_8_ = bf16[1024,256]{1,0:T(8,128)(2,1)S(1)} collective-permute-done((bf16[1024,256]{1,0:T(8,128)(2,1)S(1)}, bf16[1024,256]{1,0:T(8,128)(2,1)S(1)}, u32[]{:S(2)}, u32[]{:S(2)}) %collective-permute-start.28) | collective-permute-done | bytes 524320 | tf_op jit(solution)/shard_map/ppermute | solution.py:61
  109.3 2.6 %collective-permute-done.27.refs_7_ = bf16[1024,256]{1,0:T(8,128)(2,1)S(1)} collective-permute-done((bf16[1024,256]{1,0:T(8,128)(2,1)S(1)}, bf16[1024,256]{1,0:T(8,128)(2,1)S(1)}, u32[]{:S(2)}, u32[]{:S(2)}) %collective-permute-start.27) | collective-permute-done | bytes 524320 | tf_op jit(solution)/shard_map/ppermute | solution.py:61
  111.9 2.0 %attend.3 = (bf16[256,256]{1,0:T(8,128)(2,1)S(1)}, bf16[256,256]{1,0:T(8,128)(2,1)S(1)}, bf16[256,256]{1,0:T(8,128)(2,1)S(1)}, bf16[256,256]{1,0:T(8,128)(2,1)S(1)}) custom-call(s32[8]{0:T(128)S(1)} %stack.35.place, s32[4,128]{1,0:T(4,128)S(1)} %bitcast.43, s32[4,128]{1,0:T(4,128)S(1)} %collective-permute-done.6.low_span.refs_1_, s32[1,4096]{1,0:T(1,128)S(1)} %copy-done.1, ...), custom_call_target="tpu_custom_call" | custom-call | flops 134217728 | bytes 6291456 | tf_op jit(solution)/shard_map/attend/pallas_call | solution.py:314
  113.9 3.8 %collective-permute-start.29 = (bf16[256,256]{1,0:T(8,128)(2,1)S(1)}, bf16[256,256]{1,0:T(8,128)(2,1)S(1)}, u32[]{:S(2)}, u32[]{:S(2)}) collective-permute-start(bf16[256,256]{1,0:T(8,128)(2,1)S(1)} %get-tuple-element.103), channel_id=1, source_target_pairs={{0,2},{1,3},{2,0},{3,1},{4,6},{5,7},{6,4},{7,5},{8,10},{9,11},{10,... | collective-permute-start | bytes 393224 | tf_op jit(solution)/shard_map/ppermute | solution.py:61
  118.1 2.0 %collective-permute-done.29.c1 = bf16[256,256]{1,0:T(8,128)(2,1)S(1)} collective-permute-done((bf16[256,256]{1,0:T(8,128)(2,1)S(1)}, bf16[256,256]{1,0:T(8,128)(2,1)S(1)}, u32[]{:S(2)}, u32[]{:S(2)}) %collective-permute-start.29) | collective-permute-done | bytes 131104 | tf_op jit(solution)/shard_map/ppermute | solution.py:61
  120.1 2.1 %collective-permute-done.30.c2 = bf16[256,256]{1,0:T(8,128)(2,1)S(1)} collective-permute-done((bf16[256,256]{1,0:T(8,128)(2,1)S(1)}, bf16[256,256]{1,0:T(8,128)(2,1)S(1)}, u32[]{:S(2)}, u32[]{:S(2)}) %collective-permute-start.30) | collective-permute-done | bytes 131104 | tf_op jit(solution)/shard_map/ppermute | solution.py:61
  122.2 2.0 %collective-permute-done.31.c3 = bf16[256,256]{1,0:T(8,128)(2,1)S(1)} collective-permute-done((bf16[256,256]{1,0:T(8,128)(2,1)S(1)}, bf16[256,256]{1,0:T(8,128)(2,1)S(1)}, u32[]{:S(2)}, u32[]{:S(2)}) %collective-permute-start.31) | collective-permute-done | bytes 131104 | tf_op jit(solution)/shard_map/ppermute | solution.py:61
  124.2 3.4 %outputs.3 = bf16[256,2048]{1,0:T(8,128)(2,1)S(1)} custom-call(s32[8]{0:T(128)S(1)} %stack.35.place, bf16[256,256]{1,0:T(8,128)(2,1)S(1)} %get-tuple-element.102.c0, bf16[256,256]{1,0:T(8,128)(2,1)S(1)} %collective-permute-done.29.c1, bf16[256,256]{1,0:T(8,128)(2,1)S(1)} %collective-permute-done.30.c2, bf16[256,256]{1,0:T(8,128)(2,1)S(1)} %collective-permute-done.31.c3, ...), custom_call_target="tpu_custom_call" | custom-call | flops 1073741824 | bytes 4194304 | tf_op jit(solution)/shard_map/outputs/pallas_call | solution.py:369
  127.6 2.8 %collective-permute-start.35 = (bf16[128,2048]{1,0:T(8,128)(2,1)S(1)}, bf16[128,2048]{1,0:T(8,128)(2,1)S(1)}, u32[]{:S(2)}, u32[]{:S(2)}) collective-permute-start(bf16[128,2048]{1,0:T(8,128)(2,1)S(1)} %slice.43), channel_id=1, source_target_pairs={{0,1},{1,0},{2,3},{3,2},{4,5},{5,4},{6,7},{7,6},{8,9},{9,8},{10,11... | collective-permute-start | bytes 1572872 | tf_op jit(solution)/shard_map/ppermute | solution.py:61
  130.4 3.4 %outputs.2 = bf16[256,2048]{1,0:T(8,128)(2,1)S(1)} custom-call(s32[8]{0:T(128)S(1)} %stack.35.place, bf16[256,256]{1,0:T(8,128)(2,1)S(1)} %get-tuple-element.102.c0, bf16[256,256]{1,0:T(8,128)(2,1)S(1)} %collective-permute-done.29.c1, bf16[256,256]{1,0:T(8,128)(2,1)S(1)} %collective-permute-done.30.c2, bf16[256,256]{1,0:T(8,128)(2,1)S(1)} %collective-permute-done.31.c3, ...), custom_call_target="tpu_custom_call" | custom-call | flops 1073741824 | bytes 4194304 | tf_op jit(solution)/shard_map/outputs/pallas_call | solution.py:369
  134.1 1.8 %collective-permute-done.34 = bf16[128,2048]{1,0:T(8,128)(2,1)S(1)} collective-permute-done((bf16[128,2048]{1,0:T(8,128)(2,1)S(1)}, bf16[128,2048]{1,0:T(8,128)(2,1)S(1)}, u32[]{:S(2)}, u32[]{:S(2)}) %collective-permute-start.34) | collective-permute-done | bytes 524320 | tf_op jit(solution)/shard_map/ppermute | solution.py:61
  136.0 1.2 fusion.5
  (72 shorter events, 5.9 us)
Async XLA Ops:
  0.0 11.3 %copy-start.5 = (bf16[1,128,4096]{2,1,0:T(8,128)(2,1)S(1)}, bf16[1,128,4096]{2,1,0:T(8,128)(2,1)}, u32[]{:S(2)}) copy-start(bf16[1,128,4096]{2,1,0:T(8,128)(2,1)} %param.9) | copy-start | bytes 3145732
  0.0 11.6 %copy-start.7 = (bf16[1,4096]{1,0:T(2,128)(2,1)S(1)}, bf16[1,4096]{1,0:T(2,128)(2,1)}, u32[]{:S(2)}) copy-start(bf16[1,4096]{1,0:T(2,128)(2,1)} %param.11) | copy-start | bytes 24580
  1.2 20.8 %collective-permute-start.4 = (bf16[64,4096]{1,0:T(8,128)(2,1)S(1)}, bf16[64,4096]{1,0:T(8,128)(2,1)S(1)}, u32[]{:S(2)}, u32[]{:S(2)}) collective-permute-start(bf16[64,4096]{1,0:T(8,128)(2,1)S(1)} %dynamic-slice_bitcast_fusion), channel_id=1, source_target_pairs={{0,18},{1,19},{2,16},{3,17},{4,22},{5,23},{6,20},{7,21},{8,26},{9,... | collective-permute-start | bytes 1572872 | tf_op jit(solution)/shard_map/ppermute | solution.py:61
  6.8 8.4 %collective-permute-start.2 = (bf16[1,512,256]{2,1,0:T(8,128)(2,1)S(1)}, bf16[1,512,256]{2,1,0:T(8,128)(2,1)S(1)}, u32[]{:S(2)}, u32[]{:S(2)}) collective-permute-start(bf16[1,512,256]{2,1,0:T(8,128)(2,1)S(1)} %get-tuple-element.116), channel_id=1, source_target_pairs={{0,64},{1,65},{2,66},{3,67},{4,68},{5,69},{6,70},{7,71},{8,72},{9,... | collective-permute-start | bytes 786440 | tf_op jit(solution)/shard_map/ppermute | solution.py:61
  9.5 11.7 %collective-permute-start.1 = (bf16[1,512,256]{2,1,0:T(8,128)(2,1)S(1)}, bf16[1,512,256]{2,1,0:T(8,128)(2,1)S(1)}, u32[]{:S(2)}, u32[]{:S(2)}) collective-permute-start(bf16[1,512,256]{2,1,0:T(8,128)(2,1)S(1)} %get-tuple-element.117), channel_id=1, source_target_pairs={{0,96},{1,97},{2,98},{3,99},{4,100},{5,101},{6,102},{7,103},{8,104... | collective-permute-start | bytes 786440 | tf_op jit(solution)/shard_map/ppermute | solution.py:61
  10.4 11.2 %collective-permute-start = (bf16[1,512,256]{2,1,0:T(8,128)(2,1)S(1)}, bf16[1,512,256]{2,1,0:T(8,128)(2,1)S(1)}, u32[]{:S(2)}, u32[]{:S(2)}) collective-permute-start(bf16[1,512,256]{2,1,0:T(8,128)(2,1)S(1)} %get-tuple-element.118), channel_id=1, source_target_pairs={{0,32},{1,33},{2,34},{3,35},{4,36},{5,37},{6,38},{7,39},{8,40},{9,... | collective-permute-start | bytes 786440 | tf_op jit(solution)/shard_map/ppermute | solution.py:61
  11.0 10.6 %collective-permute-start.3 = (bf16[1,512,256]{2,1,0:T(8,128)(2,1)}, bf16[1,512,256]{2,1,0:T(8,128)(2,1)S(1)}, u32[]{:S(2)}, u32[]{:S(2)}) collective-permute-start(bf16[1,512,256]{2,1,0:T(8,128)(2,1)} %get-tuple-element.115.refs_0_), channel_id=1, source_target_pairs={{0,2},{1,3},{2,0},{3,1},{4,6},{5,7},{6,4},{7,5},{8,10},{9,11},{10,... | collective-permute-start | bytes 786440 | tf_op jit(solution)/shard_map/ppermute | solution.py:61
  21.6 5.6 %copy-start.2 = (bf16[1,512,256]{2,1,0:T(8,128)(2,1)}, bf16[1,512,256]{2,1,0:T(8,128)(2,1)S(1)}, u32[]{:S(2)}) copy-start(bf16[1,512,256]{2,1,0:T(8,128)(2,1)S(1)} %collective-permute-done.3.refs_2_) | copy-start | bytes 786436
  21.9 7.6 %collective-permute-start.11 = (bf16[128,4096]{1,0:T(8,128)(2,1)S(1)}, bf16[128,4096]{1,0:T(8,128)(2,1)}, u32[]{:S(2)}, u32[]{:S(2)}) collective-permute-start(bf16[128,4096]{1,0:T(8,128)(2,1)S(1)} %fusion.4.h0), channel_id=1, source_target_pairs={{0,1},{1,0},{2,3},{3,2},{4,5},{5,4},{6,7},{7,6},{8,9},{9,8},{10,11... | collective-permute-start | bytes 3145736 | tf_op jit(solution)/shard_map/ppermute | solution.py:61
  23.3 15.1 %collective-permute-start.10 = (bf16[64,4096]{1,0:T(8,128)(2,1)S(1)}, bf16[64,4096]{1,0:T(8,128)(2,1)S(1)}, u32[]{:S(2)}, u32[]{:S(2)}) collective-permute-start(bf16[64,4096]{1,0:T(8,128)(2,1)S(1)} %collective-permute-done.4.refs_0_), channel_id=1, source_target_pairs={{0,12},{1,13},{2,14},{3,15},{4,0},{5,1},{6,2},{7,3},{8,4},{9,5},{1... | collective-permute-start | bytes 1572872 | tf_op jit(solution)/shard_map/ppermute | solution.py:61
  27.1 14.6 %collective-permute-start.9 = (bf16[64,4096]{1,0:T(8,128)(2,1)S(1)}, bf16[64,4096]{1,0:T(8,128)(2,1)S(1)}, u32[]{:S(2)}, u32[]{:S(2)}) collective-permute-start(bf16[64,4096]{1,0:T(8,128)(2,1)S(1)} %collective-permute-done.4.refs_0_), channel_id=1, source_target_pairs={{0,4},{1,5},{2,6},{3,7},{4,8},{5,9},{6,10},{7,11},{8,12},{9,13},{1... | collective-permute-start | bytes 1572872 | tf_op jit(solution)/shard_map/ppermute | solution.py:61
  27.2 24.5 %collective-permute-start.5 = (bf16[3,512,256]{2,1,0:T(8,128)(2,1)S(1)}, bf16[3,512,256]{2,1,0:T(8,128)(2,1)}, u32[]{:S(2)}, u32[]{:S(2)}) collective-permute-start(bf16[3,512,256]{2,1,0:T(8,128)(2,1)S(1)} %constant_dynamic-update-slice_fusion.refs_0_), channel_id=1, source_target_pairs={{0,2},{1,3},{2,0},{3,1},{4,6},{5,7},{6,4},{7,5},{8,10},{9,11},{10,... | collective-permute-start | bytes 2359304 | tf_op jit(solution)/shard_map/ppermute | solution.py:61
  28.9 15.6 %collective-permute-start.7 = (bf16[1,512,256]{2,1,0:T(8,128)(2,1)}, bf16[1,512,256]{2,1,0:T(8,128)(2,1)}, u32[]{:S(2)}, u32[]{:S(2)}) collective-permute-start(bf16[1,512,256]{2,1,0:T(8,128)(2,1)} %get-tuple-element.115.refs_0_), channel_id=1, source_target_pairs={{0,1},{1,0},{2,3},{3,2},{4,5},{5,4},{6,7},{7,6},{8,9},{9,8},{10,11... | collective-permute-start | bytes 786440 | tf_op jit(solution)/shard_map/ppermute | solution.py:61
  29.5 15.1 %collective-permute-start.8 = (bf16[1,512,256]{2,1,0:T(8,128)(2,1)}, bf16[1,512,256]{2,1,0:T(8,128)(2,1)S(1)}, u32[]{:S(2)}, u32[]{:S(2)}) collective-permute-start(bf16[1,512,256]{2,1,0:T(8,128)(2,1)} %copy-done.2), channel_id=1, source_target_pairs={{0,1},{1,0},{2,3},{3,2},{4,5},{5,4},{6,7},{7,6},{8,9},{9,8},{10,11... | collective-permute-start | bytes 786440 | tf_op jit(solution)/shard_map/ppermute | solution.py:61
  33.7 10.8 %copy-start.4 = (s32[1,512]{1,0:T(1,128)S(1)}, s32[1,512]{1,0:T(1,128)}, u32[]{:S(2)}) copy-start(s32[1,512]{1,0:T(1,128)} %param.16) | copy-start | bytes 6148
  33.7 12.8 %copy-start.3 = (bf16[1,512,256]{2,1,0:T(8,128)(2,1)S(1)}, bf16[1,512,256]{2,1,0:T(8,128)(2,1)}, u32[]{:S(2)}) copy-start(bf16[1,512,256]{2,1,0:T(8,128)(2,1)} %copy-done.2) | copy-start | bytes 786436
  41.7 10.0 %collective-permute-start.13 = (bf16[32,4096]{1,0:T(8,128)(2,1)S(1)}, bf16[32,4096]{1,0:T(8,128)(2,1)S(1)}, u32[]{:S(2)}, u32[]{:S(2)}) collective-permute-start(bf16[32,4096]{1,0:T(8,128)(2,1)S(1)} %slice.31), channel_id=1, source_target_pairs={{0,12},{1,13},{2,14},{3,15},{4,0},{5,1},{6,2},{7,3},{8,4},{9,5},{1... | collective-permute-start | bytes 786440 | tf_op jit(solution)/shard_map/ppermute | solution.py:61
  42.1 9.6 %collective-permute-start.12 = (bf16[32,4096]{1,0:T(8,128)(2,1)S(1)}, bf16[32,4096]{1,0:T(8,128)(2,1)S(1)}, u32[]{:S(2)}, u32[]{:S(2)}) collective-permute-start(bf16[32,4096]{1,0:T(8,128)(2,1)S(1)} %slice.30), channel_id=1, source_target_pairs={{0,4},{1,5},{2,6},{3,7},{4,8},{5,9},{6,10},{7,11},{8,12},{9,13},{1... | collective-permute-start | bytes 786440 | tf_op jit(solution)/shard_map/ppermute | solution.py:61
  44.5 7.2 %collective-permute-start.6 = (s32[4,128]{1,0:T(4,128)S(1)}, s32[4,128]{1,0:T(4,128)S(1)}, u32[]{:S(2)}, u32[]{:S(2)}) collective-permute-start(s32[4,128]{1,0:T(4,128)S(1)} %bitcast.40), channel_id=1, source_target_pairs={{0,16},{1,17},{2,18},{3,19},{4,20},{5,21},{6,22},{7,23},{8,24},{9,... | collective-permute-start | bytes 6152 | tf_op jit(solution)/shard_map/ppermute | solution.py:61
  44.6 10.1 %collective-permute-start.14 = (bf16[3,512,256]{2,1,0:T(8,128)(2,1)S(1)}, bf16[3,512,256]{2,1,0:T(8,128)(2,1)S(1)}, u32[]{:S(2)}, u32[]{:S(2)}) collective-permute-start(bf16[3,512,256]{2,1,0:T(8,128)(2,1)S(1)} %constant_dynamic-update-slice_fusion.refs_0_), channel_id=1, source_target_pairs={{0,1},{1,0},{2,3},{3,2},{4,5},{5,4},{6,7},{7,6},{8,9},{9,8},{10,11... | collective-permute-start | bytes 2359304 | tf_op jit(solution)/shard_map/ppermute | solution.py:61
  50.3 1.3 copy-start
  51.7 3.0 %collective-permute-start.15 = (bf16[3,512,256]{2,1,0:T(8,128)(2,1)}, bf16[3,512,256]{2,1,0:T(8,128)(2,1)S(1)}, u32[]{:S(2)}, u32[]{:S(2)}) collective-permute-start(bf16[3,512,256]{2,1,0:T(8,128)(2,1)} %collective-permute-done.5.refs_2_), channel_id=1, source_target_pairs={{0,1},{1,0},{2,3},{3,2},{4,5},{5,4},{6,7},{7,6},{8,9},{9,8},{10,11... | collective-permute-start | bytes 2359304 | tf_op jit(solution)/shard_map/ppermute | solution.py:61
  52.0 26.1 %collective-permute-start.19 = (bf16[128,4096]{1,0:T(8,128)(2,1)S(1)}, bf16[128,4096]{1,0:T(8,128)(2,1)S(1)}, u32[]{:S(2)}, u32[]{:S(2)}) collective-permute-start(bf16[128,4096]{1,0:T(8,128)(2,1)S(1)} %fusion.4.h0), channel_id=1, source_target_pairs={{0,18},{1,19},{2,16},{3,17},{4,22},{5,23},{6,20},{7,21},{8,26},{9,... | collective-permute-start | bytes 3145736 | tf_op jit(solution)/shard_map/ppermute | solution.py:61
  62.1 16.0 %collective-permute-start.16 = (bf16[2,512,256]{2,1,0:T(8,128)(2,1)S(1)}, bf16[2,512,256]{2,1,0:T(8,128)(2,1)S(1)}, u32[]{:S(2)}, u32[]{:S(2)}) collective-permute-start(bf16[2,512,256]{2,1,0:T(8,128)(2,1)S(1)} %get-tuple-element.78), channel_id=1, source_target_pairs={{0,16},{1,17},{2,18},{3,19},{4,20},{5,21},{6,22},{7,23},{8,24},{9,... | collective-permute-start | bytes 1572872 | tf_op jit(solution)/shard_map/ppermute | solution.py:61
  63.2 14.9 %collective-permute-start.18 = (bf16[2,512,256]{2,1,0:T(8,128)(2,1)S(1)}, bf16[2,512,256]{2,1,0:T(8,128)(2,1)S(1)}, u32[]{:S(2)}, u32[]{:S(2)}) collective-permute-start(bf16[2,512,256]{2,1,0:T(8,128)(2,1)S(1)} %get-tuple-element.79.refs_7_), channel_id=1, source_target_pairs={{0,12},{1,13},{2,14},{3,15},{4,0},{5,1},{6,2},{7,3},{8,4},{9,5},{1... | collective-permute-start | bytes 1572872 | tf_op jit(solution)/shard_map/ppermute | solution.py:61
  64.4 13.7 %collective-permute-start.17 = (bf16[2,512,256]{2,1,0:T(8,128)(2,1)S(1)}, bf16[2,512,256]{2,1,0:T(8,128)(2,1)S(1)}, u32[]{:S(2)}, u32[]{:S(2)}) collective-permute-start(bf16[2,512,256]{2,1,0:T(8,128)(2,1)S(1)} %get-tuple-element.79.refs_7_), channel_id=1, source_target_pairs={{0,4},{1,5},{2,6},{3,7},{4,8},{5,9},{6,10},{7,11},{8,12},{9,13},{1... | collective-permute-start | bytes 1572872 | tf_op jit(solution)/shard_map/ppermute | solution.py:61
  64.6 13.5 %collective-permute-start.20 = (bf16[256,256]{1,0:T(8,128)(2,1)S(1)}, bf16[256,256]{1,0:T(8,128)(2,1)S(1)}, u32[]{:S(2)}, u32[]{:S(2)}) collective-permute-start(bf16[256,256]{1,0:T(8,128)(2,1)S(1)} %get-tuple-element.83), channel_id=1, source_target_pairs={{0,16},{1,17},{2,18},{3,19},{4,20},{5,21},{6,22},{7,23},{8,24},{9,... | collective-permute-start | bytes 393224 | tf_op jit(solution)/shard_map/ppermute | solution.py:61
  78.1 6.6 %collective-permute-start.23 = (bf16[128,4096]{1,0:T(8,128)(2,1)S(1)}, bf16[128,4096]{1,0:T(8,128)(2,1)S(1)}, u32[]{:S(2)}, u32[]{:S(2)}) collective-permute-start(bf16[128,4096]{1,0:T(8,128)(2,1)S(1)} %collective-permute-done.19.h0), channel_id=1, source_target_pairs={{0,1},{1,0},{2,3},{3,2},{4,5},{5,4},{6,7},{7,6},{8,9},{9,8},{10,11... | collective-permute-start | bytes 3145736 | tf_op jit(solution)/shard_map/ppermute | solution.py:61
  79.9 15.9 %collective-permute-start.22 = (bf16[2,512,256]{2,1,0:T(8,128)(2,1)S(1)}, bf16[2,512,256]{2,1,0:T(8,128)(2,1)S(1)}, u32[]{:S(2)}, u32[]{:S(2)}) collective-permute-start(bf16[2,512,256]{2,1,0:T(8,128)(2,1)S(1)} %collective-permute-done.16.refs_10_), channel_id=1, source_target_pairs={{0,12},{1,13},{2,14},{3,15},{4,0},{5,1},{6,2},{7,3},{8,4},{9,5},{1... | collective-permute-start | bytes 1572872 | tf_op jit(solution)/shard_map/ppermute | solution.py:61
  80.4 15.4 %collective-permute-start.21 = (bf16[2,512,256]{2,1,0:T(8,128)(2,1)S(1)}, bf16[2,512,256]{2,1,0:T(8,128)(2,1)S(1)}, u32[]{:S(2)}, u32[]{:S(2)}) collective-permute-start(bf16[2,512,256]{2,1,0:T(8,128)(2,1)S(1)} %collective-permute-done.16.refs_10_), channel_id=1, source_target_pairs={{0,4},{1,5},{2,6},{3,7},{4,8},{5,9},{6,10},{7,11},{8,12},{9,13},{1... | collective-permute-start | bytes 1572872 | tf_op jit(solution)/shard_map/ppermute | solution.py:61
  81.4 12.9 %collective-permute-start.25 = (bf16[64,4096]{1,0:T(8,128)(2,1)S(1)}, bf16[64,4096]{1,0:T(8,128)(2,1)S(1)}, u32[]{:S(2)}, u32[]{:S(2)}) collective-permute-start(bf16[64,4096]{1,0:T(8,128)(2,1)S(1)} %collective-permute-done.4.refs_0_), channel_id=1, source_target_pairs={{0,16},{1,17},{2,18},{3,19},{4,20},{5,21},{6,22},{7,23},{8,24},{9,... | collective-permute-start | bytes 1572872 | tf_op jit(solution)/shard_map/ppermute | solution.py:61
  82.1 13.7 %collective-permute-start.26 = (bf16[64,4096]{1,0:T(8,128)(2,1)S(1)}, bf16[64,4096]{1,0:T(8,128)(2,1)S(1)}, u32[]{:S(2)}, u32[]{:S(2)}) collective-permute-start(bf16[64,4096]{1,0:T(8,128)(2,1)S(1)} %get-tuple-element.89), channel_id=1, source_target_pairs={{0,18},{1,19},{2,16},{3,17},{4,22},{5,23},{6,20},{7,21},{8,26},{9,... | collective-permute-start | bytes 1572872 | tf_op jit(solution)/shard_map/ppermute | solution.py:61
  88.1 15.1 %copy-start.1 = (s32[1,4096]{1,0:T(1,128)S(1)}, s32[1,4096]{1,0:T(1,128)}, u32[]{:S(2)}) copy-start(s32[1,4096]{1,0:T(1,128)} %refs_2_.3) | copy-start | bytes 49156
  88.1 9.0 %collective-permute-start.24 = (bf16[256,256]{1,0:T(8,128)(2,1)S(1)}, bf16[256,256]{1,0:T(8,128)(2,1)S(1)}, u32[]{:S(2)}, u32[]{:S(2)}) collective-permute-start(bf16[256,256]{1,0:T(8,128)(2,1)S(1)} %get-tuple-element.87), channel_id=1, source_target_pairs={{0,16},{1,17},{2,18},{3,19},{4,20},{5,21},{6,22},{7,23},{8,24},{9,... | collective-permute-start | bytes 393224 | tf_op jit(solution)/shard_map/ppermute | solution.py:61
  97.2 12.1 %collective-permute-start.28 = (bf16[1024,256]{1,0:T(8,128)(2,1)S(1)}, bf16[1024,256]{1,0:T(8,128)(2,1)S(1)}, u32[]{:S(2)}, u32[]{:S(2)}) collective-permute-start(bf16[1024,256]{1,0:T(8,128)(2,1)S(1)} %pad_maximum_fusion.1), channel_id=1, source_target_pairs={{0,12},{1,13},{2,14},{3,15},{4,0},{5,1},{6,2},{7,3},{8,4},{9,5},{1... | collective-permute-start | bytes 1572872 | tf_op jit(solution)/shard_map/ppermute | solution.py:61
  99.0 12.9 %collective-permute-start.27 = (bf16[1024,256]{1,0:T(8,128)(2,1)S(1)}, bf16[1024,256]{1,0:T(8,128)(2,1)S(1)}, u32[]{:S(2)}, u32[]{:S(2)}) collective-permute-start(bf16[1024,256]{1,0:T(8,128)(2,1)S(1)} %pad_maximum_fusion), channel_id=1, source_target_pairs={{0,4},{1,5},{2,6},{3,7},{4,8},{5,9},{6,10},{7,11},{8,12},{9,13},{1... | collective-permute-start | bytes 1572872 | tf_op jit(solution)/shard_map/ppermute | solution.py:61
  99.1 19.1 %collective-permute-start.32 = (bf16[64,4096]{1,0:T(8,128)(2,1)S(1)}, bf16[64,4096]{1,0:T(8,128)(2,1)S(1)}, u32[]{:S(2)}, u32[]{:S(2)}) collective-permute-start(bf16[64,4096]{1,0:T(8,128)(2,1)S(1)} %collective-permute-done.9.refs_1_), channel_id=1, source_target_pairs={{0,16},{1,17},{2,18},{3,19},{4,20},{5,21},{6,22},{7,23},{8,24},{9,... | collective-permute-start | bytes 1572872 | tf_op jit(solution)/shard_map/ppermute | solution.py:61
  100.5 17.6 %collective-permute-start.33 = (bf16[64,4096]{1,0:T(8,128)(2,1)S(1)}, bf16[64,4096]{1,0:T(8,128)(2,1)S(1)}, u32[]{:S(2)}, u32[]{:S(2)}) collective-permute-start(bf16[64,4096]{1,0:T(8,128)(2,1)S(1)} %get-tuple-element.112), channel_id=1, source_target_pairs={{0,18},{1,19},{2,16},{3,17},{4,22},{5,23},{6,20},{7,21},{8,26},{9,... | collective-permute-start | bytes 1572872 | tf_op jit(solution)/shard_map/ppermute | solution.py:61
  113.9 6.2 %collective-permute-start.29 = (bf16[256,256]{1,0:T(8,128)(2,1)S(1)}, bf16[256,256]{1,0:T(8,128)(2,1)S(1)}, u32[]{:S(2)}, u32[]{:S(2)}) collective-permute-start(bf16[256,256]{1,0:T(8,128)(2,1)S(1)} %get-tuple-element.103), channel_id=1, source_target_pairs={{0,2},{1,3},{2,0},{3,1},{4,6},{5,7},{6,4},{7,5},{8,10},{9,11},{10,... | collective-permute-start | bytes 393224 | tf_op jit(solution)/shard_map/ppermute | solution.py:61
  117.8 4.4 %collective-permute-start.30 = (bf16[256,256]{1,0:T(8,128)(2,1)S(1)}, bf16[256,256]{1,0:T(8,128)(2,1)S(1)}, u32[]{:S(2)}, u32[]{:S(2)}) collective-permute-start(bf16[256,256]{1,0:T(8,128)(2,1)S(1)} %get-tuple-element.104), channel_id=1, source_target_pairs={{0,16},{1,17},{2,18},{3,19},{4,20},{5,21},{6,22},{7,23},{8,24},{9,... | collective-permute-start | bytes 393224 | tf_op jit(solution)/shard_map/ppermute | solution.py:61
  117.8 6.4 %collective-permute-start.31 = (bf16[256,256]{1,0:T(8,128)(2,1)S(1)}, bf16[256,256]{1,0:T(8,128)(2,1)S(1)}, u32[]{:S(2)}, u32[]{:S(2)}) collective-permute-start(bf16[256,256]{1,0:T(8,128)(2,1)S(1)} %get-tuple-element.105), channel_id=1, source_target_pairs={{0,18},{1,19},{2,16},{3,17},{4,22},{5,23},{6,20},{7,21},{8,26},{9,... | collective-permute-start | bytes 393224 | tf_op jit(solution)/shard_map/ppermute | solution.py:61
  127.6 6.4 %collective-permute-start.35 = (bf16[128,2048]{1,0:T(8,128)(2,1)S(1)}, bf16[128,2048]{1,0:T(8,128)(2,1)S(1)}, u32[]{:S(2)}, u32[]{:S(2)}) collective-permute-start(bf16[128,2048]{1,0:T(8,128)(2,1)S(1)} %slice.43), channel_id=1, source_target_pairs={{0,1},{1,0},{2,3},{3,2},{4,5},{5,4},{6,7},{7,6},{8,9},{9,8},{10,11... | collective-permute-start | bytes 1572872 | tf_op jit(solution)/shard_map/ppermute | solution.py:61
  133.9 2.1 %copy-start.6 = (bf16[1,128,4096]{2,1,0:T(8,128)(2,1)S(1)}, bf16[1,128,4096]{2,1,0:T(8,128)(2,1)}, u32[]{:S(2)}) copy-start(bf16[1,128,4096]{2,1,0:T(8,128)(2,1)} %param.9) | copy-start | bytes 3145732
  133.9 2.0 %collective-permute-start.34 = (bf16[128,2048]{1,0:T(8,128)(2,1)S(1)}, bf16[128,2048]{1,0:T(8,128)(2,1)S(1)}, u32[]{:S(2)}, u32[]{:S(2)}) collective-permute-start(bf16[128,2048]{1,0:T(8,128)(2,1)S(1)} %slice.41), channel_id=1, source_target_pairs={{0,1},{1,0},{2,3},{3,2},{4,5},{5,4},{6,7},{7,6},{8,9},{9,8},{10,11... | collective-permute-start | bytes 1572872 | tf_op jit(solution)/shard_map/ppermute | solution.py:61
